TPU v7x, 32 devices: a whole 2x2x4 slice. The times are simulated.
32 devices in a mesh: dp: 8 (over z, x), hst: 4 (over y, core).
Axes of the slice: x: 2, y: 2, z: 4, core: 2. Of those that a mesh axis runs over, the one named last changes fastest.
Arguments:
- tokens: bfloat16 [128, 7168], P('dp', 'hst'), may hold values from -6 to 6
- cotangent: bfloat16 [128, 7168], P('dp', 'hst'), may hold values from -6 to 6
- expert_ids: int32 [128, 2], P('dp'), may hold values from 0 to 7, all different within a row; in each aligned block of 16 rows (0 to 15, 16 to 31, ...) at most 4 rows name the same one
- gate_values: float32 [128, 2], P('dp'), may hold values from 0.2 to 1
- w_gate: bfloat16 [8, 4864, 7168], P('hst', 'dp'), may hold values from -0.0625 to 0.0625
- w_up: bfloat16 [8, 4864, 7168], P('hst', 'dp'), may hold values from -0.0625 to 0.0625
- w_down: bfloat16 [8, 4864, 7168], P('hst', 'dp'), may hold values from -0.078125 to 0.078125
Outputs:
- mixed: bfloat16 [128, 7168], P('dp', 'hst')
- grad_tokens: bfloat16 [128, 7168], P('dp', 'hst')
- grad_gate: bfloat16 [8, 4864, 7168], P('hst', 'dp')
- grad_up: bfloat16 [8, 4864, 7168], P('hst', 'dp')
- grad_down: bfloat16 [8, 4864, 7168], P('hst', 'dp')
Inputs may be any that keep to these rules, and one draw needn't show every extreme that they name: `expert_ids`: within each block of 16 rows (the rows of one index of dp), a token names two different experts, and no expert is named by more than 4 routes; since a block has 8 routes and 8 slots, every expert fills all 4 of its slots in every block.
All inputs are finite; a program needn't handle non-finite values.
Results may differ from a plain program's by a relative error of at most 0.023.
Values may be sent and summed in bfloat16 or wider, within the bound.
No kernel may reach another device: no remote copies, remote signals or barrier semaphores. Data moves between devices by JAX's collectives and lax.ppermute only.
A program may use at most 192 MiB of HBM per device.

v0:
```python
import functools
import math

import jax
import jax.numpy as jnp
from jax import lax
from jax.experimental import pallas as pl
from jax.experimental.pallas import tpu as pltpu
from jax.sharding import PartitionSpec as P

CAP = 4
LANES = 128
MIB = 1 << 20
MFLOP = 10**6
F32 = jnp.float32
BF16 = jnp.bfloat16
AXES = ("dp", "hst")


def dot(a, b):
    return lax.dot_general(a, b, (((1,), (0,)), ((), ())), preferred_element_type=F32)


def dot_t(a, b):
    return lax.dot_general(a, b, (((1,), (1,)), ((), ())), preferred_element_type=F32)


def log2(n):
    assert n & (n - 1) == 0
    return n.bit_length() - 1


class Grid:
    def __init__(self, dp, hst):
        self.dp, self.hst = dp, hst
        self.nc = 2 if hst % 2 == 0 else 1
        self.ny = hst // self.nc
        self.nx = self.ny if dp % self.ny == 0 else 1
        self.nz = dp // self.nx
        assert self.nz & (self.nz - 1) == 0
        self.square = [(a, b) for a in range(self.nx) for b in range(self.ny)]

    def shift(self, value, dz=0, dx=0, dy=0, dc=0):
        pairs = []
        for z in range(self.nz):
            for x in range(self.nx):
                for y in range(self.ny):
                    for c in range(self.nc):
                        to_dp = (z ^ dz) * self.nx + (x + dx) % self.nx
                        to_hst = (y + dy) % self.ny * self.nc + (c + dc) % self.nc
                        here = (z * self.nx + x) * self.hst + y * self.nc + c
                        pairs.append((here, to_dp * self.hst + to_hst))
        return lax.ppermute(value, AXES, pairs)

    def along_z(self, mine):
        return [mine] + [self.shift(mine, dz=k) for k in range(1, self.nz)]

    def over_plane(self, column):
        return {(a, b): self.shift(column, dx=a, dy=b) if a or b else column for a, b in self.square}

    def over_cores(self, column, others):
        blocks = [column, others]
        for c in range(1, self.nc):
            blocks += [self.shift(column, dc=c), self.shift(others, dc=c)]
        return blocks

    def source(self, k):
        host = lax.axis_index("hst")
        y, core = host >> log2(self.nc), host & (self.nc - 1)
        from_y = (y - (k & (self.ny - 1))) & (self.ny - 1)
        return (from_y << log2(self.nc)) + ((core + (k >> log2(self.ny))) & (self.nc - 1))


def call(kernel, name, outs, args, specs=None, out_specs=None, scratch=(), grid=(), limit=16, cost=0, aliases=None):
    specs = specs or [pl.BlockSpec(memory_space=pltpu.VMEM)] * len(args)
    out_specs = out_specs or [pl.BlockSpec(memory_space=pltpu.VMEM)] * len(outs)
    return pl.pallas_call(
        kernel,
        name=name,
        grid=grid,
        out_shape=outs,
        in_specs=specs,
        out_specs=out_specs,
        scratch_shapes=list(scratch),
        input_output_aliases=aliases or {},
        compiler_params=pltpu.CompilerParams(vmem_limit_bytes=limit * MIB),
        cost_estimate=pl.CostEstimate(flops=cost * MFLOP, bytes_accessed=0, transcendentals=0),
    )(*args)


def shaped(dtype, *dims):
    return jax.ShapeDtypeStruct(dims, dtype)


VECTORS = pl.BlockSpec(memory_space=pltpu.VMEM)
ANYWHERE = pl.BlockSpec(memory_space=pl.ANY)


def hbm(weight):
    return pltpu.with_memory_space_constraint(weight, pltpu.HBM)


def pack_kernel(tokens, ids, gates, later, out_ref, later_ref, tokens_ref, ids_ref, gates_ref, sems):
    pairs = [(tokens, tokens_ref), (ids, ids_ref), (gates, gates_ref), (later, later_ref)]
    copies = [pltpu.make_async_copy(a, b, sems.at[k]) for k, (a, b) in enumerate(pairs)]
    for copy in copies:
        copy.start()
    for copy in copies:
        copy.wait()
    rows, width = tokens_ref.shape
    out_ref[:, :width] = tokens_ref[...]
    values = gates_ref[...]
    high = values.astype(BF16).astype(F32)
    middle = (values - high).astype(BF16).astype(F32)
    low = values - high - middle
    fields = jnp.concatenate([ids_ref[...].astype(F32), high, middle, low], axis=0)
    fields = jnp.pad(fields, ((0, LANES - fields.shape[0]), (0, LANES - rows)))
    out_ref[:, width:] = jnp.transpose(fields)[:rows].astype(BF16)


def stack_kernel(count, later, *refs):
    parts, out_ref = refs[:count], refs[-1 - later]
    rows = parts[0].shape[0]
    for k, part in enumerate(parts):
        out_ref[k * rows : (k + 1) * rows] = part[...]
    if later:
        refs[-1][...] = refs[count][...]


def stack(parts, after, name, later=()):
    rows, width = parts[0].shape
    outs = call(
        functools.partial(stack_kernel, len(parts), len(later)),
        name,
        [shaped(BF16, rows * len(parts), width)] + [shaped(BF16, *array.shape) for array in later],
        [*parts, *later, *after],
        specs=[VECTORS] * (len(parts) + len(later)) + [ANYWHERE] * len(after),
        limit=16,
    )
    return outs if later else outs[0]


def add_kernel(count, skip, pieces, *refs):
    parts, outs = refs[:count], refs[count + skip : count + skip + pieces]
    total = parts[0][...].astype(F32)
    for part in parts[1:]:
        total = total + part[...].astype(F32)
    total = total.astype(BF16).reshape((pieces,) + outs[0].shape)
    for k, out in enumerate(outs):
        out[...] = total[k]


def add(parts, pieces, after, name, later=()):
    *lead, rows, width = parts[0].shape
    each = math.prod(lead) * rows // pieces
    first = len(parts) + len(after)
    return call(
        functools.partial(add_kernel, len(parts), len(after) + len(later), pieces),
        name,
        [shaped(BF16, each, width)] * pieces + [shaped(BF16, *array.shape) for array in later],
        [*parts, *after, *later],
        specs=[VECTORS] * len(parts) + [ANYWHERE] * (len(after) + len(later)),
        out_specs=[VECTORS] * pieces + [ANYWHERE] * len(later),
        aliases={first + k: pieces + k for k in range(len(later))},
    )


def doubled_along_z(grid, mine, meanwhile):
    column, k, done = mine, 1, None
    while k < grid.nz:
        got = grid.shift(column, dz=k)
        if 2 * k >= grid.nz:
            done = meanwhile(column)
        column = stack([column, got], [] if done is None else [done], "double")
        k *= 2
    return column, meanwhile(column) if done is None else done


def back_over_cores(grid, parts, after, name):
    got = [grid.shift(parts[c], dc=-c) for c in range(1, grid.nc)]
    return add([parts[0], *got], len(grid.square), after, name)


def back_over_plane(grid, kept, after, name, later=()):
    got = [grid.shift(part, dx=-a, dy=-b) for part, (a, b) in zip(kept[1:], grid.square[1:])]
    return add([kept[0], *got], grid.nz, after, name, later)


def back_along_z(grid, total):
    return [total[0]] + [grid.shift(total[k], dz=k) for k in range(1, grid.nz)]


def finish_kernel(count, *refs):
    for n, out in enumerate(refs[-2:]):
        total = refs[n * count][...].astype(F32)
        for part in refs[n * count + 1 : (n + 1) * count]:
            total = total + part[...].astype(F32)
        out[...] = total.astype(BF16)


def finish(first, second, after):
    return call(
        functools.partial(finish_kernel, len(first)),
        "finish",
        [shaped(BF16, *first[0].shape)] * 2,
        [*first, *second, *after],
        specs=[VECTORS] * (2 * len(first)) + [ANYWHERE] * len(after),
    )


def tables(aux, first, rows, local, block):
    tokens = aux.shape[0]
    across = jnp.transpose(aux.astype(F32))
    ids = [across[k : k + 1] for k in range(2)]
    gates = [across[2 + k : 3 + k] + across[4 + k : 5 + k] + across[6 + k : 7 + k] for k in range(2)]
    total = local * rows
    r = lax.broadcasted_iota(jnp.int32, (total, tokens), 0)
    j = lax.broadcasted_iota(jnp.int32, (total, tokens), 1)
    expert = ((r >> log2(rows)) + first).astype(F32)
    own_block = ((r & (rows - 1)) >> log2(CAP)) == (j >> log2(block))
    slot = (r & (CAP - 1)).astype(F32)
    hits = [(ids[k] == expert).astype(F32) for k in range(2)]
    hit = hits[0] + hits[1]
    up = lax.broadcasted_iota(jnp.int32, (tokens, tokens), 0)
    to = lax.broadcasted_iota(jnp.int32, (tokens, tokens), 1)
    earlier = ((up >> log2(block)) == (to >> log2(block))) & (up < to)
    position = dot(hit.astype(BF16), jnp.where(earlier, 1.0, 0.0).astype(BF16))
    select = jnp.where(own_block & (position == slot), hit, 0.0)
    gate = jnp.sum(select * (hits[0] * gates[0] + hits[1] * gates[1]), axis=1, keepdims=True)
    return select, gate


class Stream:
    def __init__(self, s, weight, room, sems, place):
        self.s, self.weight, self.room, self.sems, self.place = s, weight, room, sems, place
        for k in range(min(2, s.slices)):
            for p in range(len(s.pieces)):
                self.copy(k, p).start()

    def slot(self, k, p):
        return lax.rem(k, 2) * len(self.s.pieces) + p

    def copy(self, k, p):
        at, size = self.s.pieces[p]
        start = pl.multiple_of(self.place(k) * self.s.width + at, LANES)
        slot = self.slot(k, p)
        return pltpu.make_async_copy(
            self.weight.at[:, :, pl.ds(start, size)], self.room.at[slot, :, :, pl.ds(0, size)], self.sems.at[slot]
        )

    def get(self, k, p):
        self.copy(k, p).wait()
        return self.room.at[self.slot(k, p), :, :, pl.ds(0, self.s.pieces[p][1])]

    def free(self, k, p):
        @pl.when(k + 2 < self.s.slices)
        def _():
            self.copy(k + 2, p).start()


def held_copy(s, weight, held, sems, k, p):
    at, size = s.pieces[p]
    columns = (slice(None), slice(None), pl.ds(pl.multiple_of(k * s.width + at, LANES), size))
    return pltpu.make_async_copy(weight.at[columns], held.at[columns], sems.at[k * len(s.pieces) + p])


def hold_kernel(s, weight, _, held, sems):
    copies = [held_copy(s, weight, held, sems, k, p) for k in range(s.early) for p in range(len(s.pieces))]
    for copy in copies:
        copy.start()
    for copy in copies:
        copy.wait()


def hold(s, weight, after):
    (held,) = call(
        functools.partial(hold_kernel, s),
        "hold_gate",
        [pltpu.VMEM(weight.shape, BF16)],
        [hbm(weight), after],
        specs=[ANYWHERE] * 2,
        scratch=[pltpu.SemaphoreType.DMA((s.early * len(s.pieces),))],
        cost=12000,
    )
    return held


class Sizes:
    def __init__(self, grid, tokens, w_gate):
        self.grid = grid
        self.local, self.hidden, self.features = w_gate.shape
        self.block, self.width = tokens.shape
        self.rows = grid.dp * CAP
        self.total = self.local * self.rows
        self.count = grid.dp * self.block
        self.column = grid.nz * self.block
        self.blocks = grid.nc * grid.ny * grid.nx
        self.slices = grid.nc * grid.ny
        whole = self.width % 256 == 0 and self.width > 1024
        self.pieces = [(0, 1024), (1024, self.width - 1024)] if whole else [(0, self.width)]
        self.early = self.slices // 2

    def block_of(self, blocks, c, a, b):
        n = self.grid.square.index((a, b)) - 1
        return blocks[2 * c] if n < 0 else blocks[2 * c + 1].at[n * self.column : (n + 1) * self.column]

    def at(self, e):
        return slice(e * self.rows, (e + 1) * self.rows)


def routed(s, blocks, select):
    for k in range(s.slices):
        group = [s.block_of(blocks, k // s.grid.ny, a, k % s.grid.ny)[:, : s.width] for a in range(s.grid.nx)]
        yield k, dot(select, jnp.concatenate(group, axis=0))


def gate_up_kernel(s, *refs):
    blocks, refs = refs[: 2 * s.grid.nc], refs[2 * s.grid.nc :]
    _, wg_ref, wu_ref, _, x_ref, select_ref, back_ref, gate_ref, act_ref, p_ref, q_ref, held_ref = refs[:12]
    room, sems, held_sems, g_acc, u_acc = refs[12:]
    ups = Stream(s, wu_ref, room, sems, lambda k: k)
    for k in range(s.early, min(2, s.slices)):
        for p in range(len(s.pieces)):
            held_copy(s, wg_ref, held_ref, held_sems, k, p).start()
    aux = jnp.concatenate([s.block_of(blocks, 0, a, 0)[:, s.width :] for a in range(s.grid.nx)], axis=0)
    select, gate = tables(aux, lax.axis_index("hst") * s.local, s.rows, s.local, s.block)
    gate_ref[...] = jnp.broadcast_to(gate, gate_ref.shape)
    select_ref[...] = select.astype(BF16)
    back_ref[...] = jnp.transpose(select).astype(BF16)
    for k, picked in routed(s, blocks, select.astype(BF16)):
        x_ref[s.grid.source(k)] = picked.astype(BF16)
    g_acc[...] = jnp.zeros_like(g_acc)
    u_acc[...] = jnp.zeros_like(u_acc)

    def step(k, _):
        for p, (at, size) in enumerate(s.pieces):

            @pl.when((k + 2 >= s.early) & (k + 2 < s.slices))
            def _():
                held_copy(s, wg_ref, held_ref, held_sems, k + 2, p).start()

            @pl.when(k >= s.early)
            def _():
                held_copy(s, wg_ref, held_ref, held_sems, k, p).wait()

            up = ups.get(k, p)
            gate = held_ref.at[:, :, pl.ds(pl.multiple_of(k * s.width + at, LANES), size)]
            for e in range(s.local):
                x = x_ref[k, s.at(e), at : at + size]
                g_acc[e] += dot_t(x, gate[e])
                u_acc[e] += dot_t(x, up[e])
            ups.free(k, p)
        return 0

    lax.fori_loop(0, s.slices, step, 0)
    for e in range(s.local):
        g, u = g_acc[e], u_acc[e]
        sigma = jax.nn.sigmoid(g)
        act_ref[e] = (g * sigma * u).astype(BF16)
        p_ref[e] = u * sigma * (1.0 + g * (1.0 - sigma))
        q_ref[e] = g * sigma


def to_tokens(s, k, at, found, back_ref, outs):
    sums = dot(back_ref[...], jnp.concatenate(found, axis=0)).astype(BF16)
    size = sums.shape[-1]
    sums = sums.reshape(s.grid.nx, s.column, size)
    for c, out in enumerate(outs):

        @pl.when(k >> log2(s.grid.ny) == c)
        def _():
            out[:, k & (s.grid.ny - 1), :, at : at + size] = sums


def down_kernel(s, *refs):
    first = 2 * s.grid.nc
    blocks = refs[:first]
    select_ref, gate_ref, back_ref, act_ref, p_ref, q_ref, w_ref = refs[first : first + 7]
    outs, (d_ref, dg_ref, du_ref, room, sems, acc) = refs[first + 7 : -6], refs[-6:]
    weights = Stream(s, w_ref, room, sems, s.grid.source)
    for k, picked in routed(s, blocks, select_ref[...]):
        d_ref[s.grid.source(k)] = (picked * gate_ref[:, :1]).astype(BF16)
    acc[...] = jnp.zeros_like(acc)

    def step(k, _):
        for p, (at, size) in enumerate(s.pieces):
            weight = weights.get(k, p)
            found = []
            for e in range(s.local):
                found.append((dot(act_ref[e], weight[e]) * gate_ref[s.at(e), :1]).astype(BF16))
                acc[e] += dot_t(d_ref[s.grid.source(k), s.at(e), at : at + size], weight[e])
            to_tokens(s, k, at, found, back_ref, outs)
            weights.free(k, p)
        return 0

    lax.fori_loop(0, s.slices, step, 0)
    for e in range(s.local):
        dg_ref[e] = (acc[e] * p_ref[e]).astype(BF16)
        du_ref[e] = (acc[e] * q_ref[e]).astype(BF16)


def backward_kernel(s, dg_ref, du_ref, back_ref, held_ref, w_ref, _, *refs):
    outs, (room, sems) = refs[:-2], refs[-2:]
    weights = Stream(s, w_ref, room, sems, s.grid.source)

    def step(k, _):
        for p, (at, size) in enumerate(s.pieces):
            gate = held_ref.at[:, :, pl.ds(pl.multiple_of(s.grid.source(k) * s.width + at, LANES), size)]
            up = weights.get(k, p)
            found = [(dot(dg_ref[e], gate[e]) + dot(du_ref[e], up[e])).astype(BF16) for e in range(s.local)]
            to_tokens(s, k, at, found, back_ref, outs)
            weights.free(k, p)
        return 0

    lax.fori_loop(0, s.slices, step, 0)


def turn(s, left_ref, turned):
    for e in range(s.local):
        turned[e] = jnp.transpose(left_ref[e].astype(F32)).astype(BF16)


def grads_kernel(s, count, *refs):
    lefts, rows_refs = refs[:count], refs[count : 2 * count]
    outs, (marker, turned, store, sems) = refs[2 * count + 1 : -4], refs[-4:]
    marker[...] = jnp.zeros_like(marker)
    pieces = len(s.pieces)

    def copy(out, k, p):
        at, size = s.pieces[p]
        slot = lax.rem(k, 2) * pieces + p
        start = pl.multiple_of(k * s.width + at, LANES)
        return pltpu.make_async_copy(
            store.at[slot, :, :, pl.ds(0, size)], out.at[:, :, pl.ds(start, size)], sems.at[slot]
        )

    for left_ref, rows_ref, out in zip(lefts, rows_refs, outs):
        turn(s, left_ref, turned)

        def step(k, _):
            for p, (at, size) in enumerate(s.pieces):

                @pl.when(k >= 2)
                def _():
                    copy(out, k - 2, p).wait()

                for e in range(s.local):
                    rows = rows_ref[k, s.at(e), at : at + size]
                    store[lax.rem(k, 2) * pieces + p, e, :, :size] = dot(turned[e], rows).astype(BF16)
                copy(out, k, p).start()
            return 0

        lax.fori_loop(0, s.slices, step, 0)
        for k in range(max(0, s.slices - 2), s.slices):
            for p in range(pieces):
                copy(out, k, p).wait()


def grads(s, name, lefts, rights, after):
    room = max(size for _, size in s.pieces)
    count = len(lefts)
    slots = 2 * len(s.pieces)
    return call(
        functools.partial(grads_kernel, s, count),
        name,
        [shaped(BF16, s.local, s.hidden, s.features)] * count + [shaped(F32, 8, LANES)],
        [*lefts, *rights, after],
        specs=[VECTORS] * (2 * count) + [ANYWHERE],
        out_specs=[ANYWHERE] * count + [VECTORS],
        scratch=[
            pltpu.VMEM((s.local, s.hidden, s.rows), BF16),
            pltpu.VMEM((slots, s.local, s.hidden, room), BF16),
            pltpu.SemaphoreType.DMA((slots,)),
        ],
        cost=46000,
    )


def body(tokens, cotangent, expert_ids, gate_values, w_gate, w_up, w_down):
    grid = Grid(lax.axis_size("dp"), lax.axis_size("hst"))
    s = Sizes(grid, tokens, w_gate)

    sources = [tokens, expert_ids.T, gate_values.T, cotangent]
    message, cotangent = call(
        pack_kernel,
        "pack",
        [shaped(BF16, s.block, s.width + LANES), shaped(BF16, s.block, s.width)],
        [hbm(source) for source in sources],
        specs=[ANYWHERE] * 4,
        scratch=[pltpu.VMEM(a.shape, a.dtype) for a in sources[:3]] + [pltpu.SemaphoreType.DMA((4,))],
    )
    x_parts = grid.along_z(message)
    x_column, cotangent = stack(x_parts, [], "stack_tokens", [cotangent])
    x_plane = grid.over_plane(x_column)
    d_column, held_gate = doubled_along_z(grid, cotangent, lambda after: hold(s, w_gate, after))
    x_others = stack([x_plane[at] for at in grid.square[1:]], [d_column], "stack_tokens_plane")
    x_blocks = grid.over_cores(x_column, x_others)
    d_column = stack([d_column], [x_others], "stack_cotangents")
    d_plane = grid.over_plane(d_column)
    room = max(size for _, size in s.pieces)
    slots = 2 * len(s.pieces)
    streams = [pltpu.VMEM((slots, s.local, s.hidden, room), BF16), pltpu.SemaphoreType.DMA((slots,))]

    hidden_shape = (s.local, s.rows, s.hidden)
    sums_room = pltpu.VMEM(hidden_shape, F32)
    rows_shape = shaped(BF16, s.slices, s.total, s.width)
    x_rows, select, back, gate, act, p, q, held_gate = call(
        functools.partial(gate_up_kernel, s),
        "gate_up",
        [
            rows_shape,
            shaped(BF16, s.total, s.count),
            shaped(BF16, s.count, s.total),
            shaped(F32, s.total, LANES),
            shaped(BF16, *hidden_shape),
            shaped(F32, *hidden_shape),
            shaped(F32, *hidden_shape),
            pltpu.VMEM(w_gate.shape, BF16),
        ],
        [*x_blocks, held_gate, hbm(w_gate), hbm(w_up), d_column],
        specs=[VECTORS] * (len(x_blocks) + 1) + [ANYWHERE] * 3,
        aliases={len(x_blocks): 7},
        scratch=[*streams, pltpu.SemaphoreType.DMA((s.slices * len(s.pieces),)), sums_room, sums_room],
        cost=46000,
    )
    d_others = stack([d_plane[at] for at in grid.square[1:]], [gate], "stack_cotangents_plane")
    d_blocks = grid.over_cores(d_column, d_others)
    sums = shaped(BF16, grid.nx, grid.ny, s.column, s.width)
    *out_parts, d_rows, d_gate, d_up = call(
        functools.partial(down_kernel, s),
        "down",
        [sums] * grid.nc + [rows_shape, shaped(BF16, *hidden_shape), shaped(BF16, *hidden_shape)],
        [*d_blocks, select, gate, back, act, p, q, hbm(w_down)],
        specs=[VECTORS] * (len(d_blocks) + 6) + [ANYWHERE],
        scratch=[*streams, sums_room],
        cost=46000,
    )
    mixed_kept = back_over_cores(grid, out_parts, [], "mixed_cores")
    back_parts = call(
        functools.partial(backward_kernel, s),
        "backward",
        [sums] * grid.nc,
        [d_gate, d_up, back, held_gate, hbm(w_up), mixed_kept[0]],
        specs=[VECTORS] * 4 + [ANYWHERE] * 2,
        scratch=streams,
        cost=46000,
    )
    *mixed_total, last = back_over_plane(grid, mixed_kept, back_parts[:1], "mixed_plane", back_parts[-1:])
    token_kept = back_over_cores(grid, [*back_parts[:-1], last], [], "tokens_cores")
    grad_gate, grad_down, done = grads(s, "grad_gate_down", [d_gate, act], [x_rows, d_rows], token_kept[0])
    token_total = back_over_plane(grid, token_kept, [done], "tokens_plane")
    grad_up, done = grads(s, "grad_up", [d_up], [x_rows], token_total[0])
    mixed, grad_tokens = finish(back_along_z(grid, mixed_total), back_along_z(grid, token_total), [done])
    return mixed, grad_tokens, grad_gate, grad_up, grad_down


def solution(mesh):
    return jax.shard_map(
        body,
        mesh=mesh,
        in_specs=(
            P("dp", "hst"),
            P("dp", "hst"),
            P("dp", None),
            P("dp", None),
            P("hst", "dp", None),
            P("hst", "dp", None),
            P("hst", "dp", None),
        ),
        out_specs=(
            P("dp", "hst"),
            P("dp", "hst"),
            P("hst", "dp", None),
            P("hst", "dp", None),
            P("hst", "dp", None),
        ),
        check_vma=False,
    )
```

profile of v0, /device:TPU:0, one launch (start us, length us, event | category | flops | bytes accessed | tf_op | source)
XLA Modules:
  0.0 109.9 jit_solution(10727392137347406727)
XLA Ops:
  0.6 1.0 pack.1
  1.6 5.1 %collective-permute-start.2 = (bf16[16,1920]{1,0:T(8,128)(2,1)S(1)}, bf16[16,1920]{1,0:T(8,128)(2,1)S(1)}, u32[]{:S(2)}, u32[]{:S(2)}) collective-permute-start(bf16[16,1920]{1,0:T(8,128)(2,1)S(1)} %get-tuple-element.48.refs_0_), channel_id=1, source_target_pairs={{0,24},{1,25},{2,26},{3,27},{4,28},{5,29},{6,30},{7,31},{8,16},{9,... | collective-permute-start | bytes 184328 | tf_op jit(solution)/shard_map/ppermute | solution.py:53
  6.8 0.0 collective-permute-start.1
  6.8 0.6 collective-permute-start
  7.4 1.8 %collective-permute-done.2.refs_3_ = bf16[16,1920]{1,0:T(8,128)(2,1)S(1)} collective-permute-done((bf16[16,1920]{1,0:T(8,128)(2,1)S(1)}, bf16[16,1920]{1,0:T(8,128)(2,1)S(1)}, u32[]{:S(2)}, u32[]{:S(2)}) %collective-permute-start.2) | collective-permute-done | bytes 61472 | tf_op jit(solution)/shard_map/ppermute | solution.py:53
  9.2 2.8 %collective-permute-done.1.refs_2_ = bf16[16,1920]{1,0:T(8,128)(2,1)S(1)} collective-permute-done((bf16[16,1920]{1,0:T(8,128)(2,1)S(1)}, bf16[16,1920]{1,0:T(8,128)(2,1)S(1)}, u32[]{:S(2)}, u32[]{:S(2)}) %collective-permute-start.1) | collective-permute-done | bytes 61472 | tf_op jit(solution)/shard_map/ppermute | solution.py:53
  12.1 0.0 collective-permute-done.refs_1_
  12.1 1.2 %collective-permute-start.3 = (bf16[16,1792]{1,0:T(8,128)(2,1)S(1)}, bf16[16,1792]{1,0:T(8,128)(2,1)S(1)}, u32[]{:S(2)}, u32[]{:S(2)}) collective-permute-start(bf16[16,1792]{1,0:T(8,128)(2,1)S(1)} %get-tuple-element.50.refs_0_), channel_id=1, source_target_pairs={{0,8},{1,9},{2,10},{3,11},{4,12},{5,13},{6,14},{7,15},{8,0},{9,1},... | collective-permute-start | bytes 172040 | tf_op jit(solution)/shard_map/ppermute | solution.py:53
  13.3 2.4 %collective-permute-start.7 = (bf16[64,1920]{1,0:T(8,128)(2,1)S(1)}, bf16[64,1920]{1,0:T(8,128)(2,1)S(1)}, u32[]{:S(2)}, u32[]{:S(2)}) collective-permute-start(bf16[64,1920]{1,0:T(8,128)(2,1)S(1)} %get-tuple-element.51.refs_0_), channel_id=1, source_target_pairs={{0,6},{1,7},{2,4},{3,5},{4,2},{5,3},{6,0},{7,1},{8,14},{9,15},{10,... | collective-permute-start | bytes 737288 | tf_op jit(solution)/shard_map/ppermute | solution.py:53
  15.7 0.5 collective-permute-start.6
  16.2 0.5 collective-permute-start.5
  16.8 0.0 collective-permute-done.3.refs_1_
  16.8 2.2 %collective-permute-start.4 = (bf16[32,1792]{1,0:T(8,128)(2,1)S(1)}, bf16[32,1792]{1,0:T(8,128)(2,1)S(1)}, u32[]{:S(2)}, u32[]{:S(2)}) collective-permute-start(bf16[32,1792]{1,0:T(8,128)(2,1)S(1)} %double.2._.refs_0_), channel_id=1, source_target_pairs={{0,16},{1,17},{2,18},{3,19},{4,20},{5,21},{6,22},{7,23},{8,24},{9,... | collective-permute-start | bytes 344072 | tf_op jit(solution)/shard_map/ppermute | solution.py:53
  19.0 3.6 %hold_gate.1.refs_2_.refs_4_ = bf16[2,608,7168]{2,1,0:T(8,128)(2,1)S(1)} custom-call(bf16[2,608,7168]{2,1,0:T(8,128)(2,1)} %refs_5_.1, bf16[32,1792]{1,0:T(8,128)(2,1)S(1)} %double.2._.refs_0_), custom_call_target="tpu_custom_call" | custom-call | flops 12000000000 | tf_op jit(solution)/shard_map/hold_gate/pallas_call | solution.py:77
  22.6 1.2 %collective-permute-done.4.refs_1_ = bf16[32,1792]{1,0:T(8,128)(2,1)S(1)} collective-permute-done((bf16[32,1792]{1,0:T(8,128)(2,1)S(1)}, bf16[32,1792]{1,0:T(8,128)(2,1)S(1)}, u32[]{:S(2)}, u32[]{:S(2)}) %collective-permute-start.4) | collective-permute-done | bytes 114720 | tf_op jit(solution)/shard_map/ppermute | solution.py:53
  23.8 0.0 collective-permute-done.7.refs_2_
  23.8 2.1 %collective-permute-done.6.refs_1_ = bf16[64,1920]{1,0:T(8,128)(2,1)S(1)} collective-permute-done((bf16[64,1920]{1,0:T(8,128)(2,1)S(1)}, bf16[64,1920]{1,0:T(8,128)(2,1)S(1)}, u32[]{:S(2)}, u32[]{:S(2)}) %collective-permute-start.6) | collective-permute-done | bytes 245792 | tf_op jit(solution)/shard_map/ppermute | solution.py:53
  25.9 0.0 collective-permute-done.5.refs_0_
  25.9 0.1 stack_tokens_plane.1.refs_1_
  26.0 0.1 collective-permute-start.12
  26.1 0.5 collective-permute-start.11
  26.6 2.4 %collective-permute-start.10 = (bf16[64,1792]{1,0:T(8,128)(2,1)S(1)}, bf16[64,1792]{1,0:T(8,128)(2,1)S(1)}, u32[]{:S(2)}, u32[]{:S(2)}) collective-permute-start(bf16[64,1792]{1,0:T(8,128)(2,1)S(1)} %stack_cotangents.1.refs_7_.refs_0_), channel_id=1, source_target_pairs={{0,6},{1,7},{2,4},{3,5},{4,2},{5,3},{6,0},{7,1},{8,14},{9,15},{10,... | collective-permute-start | bytes 688136 | tf_op jit(solution)/shard_map/ppermute | solution.py:53
  29.0 0.5 collective-permute-start.9
  29.5 0.6 collective-permute-start.8
  30.1 0.0 collective-permute-done.11.refs_2_
  30.1 0.0 collective-permute-done.12.refs_3_
  30.1 13.5 %gate_up.1 = (bf16[4,64,1792]{2,1,0:T(8,128)(2,1)S(1)}, bf16[64,128]{1,0:T(8,128)(2,1)S(1)}, bf16[128,64]{1,0:T(8,128)(2,1)S(1)}, f32[64,128]{1,0:T(8,128)S(1)},...) custom-call(bf16[64,1920]{1,0:T(8,128)(2,1)S(1)} %get-tuple-element., ...), custom_call_target="tpu_custom_call", output_to_operand_aliasing={{7}: (4, {})} | custom-call | flops 46000001024 | tf_op jit(solution)/shard_map/gate_up/pallas_call | solution.py:77
  43.6 0.0 collective-permute-done.9.refs_1_
  43.7 0.1 collective-permute-start.14
  43.8 0.5 collective-permute-start.13
  44.3 2.0 %collective-permute-done.13.refs_2_ = bf16[64,1792]{1,0:T(8,128)(2,1)S(1)} collective-permute-done((bf16[64,1792]{1,0:T(8,128)(2,1)S(1)}, bf16[64,1792]{1,0:T(8,128)(2,1)S(1)}, u32[]{:S(2)}, u32[]{:S(2)}) %collective-permute-start.13) | collective-permute-done | bytes 229408 | tf_op jit(solution)/shard_map/ppermute | solution.py:53
  46.3 0.0 collective-permute-done.14.refs_3_
  46.3 11.7 %down.1 = (bf16[2,2,64,1792]{3,2,1,0:T(8,128)(2,1)S(1)}, bf16[2,2,64,1792]{3,2,1,0:T(8,128)(2,1)S(1)}, bf16[4,64,1792]{2,1,0:T(8,128)(2,1)S(1)}, bf16[2,32,608]{2,1,0:T(8,128)(2,1)S(1)}, bf16[2,32,608]{2,1,0:T(8,128)(2,1)S(1)}) custom-call(bf16[64,1792]{1,0:T(8,128)(2,1)S(1)} %stack_cotangents.1.refs_7_.refs_0_, ...), custom_call_target="tpu_custom_call" | custom-call | flops 46000001024 | tf_op jit(solution)/shard_map/down/pallas_call | solution.py:77
  58.0 0.2 collective-permute-start.15
  58.2 2.4 %collective-permute-done.15.refs_1_ = bf16[2,2,64,1792]{3,2,1,0:T(8,128)(2,1)S(1)} collective-permute-done((bf16[2,2,64,1792]{3,2,1,0:T(8,128)(2,1)S(1)}, bf16[2,2,64,1792]{3,2,1,0:T(8,128)(2,1)S(1)}, u32[]{:S(2)}, u32[]{:S(2)}) %collective-permute-start.15) | collective-permute-done | bytes 917536 | tf_op jit(solution)/shard_map/ppermute | solution.py:53
  60.5 0.2 mixed_cores.1
  60.8 1.5 %collective-permute-start.16 = (bf16[64,1792]{1,0:T(8,128)(2,1)S(1)}, bf16[64,1792]{1,0:T(8,128)(2,1)S(1)}, u32[]{:S(2)}, u32[]{:S(2)}) collective-permute-start(bf16[64,1792]{1,0:T(8,128)(2,1)S(1)} %get-tuple-element.61), channel_id=1, source_target_pairs={{0,2},{1,3},{2,0},{3,1},{4,6},{5,7},{6,4},{7,5},{8,10},{9,11},{10,... | collective-permute-start | bytes 688136 | tf_op jit(solution)/shard_map/ppermute | solution.py:53
  62.2 1.5 %collective-permute-start.17 = (bf16[64,1792]{1,0:T(8,128)(2,1)S(1)}, bf16[64,1792]{1,0:T(8,128)(2,1)S(1)}, u32[]{:S(2)}, u32[]{:S(2)}) collective-permute-start(bf16[64,1792]{1,0:T(8,128)(2,1)S(1)} %get-tuple-element.62), channel_id=1, source_target_pairs={{0,4},{1,5},{2,6},{3,7},{4,0},{5,1},{6,2},{7,3},{8,12},{9,13},{10,... | collective-permute-start | bytes 688136 | tf_op jit(solution)/shard_map/ppermute | solution.py:53
  63.7 0.6 collective-permute-start.18
  64.3 10.1 %backward.1 = (bf16[2,2,64,1792]{3,2,1,0:T(8,128)(2,1)S(1)}, bf16[2,2,64,1792]{3,2,1,0:T(8,128)(2,1)S(1)}) custom-call(bf16[2,32,608]{2,1,0:T(8,128)(2,1)S(1)} %get-tuple-element.64.dg_ref.refs_0_, bf16[2,32,608]{2,1,0:T(8,128)(2,1)S(1)} %get-tuple-element.65.du_ref.refs_0_, bf16[128,64]{1,0:T(8,128)(2,1)S(1)} %get-tuple-element.54.refs_6_.back_ref, ...), custom_call_target="tpu_custom_call" | custom-call | flops 46000001024 | tf_op jit(solution)/shard_map/backward/pallas_call | solution.py:77
  74.5 0.0 collective-permute-done.17.refs_2_
  74.5 0.1 collective-permute-done.18.refs_3_
  74.6 0.1 mixed_plane.1
  74.7 0.1 collective-permute-start.22
  74.8 1.7 %collective-permute-start.19 = (bf16[16,1792]{1,0:T(8,128)(2,1)S(1)}, bf16[16,1792]{1,0:T(8,128)(2,1)S(1)}, u32[]{:S(2)}, u32[]{:S(2)}) collective-permute-start(bf16[16,1792]{1,0:T(8,128)(2,1)S(1)} %get-tuple-element.70), channel_id=1, source_target_pairs={{0,8},{1,9},{2,10},{3,11},{4,12},{5,13},{6,14},{7,15},{8,0},{9,1},... | collective-permute-start | bytes 172040 | tf_op jit(solution)/shard_map/ppermute | solution.py:53
  76.5 0.8 collective-permute-start.20
  77.3 0.0 collective-permute-done.22.refs_1_
  77.3 0.2 tokens_cores.1
  77.5 1.5 %collective-permute-start.23 = (bf16[64,1792]{1,0:T(8,128)(2,1)S(1)}, bf16[64,1792]{1,0:T(8,128)(2,1)S(1)}, u32[]{:S(2)}, u32[]{:S(2)}) collective-permute-start(bf16[64,1792]{1,0:T(8,128)(2,1)S(1)} %get-tuple-element.75), channel_id=1, source_target_pairs={{0,2},{1,3},{2,0},{3,1},{4,6},{5,7},{6,4},{7,5},{8,10},{9,11},{10,... | collective-permute-start | bytes 688136 | tf_op jit(solution)/shard_map/ppermute | solution.py:53
  79.0 1.5 %collective-permute-start.24 = (bf16[64,1792]{1,0:T(8,128)(2,1)S(1)}, bf16[64,1792]{1,0:T(8,128)(2,1)S(1)}, u32[]{:S(2)}, u32[]{:S(2)}) collective-permute-start(bf16[64,1792]{1,0:T(8,128)(2,1)S(1)} %get-tuple-element.76), channel_id=1, source_target_pairs={{0,4},{1,5},{2,6},{3,7},{4,0},{5,1},{6,2},{7,3},{8,12},{9,13},{10,... | collective-permute-start | bytes 688136 | tf_op jit(solution)/shard_map/ppermute | solution.py:53
  80.4 0.6 collective-permute-start.25
  81.0 14.3 %grad_gate_down.1 = (bf16[2,608,7168]{2,1,0:T(8,128)(2,1)}, bf16[2,608,7168]{2,1,0:T(8,128)(2,1)}, f32[8,128]{1,0:T(8,128)S(1)}) custom-call(bf16[2,32,608]{2,1,0:T(8,128)(2,1)S(1)} %get-tuple-element.64.dg_ref.refs_0_, bf16[2,32,608]{2,1,0:T(8,128)(2,1)S(1)} %get-tuple-element.55.refs_7_.refs_1_, ...), custom_call_target="tpu_custom_call" | custom-call | flops 46000001024 | tf_op jit(solution)/shard_map/grad_gate_down/pallas_call | solution.py:77
  95.4 0.0 collective-permute-done.23.refs_1_
  95.4 2.0 %collective-permute-start.21 = (bf16[16,1792]{1,0:T(8,128)(2,1)S(1)}, bf16[16,1792]{1,0:T(8,128)(2,1)S(1)}, u32[]{:S(2)}, u32[]{:S(2)}) collective-permute-start(bf16[16,1792]{1,0:T(8,128)(2,1)S(1)} %get-tuple-element.72), channel_id=1, source_target_pairs={{0,24},{1,25},{2,26},{3,27},{4,28},{5,29},{6,30},{7,31},{8,16},{9,... | collective-permute-start | bytes 172040 | tf_op jit(solution)/shard_map/ppermute | solution.py:53
  97.4 0.0 collective-permute-done.24.refs_2_
  97.4 0.0 collective-permute-done.25.refs_3_
  97.4 0.1 tokens_plane.1
  97.5 0.8 collective-permute-start.26
  98.4 1.7 %collective-permute-start.27 = (bf16[16,1792]{1,0:T(8,128)(2,1)S(1)}, bf16[16,1792]{1,0:T(8,128)(2,1)S(1)}, u32[]{:S(2)}, u32[]{:S(2)}) collective-permute-start(bf16[16,1792]{1,0:T(8,128)(2,1)S(1)} %get-tuple-element.83), channel_id=1, source_target_pairs={{0,16},{1,17},{2,18},{3,19},{4,20},{5,21},{6,22},{7,23},{8,24},{9,... | collective-permute-start | bytes 172040 | tf_op jit(solution)/shard_map/ppermute | solution.py:53
  100.0 2.0 %collective-permute-start.28 = (bf16[16,1792]{1,0:T(8,128)(2,1)S(1)}, bf16[16,1792]{1,0:T(8,128)(2,1)S(1)}, u32[]{:S(2)}, u32[]{:S(2)}) collective-permute-start(bf16[16,1792]{1,0:T(8,128)(2,1)S(1)} %get-tuple-element.84), channel_id=1, source_target_pairs={{0,24},{1,25},{2,26},{3,27},{4,28},{5,29},{6,30},{7,31},{8,16},{9,... | collective-permute-start | bytes 172040 | tf_op jit(solution)/shard_map/ppermute | solution.py:53
  102.0 7.2 %grad_up.1 = (bf16[2,608,7168]{2,1,0:T(8,128)(2,1)}, f32[8,128]{1,0:T(8,128)S(1)}) custom-call(bf16[2,32,608]{2,1,0:T(8,128)(2,1)S(1)} %get-tuple-element.65.du_ref.refs_0_, bf16[4,64,1792]{2,1,0:T(8,128)(2,1)S(1)} %get-tuple-element.78.refs_2_.refs_1_, bf16[16,1792]{1,0:T(8,128)(2,1)S(1)} %get-tuple-element.81.refs_2_.refs_4_), custom_call_target="tpu_custom_call" | custom-call | flops 46000001024 | tf_op jit(solution)/shard_map/grad_up/pallas_call | solution.py:77
  109.2 0.0 collective-permute-done.26.refs_5_
  109.2 0.0 collective-permute-done.27.refs_6_
  109.3 0.7 finish.1
  (12 shorter events, 0.1 us)
Async XLA Ops:
  1.6 7.6 %collective-permute-start.2 = (bf16[16,1920]{1,0:T(8,128)(2,1)S(1)}, bf16[16,1920]{1,0:T(8,128)(2,1)S(1)}, u32[]{:S(2)}, u32[]{:S(2)}) collective-permute-start(bf16[16,1920]{1,0:T(8,128)(2,1)S(1)} %get-tuple-element.48.refs_0_), channel_id=1, source_target_pairs={{0,24},{1,25},{2,26},{3,27},{4,28},{5,29},{6,30},{7,31},{8,16},{9,... | collective-permute-start | bytes 184328 | tf_op jit(solution)/shard_map/ppermute | solution.py:53
  6.8 5.3 %collective-permute-start.1 = (bf16[16,1920]{1,0:T(8,128)(2,1)S(1)}, bf16[16,1920]{1,0:T(8,128)(2,1)S(1)}, u32[]{:S(2)}, u32[]{:S(2)}) collective-permute-start(bf16[16,1920]{1,0:T(8,128)(2,1)S(1)} %get-tuple-element.48.refs_0_), channel_id=1, source_target_pairs={{0,16},{1,17},{2,18},{3,19},{4,20},{5,21},{6,22},{7,23},{8,24},{9,... | collective-permute-start | bytes 184328 | tf_op jit(solution)/shard_map/ppermute | solution.py:53
  6.8 5.3 %collective-permute-start = (bf16[16,1920]{1,0:T(8,128)(2,1)S(1)}, bf16[16,1920]{1,0:T(8,128)(2,1)S(1)}, u32[]{:S(2)}, u32[]{:S(2)}) collective-permute-start(bf16[16,1920]{1,0:T(8,128)(2,1)S(1)} %get-tuple-element.48.refs_0_), channel_id=1, source_target_pairs={{0,8},{1,9},{2,10},{3,11},{4,12},{5,13},{6,14},{7,15},{8,0},{9,1},... | collective-permute-start | bytes 184328 | tf_op jit(solution)/shard_map/ppermute | solution.py:53
  12.1 4.7 %collective-permute-start.3 = (bf16[16,1792]{1,0:T(8,128)(2,1)S(1)}, bf16[16,1792]{1,0:T(8,128)(2,1)S(1)}, u32[]{:S(2)}, u32[]{:S(2)}) collective-permute-start(bf16[16,1792]{1,0:T(8,128)(2,1)S(1)} %get-tuple-element.50.refs_0_), channel_id=1, source_target_pairs={{0,8},{1,9},{2,10},{3,11},{4,12},{5,13},{6,14},{7,15},{8,0},{9,1},... | collective-permute-start | bytes 172040 | tf_op jit(solution)/shard_map/ppermute | solution.py:53
  13.3 10.5 %collective-permute-start.7 = (bf16[64,1920]{1,0:T(8,128)(2,1)S(1)}, bf16[64,1920]{1,0:T(8,128)(2,1)S(1)}, u32[]{:S(2)}, u32[]{:S(2)}) collective-permute-start(bf16[64,1920]{1,0:T(8,128)(2,1)S(1)} %get-tuple-element.51.refs_0_), channel_id=1, source_target_pairs={{0,6},{1,7},{2,4},{3,5},{4,2},{5,3},{6,0},{7,1},{8,14},{9,15},{10,... | collective-permute-start | bytes 737288 | tf_op jit(solution)/shard_map/ppermute | solution.py:53
  15.7 10.2 %collective-permute-start.6 = (bf16[64,1920]{1,0:T(8,128)(2,1)S(1)}, bf16[64,1920]{1,0:T(8,128)(2,1)S(1)}, u32[]{:S(2)}, u32[]{:S(2)}) collective-permute-start(bf16[64,1920]{1,0:T(8,128)(2,1)S(1)} %get-tuple-element.51.refs_0_), channel_id=1, source_target_pairs={{0,4},{1,5},{2,6},{3,7},{4,0},{5,1},{6,2},{7,3},{8,12},{9,13},{10,... | collective-permute-start | bytes 737288 | tf_op jit(solution)/shard_map/ppermute | solution.py:53
  16.2 9.7 %collective-permute-start.5 = (bf16[64,1920]{1,0:T(8,128)(2,1)S(1)}, bf16[64,1920]{1,0:T(8,128)(2,1)S(1)}, u32[]{:S(2)}, u32[]{:S(2)}) collective-permute-start(bf16[64,1920]{1,0:T(8,128)(2,1)S(1)} %get-tuple-element.51.refs_0_), channel_id=1, source_target_pairs={{0,2},{1,3},{2,0},{3,1},{4,6},{5,7},{6,4},{7,5},{8,10},{9,11},{10,... | collective-permute-start | bytes 737288 | tf_op jit(solution)/shard_map/ppermute | solution.py:53
  16.8 7.0 %collective-permute-start.4 = (bf16[32,1792]{1,0:T(8,128)(2,1)S(1)}, bf16[32,1792]{1,0:T(8,128)(2,1)S(1)}, u32[]{:S(2)}, u32[]{:S(2)}) collective-permute-start(bf16[32,1792]{1,0:T(8,128)(2,1)S(1)} %double.2._.refs_0_), channel_id=1, source_target_pairs={{0,16},{1,17},{2,18},{3,19},{4,20},{5,21},{6,22},{7,23},{8,24},{9,... | collective-permute-start | bytes 344072 | tf_op jit(solution)/shard_map/ppermute | solution.py:53
  26.0 4.2 %collective-permute-start.12 = (bf16[192,1920]{1,0:T(8,128)(2,1)S(1)}, bf16[192,1920]{1,0:T(8,128)(2,1)S(1)}, u32[]{:S(2)}, u32[]{:S(2)}) collective-permute-start(bf16[192,1920]{1,0:T(8,128)(2,1)S(1)} %stack_tokens_plane.1.refs_1_), channel_id=1, source_target_pairs={{0,1},{1,0},{2,3},{3,2},{4,5},{5,4},{6,7},{7,6},{8,9},{9,8},{10,11... | collective-permute-start | bytes 2211848 | tf_op jit(solution)/shard_map/ppermute | solution.py:53
  26.1 4.1 %collective-permute-start.11 = (bf16[64,1920]{1,0:T(8,128)(2,1)S(1)}, bf16[64,1920]{1,0:T(8,128)(2,1)S(1)}, u32[]{:S(2)}, u32[]{:S(2)}) collective-permute-start(bf16[64,1920]{1,0:T(8,128)(2,1)S(1)} %get-tuple-element.51.refs_0_), channel_id=1, source_target_pairs={{0,1},{1,0},{2,3},{3,2},{4,5},{5,4},{6,7},{7,6},{8,9},{9,8},{10,11... | collective-permute-start | bytes 737288 | tf_op jit(solution)/shard_map/ppermute | solution.py:53
  26.6 17.1 %collective-permute-start.10 = (bf16[64,1792]{1,0:T(8,128)(2,1)S(1)}, bf16[64,1792]{1,0:T(8,128)(2,1)S(1)}, u32[]{:S(2)}, u32[]{:S(2)}) collective-permute-start(bf16[64,1792]{1,0:T(8,128)(2,1)S(1)} %stack_cotangents.1.refs_7_.refs_0_), channel_id=1, source_target_pairs={{0,6},{1,7},{2,4},{3,5},{4,2},{5,3},{6,0},{7,1},{8,14},{9,15},{10,... | collective-permute-start | bytes 688136 | tf_op jit(solution)/shard_map/ppermute | solution.py:53
  29.0 14.7 %collective-permute-start.9 = (bf16[64,1792]{1,0:T(8,128)(2,1)S(1)}, bf16[64,1792]{1,0:T(8,128)(2,1)S(1)}, u32[]{:S(2)}, u32[]{:S(2)}) collective-permute-start(bf16[64,1792]{1,0:T(8,128)(2,1)S(1)} %stack_cotangents.1.refs_7_.refs_0_), channel_id=1, source_target_pairs={{0,4},{1,5},{2,6},{3,7},{4,0},{5,1},{6,2},{7,3},{8,12},{9,13},{10,... | collective-permute-start | bytes 688136 | tf_op jit(solution)/shard_map/ppermute | solution.py:53
  29.5 14.1 %collective-permute-start.8 = (bf16[64,1792]{1,0:T(8,128)(2,1)S(1)}, bf16[64,1792]{1,0:T(8,128)(2,1)S(1)}, u32[]{:S(2)}, u32[]{:S(2)}) collective-permute-start(bf16[64,1792]{1,0:T(8,128)(2,1)S(1)} %stack_cotangents.1.refs_7_.refs_0_), channel_id=1, source_target_pairs={{0,2},{1,3},{2,0},{3,1},{4,6},{5,7},{6,4},{7,5},{8,10},{9,11},{10,... | collective-permute-start | bytes 688136 | tf_op jit(solution)/shard_map/ppermute | solution.py:53
  43.7 2.5 %collective-permute-start.14 = (bf16[192,1792]{1,0:T(8,128)(2,1)S(1)}, bf16[192,1792]{1,0:T(8,128)(2,1)S(1)}, u32[]{:S(2)}, u32[]{:S(2)}) collective-permute-start(bf16[192,1792]{1,0:T(8,128)(2,1)S(1)} %stack_cotangents_plane.1.refs_1_), channel_id=1, source_target_pairs={{0,1},{1,0},{2,3},{3,2},{4,5},{5,4},{6,7},{7,6},{8,9},{9,8},{10,11... | collective-permute-start | bytes 2064392 | tf_op jit(solution)/shard_map/ppermute | solution.py:53
  43.8 2.5 %collective-permute-start.13 = (bf16[64,1792]{1,0:T(8,128)(2,1)S(1)}, bf16[64,1792]{1,0:T(8,128)(2,1)S(1)}, u32[]{:S(2)}, u32[]{:S(2)}) collective-permute-start(bf16[64,1792]{1,0:T(8,128)(2,1)S(1)} %stack_cotangents.1.refs_7_.refs_0_), channel_id=1, source_target_pairs={{0,1},{1,0},{2,3},{3,2},{4,5},{5,4},{6,7},{7,6},{8,9},{9,8},{10,11... | collective-permute-start | bytes 688136 | tf_op jit(solution)/shard_map/ppermute | solution.py:53
  58.0 2.5 %collective-permute-start.15 = (bf16[2,2,64,1792]{3,2,1,0:T(8,128)(2,1)S(1)}, bf16[2,2,64,1792]{3,2,1,0:T(8,128)(2,1)S(1)}, u32[]{:S(2)}, u32[]{:S(2)}) collective-permute-start(bf16[2,2,64,1792]{3,2,1,0:T(8,128)(2,1)S(1)} %get-tuple-element.59), channel_id=1, source_target_pairs={{0,1},{1,0},{2,3},{3,2},{4,5},{5,4},{6,7},{7,6},{8,9},{9,8},{10,11... | collective-permute-start | bytes 2752520 | tf_op jit(solution)/shard_map/ppermute | solution.py:53
  60.8 13.7 %collective-permute-start.16 = (bf16[64,1792]{1,0:T(8,128)(2,1)S(1)}, bf16[64,1792]{1,0:T(8,128)(2,1)S(1)}, u32[]{:S(2)}, u32[]{:S(2)}) collective-permute-start(bf16[64,1792]{1,0:T(8,128)(2,1)S(1)} %get-tuple-element.61), channel_id=1, source_target_pairs={{0,2},{1,3},{2,0},{3,1},{4,6},{5,7},{6,4},{7,5},{8,10},{9,11},{10,... | collective-permute-start | bytes 688136 | tf_op jit(solution)/shard_map/ppermute | solution.py:53
  62.2 12.2 %collective-permute-start.17 = (bf16[64,1792]{1,0:T(8,128)(2,1)S(1)}, bf16[64,1792]{1,0:T(8,128)(2,1)S(1)}, u32[]{:S(2)}, u32[]{:S(2)}) collective-permute-start(bf16[64,1792]{1,0:T(8,128)(2,1)S(1)} %get-tuple-element.62), channel_id=1, source_target_pairs={{0,4},{1,5},{2,6},{3,7},{4,0},{5,1},{6,2},{7,3},{8,12},{9,13},{10,... | collective-permute-start | bytes 688136 | tf_op jit(solution)/shard_map/ppermute | solution.py:53
  63.7 10.8 %collective-permute-start.18 = (bf16[64,1792]{1,0:T(8,128)(2,1)S(1)}, bf16[64,1792]{1,0:T(8,128)(2,1)S(1)}, u32[]{:S(2)}, u32[]{:S(2)}) collective-permute-start(bf16[64,1792]{1,0:T(8,128)(2,1)S(1)} %get-tuple-element.63), channel_id=1, source_target_pairs={{0,6},{1,7},{2,4},{3,5},{4,2},{5,3},{6,0},{7,1},{8,14},{9,15},{10,... | collective-permute-start | bytes 688136 | tf_op jit(solution)/shard_map/ppermute | solution.py:53
  74.7 2.6 %collective-permute-start.22 = (bf16[2,2,64,1792]{3,2,1,0:T(8,128)(2,1)S(1)}, bf16[2,2,64,1792]{3,2,1,0:T(8,128)(2,1)S(1)}, u32[]{:S(2)}, u32[]{:S(2)}) collective-permute-start(bf16[2,2,64,1792]{3,2,1,0:T(8,128)(2,1)S(1)} %get-tuple-element.73), channel_id=1, source_target_pairs={{0,1},{1,0},{2,3},{3,2},{4,5},{5,4},{6,7},{7,6},{8,9},{9,8},{10,11... | collective-permute-start | bytes 2752520 | tf_op jit(solution)/shard_map/ppermute | solution.py:53
  74.8 25.3 %collective-permute-start.19 = (bf16[16,1792]{1,0:T(8,128)(2,1)S(1)}, bf16[16,1792]{1,0:T(8,128)(2,1)S(1)}, u32[]{:S(2)}, u32[]{:S(2)}) collective-permute-start(bf16[16,1792]{1,0:T(8,128)(2,1)S(1)} %get-tuple-element.70), channel_id=1, source_target_pairs={{0,8},{1,9},{2,10},{3,11},{4,12},{5,13},{6,14},{7,15},{8,0},{9,1},... | collective-permute-start | bytes 172040 | tf_op jit(solution)/shard_map/ppermute | solution.py:53
  76.5 32.7 %collective-permute-start.20 = (bf16[16,1792]{1,0:T(8,128)(2,1)S(1)}, bf16[16,1792]{1,0:T(8,128)(2,1)S(1)}, u32[]{:S(2)}, u32[]{:S(2)}) collective-permute-start(bf16[16,1792]{1,0:T(8,128)(2,1)S(1)} %get-tuple-element.71), channel_id=1, source_target_pairs={{0,16},{1,17},{2,18},{3,19},{4,20},{5,21},{6,22},{7,23},{8,24},{9,... | collective-permute-start | bytes 172040 | tf_op jit(solution)/shard_map/ppermute | solution.py:53
  77.5 17.9 %collective-permute-start.23 = (bf16[64,1792]{1,0:T(8,128)(2,1)S(1)}, bf16[64,1792]{1,0:T(8,128)(2,1)S(1)}, u32[]{:S(2)}, u32[]{:S(2)}) collective-permute-start(bf16[64,1792]{1,0:T(8,128)(2,1)S(1)} %get-tuple-element.75), channel_id=1, source_target_pairs={{0,2},{1,3},{2,0},{3,1},{4,6},{5,7},{6,4},{7,5},{8,10},{9,11},{10,... | collective-permute-start | bytes 688136 | tf_op jit(solution)/shard_map/ppermute | solution.py:53
  79.0 18.5 %collective-permute-start.24 = (bf16[64,1792]{1,0:T(8,128)(2,1)S(1)}, bf16[64,1792]{1,0:T(8,128)(2,1)S(1)}, u32[]{:S(2)}, u32[]{:S(2)}) collective-permute-start(bf16[64,1792]{1,0:T(8,128)(2,1)S(1)} %get-tuple-element.76), channel_id=1, source_target_pairs={{0,4},{1,5},{2,6},{3,7},{4,0},{5,1},{6,2},{7,3},{8,12},{9,13},{10,... | collective-permute-start | bytes 688136 | tf_op jit(solution)/shard_map/ppermute | solution.py:53
  80.4 17.0 %collective-permute-start.25 = (bf16[64,1792]{1,0:T(8,128)(2,1)S(1)}, bf16[64,1792]{1,0:T(8,128)(2,1)S(1)}, u32[]{:S(2)}, u32[]{:S(2)}) collective-permute-start(bf16[64,1792]{1,0:T(8,128)(2,1)S(1)} %get-tuple-element.77), channel_id=1, source_target_pairs={{0,6},{1,7},{2,4},{3,5},{4,2},{5,3},{6,0},{7,1},{8,14},{9,15},{10,... | collective-permute-start | bytes 688136 | tf_op jit(solution)/shard_map/ppermute | solution.py:53
  95.4 13.8 %collective-permute-start.21 = (bf16[16,1792]{1,0:T(8,128)(2,1)S(1)}, bf16[16,1792]{1,0:T(8,128)(2,1)S(1)}, u32[]{:S(2)}, u32[]{:S(2)}) collective-permute-start(bf16[16,1792]{1,0:T(8,128)(2,1)S(1)} %get-tuple-element.72), channel_id=1, source_target_pairs={{0,24},{1,25},{2,26},{3,27},{4,28},{5,29},{6,30},{7,31},{8,16},{9,... | collective-permute-start | bytes 172040 | tf_op jit(solution)/shard_map/ppermute | solution.py:53
  97.5 11.7 %collective-permute-start.26 = (bf16[16,1792]{1,0:T(8,128)(2,1)S(1)}, bf16[16,1792]{1,0:T(8,128)(2,1)S(1)}, u32[]{:S(2)}, u32[]{:S(2)}) collective-permute-start(bf16[16,1792]{1,0:T(8,128)(2,1)S(1)} %get-tuple-element.82), channel_id=1, source_target_pairs={{0,8},{1,9},{2,10},{3,11},{4,12},{5,13},{6,14},{7,15},{8,0},{9,1},... | collective-permute-start | bytes 172040 | tf_op jit(solution)/shard_map/ppermute | solution.py:53
  98.4 10.9 %collective-permute-start.27 = (bf16[16,1792]{1,0:T(8,128)(2,1)S(1)}, bf16[16,1792]{1,0:T(8,128)(2,1)S(1)}, u32[]{:S(2)}, u32[]{:S(2)}) collective-permute-start(bf16[16,1792]{1,0:T(8,128)(2,1)S(1)} %get-tuple-element.83), channel_id=1, source_target_pairs={{0,16},{1,17},{2,18},{3,19},{4,20},{5,21},{6,22},{7,23},{8,24},{9,... | collective-permute-start | bytes 172040 | tf_op jit(solution)/shard_map/ppermute | solution.py:53
  100.0 9.2 %collective-permute-start.28 = (bf16[16,1792]{1,0:T(8,128)(2,1)S(1)}, bf16[16,1792]{1,0:T(8,128)(2,1)S(1)}, u32[]{:S(2)}, u32[]{:S(2)}) collective-permute-start(bf16[16,1792]{1,0:T(8,128)(2,1)S(1)} %get-tuple-element.84), channel_id=1, source_target_pairs={{0,24},{1,25},{2,26},{3,27},{4,28},{5,29},{6,30},{7,31},{8,16},{9,... | collective-permute-start | bytes 172040 | tf_op jit(solution)/shard_map/ppermute | solution.py:53
where the time goes:
time: 110 us
  Pallas kernels  63 us (57%)
  starting transfers between devices  33.7 us (31%)
  waiting for transfers between devices  12.4 us (11%)
    pallas_call x18, Pallas kernels, call(): pl.pallas_call(kernel, name=name, grid=grid, out_shape=outs, in_specs=spe...  63 us
    ppermute x29, starting transfers between devices, shift(): return lax.ppermute(value, AXES, pairs)  33.7 us
    ppermute x29, waiting for transfers between devices, shift(): return lax.ppermute(value, AXES, pairs)  12.4 us
  transfers between devices with their start and end apart: 29, of which 7 were waited for; matrix products, arithmetic and copies ran while one was open for 0% of the time, Pallas kernels for 45%

commit v1 on v0

--- a/solution.py
+++ b/solution.py
@@ -12,6 +12,7 @@
 LANES = 128
 MIB = 1 << 20
 MFLOP = 10**6
+EARLY = 2
 F32 = jnp.float32
 BF16 = jnp.bfloat16
 AXES = ("dp", "hst")
@@ -231,9 +232,9 @@
 
 
 class Stream:
-    def __init__(self, s, weight, room, sems, place):
+    def __init__(self, s, weight, room, sems, place, first=0):
         self.s, self.weight, self.room, self.sems, self.place = s, weight, room, sems, place
-        for k in range(min(2, s.slices)):
+        for k in range(first, min(first + 2, s.slices)):
             for p in range(len(s.pieces)):
                 self.copy(k, p).start()
 
@@ -265,9 +266,15 @@
 
 
 def hold_kernel(s, weight, _, held, sems):
-    copies = [held_copy(s, weight, held, sems, k, p) for k in range(s.early) for p in range(len(s.pieces))]
-    for copy in copies:
-        copy.start()
+    copies = []
+    for k in range(s.early):
+        for at, size in s.pieces:
+            source = pl.ds(pl.multiple_of(s.grid.source(k) * s.width + at, LANES), size)
+            target = pl.ds(k * s.width + at, size)
+            copies.append(
+                pltpu.make_async_copy(weight.at[:, :, source], held.at[:, :, target], sems.at[len(copies)])
+            )
+            copies[-1].start()
     for copy in copies:
         copy.wait()
 
@@ -275,8 +282,8 @@
 def hold(s, weight, after):
     (held,) = call(
         functools.partial(hold_kernel, s),
-        "hold_gate",
-        [pltpu.VMEM(weight.shape, BF16)],
+        "hold_down",
+        [pltpu.VMEM((s.local, s.hidden, s.early * s.width), BF16)],
         [hbm(weight), after],
         specs=[ANYWHERE] * 2,
         scratch=[pltpu.SemaphoreType.DMA((s.early * len(s.pieces),))],
@@ -298,7 +305,7 @@
         self.slices = grid.nc * grid.ny
         whole = self.width % 256 == 0 and self.width > 1024
         self.pieces = [(0, 1024), (1024, self.width - 1024)] if whole else [(0, self.width)]
-        self.early = self.slices // 2
+        self.early = self.slices // EARLY
 
     def block_of(self, blocks, c, a, b):
         n = self.grid.square.index((a, b)) - 1
@@ -316,10 +323,10 @@
 
 def gate_up_kernel(s, *refs):
     blocks, refs = refs[: 2 * s.grid.nc], refs[2 * s.grid.nc :]
-    _, wg_ref, wu_ref, _, x_ref, select_ref, back_ref, gate_ref, act_ref, p_ref, q_ref, held_ref = refs[:12]
-    room, sems, held_sems, g_acc, u_acc = refs[12:]
+    wg_ref, wu_ref, _, x_ref, select_ref, back_ref, gate_ref, act_ref, p_ref, q_ref, held_ref = refs[:11]
+    room, sems, held_sems, g_acc, u_acc = refs[11:]
     ups = Stream(s, wu_ref, room, sems, lambda k: k)
-    for k in range(s.early, min(2, s.slices)):
+    for k in range(min(2, s.slices)):
         for p in range(len(s.pieces)):
             held_copy(s, wg_ref, held_ref, held_sems, k, p).start()
     aux = jnp.concatenate([s.block_of(blocks, 0, a, 0)[:, s.width :] for a in range(s.grid.nx)], axis=0)
@@ -335,14 +342,11 @@
     def step(k, _):
         for p, (at, size) in enumerate(s.pieces):
 
-            @pl.when((k + 2 >= s.early) & (k + 2 < s.slices))
+            @pl.when(k + 2 < s.slices)
             def _():
                 held_copy(s, wg_ref, held_ref, held_sems, k + 2, p).start()
 
-            @pl.when(k >= s.early)
-            def _():
-                held_copy(s, wg_ref, held_ref, held_sems, k, p).wait()
-
+            held_copy(s, wg_ref, held_ref, held_sems, k, p).wait()
             up = ups.get(k, p)
             gate = held_ref.at[:, :, pl.ds(pl.multiple_of(k * s.width + at, LANES), size)]
             for e in range(s.local):
@@ -372,12 +376,33 @@
             out[:, k & (s.grid.ny - 1), :, at : at + size] = sums
 
 
-def down_kernel(s, *refs):
-    first = 2 * s.grid.nc
-    blocks = refs[:first]
-    select_ref, gate_ref, back_ref, act_ref, p_ref, q_ref, w_ref = refs[first : first + 7]
-    outs, (d_ref, dg_ref, du_ref, room, sems, acc) = refs[first + 7 : -6], refs[-6:]
-    weights = Stream(s, w_ref, room, sems, s.grid.source)
+def forward_kernel(s, act_ref, gate_ref, back_ref, held_ref, w_ref, _, *refs):
+    outs, (room, sems) = refs[:-2], refs[-2:]
+    weights = Stream(s, w_ref, room, sems, s.grid.source, s.early)
+
+    def step(k, _):
+        for p, (at, size) in enumerate(s.pieces):
+            use(k, p, at, weights.get(k, p))
+            weights.free(k, p)
+        return 0
+
+    def use(k, p, at, weight):
+        found = [(dot(act_ref[e], weight[e]) * gate_ref[s.at(e), :1]).astype(BF16) for e in range(s.local)]
+        to_tokens(s, k, at, found, back_ref, outs)
+
+    def early(k, _):
+        for p, (at, size) in enumerate(s.pieces):
+            use(k, p, at, held_ref.at[:, :, pl.ds(pl.multiple_of(k * s.width + at, LANES), size)])
+        return 0
+
+    lax.fori_loop(0, s.early, early, 0)
+    lax.fori_loop(s.early, s.slices, step, 0)
+
+
+def hidden_grads_kernel(s, *refs):
+    blocks, refs = refs[: 2 * s.grid.nc], refs[2 * s.grid.nc :]
+    select_ref, gate_ref, p_ref, q_ref, w_ref, _, d_ref, dg_ref, du_ref, room, sems, acc = refs
+    weights = Stream(s, w_ref, room, sems, lambda k: k)
     for k, picked in routed(s, blocks, select_ref[...]):
         d_ref[s.grid.source(k)] = (picked * gate_ref[:, :1]).astype(BF16)
     acc[...] = jnp.zeros_like(acc)
@@ -385,11 +410,8 @@
     def step(k, _):
         for p, (at, size) in enumerate(s.pieces):
             weight = weights.get(k, p)
-            found = []
             for e in range(s.local):
-                found.append((dot(act_ref[e], weight[e]) * gate_ref[s.at(e), :1]).astype(BF16))
-                acc[e] += dot_t(d_ref[s.grid.source(k), s.at(e), at : at + size], weight[e])
-            to_tokens(s, k, at, found, back_ref, outs)
+                acc[e] += dot_t(d_ref[k, s.at(e), at : at + size], weight[e])
             weights.free(k, p)
         return 0
 
@@ -492,7 +514,7 @@
     x_parts = grid.along_z(message)
     x_column, cotangent = stack(x_parts, [], "stack_tokens", [cotangent])
     x_plane = grid.over_plane(x_column)
-    d_column, held_gate = doubled_along_z(grid, cotangent, lambda after: hold(s, w_gate, after))
+    d_column, held_down = doubled_along_z(grid, cotangent, lambda after: hold(s, w_down, after))
     x_others = stack([x_plane[at] for at in grid.square[1:]], [d_column], "stack_tokens_plane")
     x_blocks = grid.over_cores(x_column, x_others)
     d_column = stack([d_column], [x_others], "stack_cotangents")
@@ -517,25 +539,33 @@
             shaped(F32, *hidden_shape),
             pltpu.VMEM(w_gate.shape, BF16),
         ],
-        [*x_blocks, held_gate, hbm(w_gate), hbm(w_up), d_column],
-        specs=[VECTORS] * (len(x_blocks) + 1) + [ANYWHERE] * 3,
-        aliases={len(x_blocks): 7},
+        [*x_blocks, hbm(w_gate), hbm(w_up), d_column],
+        specs=[VECTORS] * len(x_blocks) + [ANYWHERE] * 3,
         scratch=[*streams, pltpu.SemaphoreType.DMA((s.slices * len(s.pieces),)), sums_room, sums_room],
         cost=46000,
     )
     d_others = stack([d_plane[at] for at in grid.square[1:]], [gate], "stack_cotangents_plane")
     d_blocks = grid.over_cores(d_column, d_others)
     sums = shaped(BF16, grid.nx, grid.ny, s.column, s.width)
-    *out_parts, d_rows, d_gate, d_up = call(
-        functools.partial(down_kernel, s),
-        "down",
-        [sums] * grid.nc + [rows_shape, shaped(BF16, *hidden_shape), shaped(BF16, *hidden_shape)],
-        [*d_blocks, select, gate, back, act, p, q, hbm(w_down)],
-        specs=[VECTORS] * (len(d_blocks) + 6) + [ANYWHERE],
+    out_parts = call(
+        functools.partial(forward_kernel, s),
+        "forward",
+        [sums] * grid.nc,
+        [act, gate, back, held_down, hbm(w_down), d_others],
+        specs=[VECTORS] * 4 + [ANYWHERE] * 2,
+        scratch=streams,
+        cost=46000,
+    )
+    d_rows, d_gate, d_up = call(
+        functools.partial(hidden_grads_kernel, s),
+        "hidden_grads",
+        [rows_shape, shaped(BF16, *hidden_shape), shaped(BF16, *hidden_shape)],
+        [*d_blocks, select, gate, p, q, hbm(w_down), out_parts[0]],
+        specs=[VECTORS] * (len(d_blocks) + 4) + [ANYWHERE] * 2,
         scratch=[*streams, sums_room],
         cost=46000,
     )
-    mixed_kept = back_over_cores(grid, out_parts, [], "mixed_cores")
+    mixed_kept = back_over_cores(grid, out_parts, [d_gate], "mixed_cores")
     back_parts = call(
         functools.partial(backward_kernel, s),
         "backward",

time: 110 us -> 108 us (0.982)
  waiting for transfers between devices: 12.4 us -> 8.02 us
  Pallas kernels: 63 us -> 65.7 us
    ppermute x29, waiting for transfers between devices: 12.4 us -> 8.02 us  [shift(): return lax.ppermute(value, AXES, pairs)]
    pallas_call x18 -> x19, Pallas kernels: 63 us -> 65.7 us  [call(): pl.pallas_call(kernel, name=name, grid=grid, out_shape=outs, in_specs=spe...]
  transfers between devices with their start and end apart: 29 -> 29, of which waited for: 7 -> 4; matrix products, arithmetic and copies ran while one was open for 0% -> 0% of each run, Pallas kernels for 45% -> 59%
where the time goes in v1:
time: 108 us
  Pallas kernels  65.7 us (61%)
  starting transfers between devices  33.6 us (31%)
  waiting for transfers between devices  8.02 us (7%)
    pallas_call x19, Pallas kernels, call(): pl.pallas_call(kernel, name=name, grid=grid, out_shape=outs, in_specs=spe...  65.7 us
    ppermute x29, starting transfers between devices, shift(): return lax.ppermute(value, AXES, pairs)  33.6 us
    ppermute x29, waiting for transfers between devices, shift(): return lax.ppermute(value, AXES, pairs)  8.02 us
  transfers between devices with their start and end apart: 29, of which 4 were waited for; matrix products, arithmetic and copies ran while one was open for 0% of the time, Pallas kernels for 59%

profile of v1, /device:TPU:0, one launch (start us, length us, event | category | flops | bytes accessed | tf_op | source)
XLA Modules:
  0.0 108.2 jit_solution(11129612178876874756)
XLA Ops:
  0.6 1.0 pack.1
  1.6 5.1 %collective-permute-start.2 = (bf16[16,1920]{1,0:T(8,128)(2,1)S(1)}, bf16[16,1920]{1,0:T(8,128)(2,1)S(1)}, u32[]{:S(2)}, u32[]{:S(2)}) collective-permute-start(bf16[16,1920]{1,0:T(8,128)(2,1)S(1)} %get-tuple-element.48.refs_0_), channel_id=1, source_target_pairs={{0,24},{1,25},{2,26},{3,27},{4,28},{5,29},{6,30},{7,31},{8,16},{9,... | collective-permute-start | bytes 184328 | tf_op jit(solution)/shard_map/ppermute | solution.py:54
  6.8 0.0 collective-permute-start.1
  6.8 0.6 collective-permute-start
  7.4 1.8 %collective-permute-done.2.refs_3_ = bf16[16,1920]{1,0:T(8,128)(2,1)S(1)} collective-permute-done((bf16[16,1920]{1,0:T(8,128)(2,1)S(1)}, bf16[16,1920]{1,0:T(8,128)(2,1)S(1)}, u32[]{:S(2)}, u32[]{:S(2)}) %collective-permute-start.2) | collective-permute-done | bytes 61472 | tf_op jit(solution)/shard_map/ppermute | solution.py:54
  9.2 2.8 %collective-permute-done.1.refs_2_ = bf16[16,1920]{1,0:T(8,128)(2,1)S(1)} collective-permute-done((bf16[16,1920]{1,0:T(8,128)(2,1)S(1)}, bf16[16,1920]{1,0:T(8,128)(2,1)S(1)}, u32[]{:S(2)}, u32[]{:S(2)}) %collective-permute-start.1) | collective-permute-done | bytes 61472 | tf_op jit(solution)/shard_map/ppermute | solution.py:54
  12.1 0.0 collective-permute-done.refs_1_
  12.1 1.2 %collective-permute-start.6 = (bf16[16,1792]{1,0:T(8,128)(2,1)S(1)}, bf16[16,1792]{1,0:T(8,128)(2,1)S(1)}, u32[]{:S(2)}, u32[]{:S(2)}) collective-permute-start(bf16[16,1792]{1,0:T(8,128)(2,1)S(1)} %get-tuple-element.51.refs_0_), channel_id=1, source_target_pairs={{0,8},{1,9},{2,10},{3,11},{4,12},{5,13},{6,14},{7,15},{8,0},{9,1},... | collective-permute-start | bytes 172040 | tf_op jit(solution)/shard_map/ppermute | solution.py:54
  13.3 2.4 %collective-permute-start.5 = (bf16[64,1920]{1,0:T(8,128)(2,1)S(1)}, bf16[64,1920]{1,0:T(8,128)(2,1)S(1)}, u32[]{:S(2)}, u32[]{:S(2)}) collective-permute-start(bf16[64,1920]{1,0:T(8,128)(2,1)S(1)} %get-tuple-element.50.refs_0_), channel_id=1, source_target_pairs={{0,6},{1,7},{2,4},{3,5},{4,2},{5,3},{6,0},{7,1},{8,14},{9,15},{10,... | collective-permute-start | bytes 737288 | tf_op jit(solution)/shard_map/ppermute | solution.py:54
  15.7 0.5 collective-permute-start.4
  16.2 0.5 collective-permute-start.3
  16.8 0.0 collective-permute-done.6.refs_1_
  16.8 2.2 %collective-permute-start.7 = (bf16[32,1792]{1,0:T(8,128)(2,1)S(1)}, bf16[32,1792]{1,0:T(8,128)(2,1)S(1)}, u32[]{:S(2)}, u32[]{:S(2)}) collective-permute-start(bf16[32,1792]{1,0:T(8,128)(2,1)S(1)} %double.2._.refs_0_), channel_id=1, source_target_pairs={{0,16},{1,17},{2,18},{3,19},{4,20},{5,21},{6,22},{7,23},{8,24},{9,... | collective-permute-start | bytes 344072 | tf_op jit(solution)/shard_map/ppermute | solution.py:54
  19.0 3.6 %hold_down.1.refs_2_.held_ref = bf16[2,608,3584]{2,1,0:T(8,128)(2,1)S(1)} custom-call(bf16[2,608,7168]{2,1,0:T(8,128)(2,1)} %refs_8_.1, bf16[32,1792]{1,0:T(8,128)(2,1)S(1)} %double.2._.refs_0_), custom_call_target="tpu_custom_call" | custom-call | flops 12000000000 | tf_op jit(solution)/shard_map/hold_down/pallas_call | solution.py:78
  22.6 1.2 %collective-permute-done.7.refs_1_ = bf16[32,1792]{1,0:T(8,128)(2,1)S(1)} collective-permute-done((bf16[32,1792]{1,0:T(8,128)(2,1)S(1)}, bf16[32,1792]{1,0:T(8,128)(2,1)S(1)}, u32[]{:S(2)}, u32[]{:S(2)}) %collective-permute-start.7) | collective-permute-done | bytes 114720 | tf_op jit(solution)/shard_map/ppermute | solution.py:54
  23.8 0.0 collective-permute-done.5.refs_2_
  23.8 2.1 %collective-permute-done.4.refs_1_ = bf16[64,1920]{1,0:T(8,128)(2,1)S(1)} collective-permute-done((bf16[64,1920]{1,0:T(8,128)(2,1)S(1)}, bf16[64,1920]{1,0:T(8,128)(2,1)S(1)}, u32[]{:S(2)}, u32[]{:S(2)}) %collective-permute-start.4) | collective-permute-done | bytes 245792 | tf_op jit(solution)/shard_map/ppermute | solution.py:54
  25.9 0.0 collective-permute-done.3.refs_0_
  25.9 0.1 stack_tokens_plane.1.refs_1_
  26.0 0.1 collective-permute-start.9
  26.1 0.5 collective-permute-start.8
  26.6 0.1 collective-permute-start.14
  26.7 2.3 %collective-permute-start.12 = (bf16[64,1792]{1,0:T(8,128)(2,1)S(1)}, bf16[64,1792]{1,0:T(8,128)(2,1)S(1)}, u32[]{:S(2)}, u32[]{:S(2)}) collective-permute-start(bf16[64,1792]{1,0:T(8,128)(2,1)S(1)} %stack_cotangents.1.refs_6_.refs_0_), channel_id=1, source_target_pairs={{0,6},{1,7},{2,4},{3,5},{4,2},{5,3},{6,0},{7,1},{8,14},{9,15},{10,... | collective-permute-start | bytes 688136 | tf_op jit(solution)/shard_map/ppermute | solution.py:54
  29.1 0.5 collective-permute-start.11
  29.6 0.0 collective-permute-done.8.refs_2_
  29.6 0.6 collective-permute-start.10
  30.2 0.0 collective-permute-done.9.refs_3_
  30.2 14.5 %gate_up.1 = (bf16[4,64,1792]{2,1,0:T(8,128)(2,1)S(1)}, bf16[64,128]{1,0:T(8,128)(2,1)S(1)}, bf16[128,64]{1,0:T(8,128)(2,1)S(1)}, f32[64,128]{1,0:T(8,128)S(1)},...) custom-call(bf16[64,1920]{1,0:T(8,128)(2,1)S(1)} %get-tuple-element., ...), custom_call_target="tpu_custom_call" | custom-call | flops 46000001024 | tf_op jit(solution)/shard_map/gate_up/pallas_call | solution.py:78
  44.7 0.0 collective-permute-done.12.refs_2_
  44.8 0.0 collective-permute-done.11.refs_1_
  44.8 0.0 collective-permute-done.10.refs_0_
  44.8 0.1 collective-permute-start.15
  44.9 5.4 %forward.1 = (bf16[2,2,64,1792]{3,2,1,0:T(8,128)(2,1)S(1)}, bf16[2,2,64,1792]{3,2,1,0:T(8,128)(2,1)S(1)}) custom-call(bf16[2,32,608]{2,1,0:T(8,128)(2,1)S(1)} %get-tuple-element.52.act_ref.refs_1_, f32[64,128]{1,0:T(8,128)S(1)} %get-tuple-element.53.refs_3_.gate_ref.refs_5_, bf16[128,64]{1,0:T(8,128)(2,1)S(1)} %get-tuple-element.54.back_ref, ...), custom_call_target="tpu_custom_call" | custom-call | flops 46000001024 | tf_op jit(solution)/shard_map/forward/pallas_call | solution.py:78
  50.3 0.5 collective-permute-start.13
  50.9 8.0 %hidden_grads.1 = (bf16[4,64,1792]{2,1,0:T(8,128)(2,1)S(1)}, bf16[2,32,608]{2,1,0:T(8,128)(2,1)S(1)}, bf16[2,32,608]{2,1,0:T(8,128)(2,1)S(1)}) custom-call(bf16[64,1792]{1,0:T(8,128)(2,1)S(1)} %stack_cotangents.1.refs_6_.refs_0_, bf16[192,1792]{1,0:T(8,128)(2,1)S(1)} %stack_cotangents_plane.1._.refs_1_, ...), custom_call_target="tpu_custom_call" | custom-call | flops 46000001024 | tf_op jit(solution)/shard_map/hidden_grads/pallas_call | solution.py:78
  58.9 0.0 collective-permute-done.13.refs_1_
  58.9 0.2 mixed_cores.1
  59.1 1.5 %collective-permute-start.16 = (bf16[64,1792]{1,0:T(8,128)(2,1)S(1)}, bf16[64,1792]{1,0:T(8,128)(2,1)S(1)}, u32[]{:S(2)}, u32[]{:S(2)}) collective-permute-start(bf16[64,1792]{1,0:T(8,128)(2,1)S(1)} %get-tuple-element.62), channel_id=1, source_target_pairs={{0,2},{1,3},{2,0},{3,1},{4,6},{5,7},{6,4},{7,5},{8,10},{9,11},{10,... | collective-permute-start | bytes 688136 | tf_op jit(solution)/shard_map/ppermute | solution.py:54
  60.6 1.5 %collective-permute-start.17 = (bf16[64,1792]{1,0:T(8,128)(2,1)S(1)}, bf16[64,1792]{1,0:T(8,128)(2,1)S(1)}, u32[]{:S(2)}, u32[]{:S(2)}) collective-permute-start(bf16[64,1792]{1,0:T(8,128)(2,1)S(1)} %get-tuple-element.63), channel_id=1, source_target_pairs={{0,4},{1,5},{2,6},{3,7},{4,0},{5,1},{6,2},{7,3},{8,12},{9,13},{10,... | collective-permute-start | bytes 688136 | tf_op jit(solution)/shard_map/ppermute | solution.py:54
  62.1 0.6 collective-permute-start.18
  62.7 10.2 %backward.1 = (bf16[2,2,64,1792]{3,2,1,0:T(8,128)(2,1)S(1)}, bf16[2,2,64,1792]{3,2,1,0:T(8,128)(2,1)S(1)}) custom-call(bf16[2,32,608]{2,1,0:T(8,128)(2,1)S(1)} %get-tuple-element.60.refs_2_.dg_ref.refs_0_, bf16[2,32,608]{2,1,0:T(8,128)(2,1)S(1)} %get-tuple-element.65.du_ref.refs_0_, bf16[128,64]{1,0:T(8,128)(2,1)S(1)} %get-tuple-element.54.back_ref, ...), custom_call_target="tpu_custom_call" | custom-call | flops 46000001024 | tf_op jit(solution)/shard_map/backward/pallas_call | solution.py:78
  72.9 0.0 collective-permute-done.17.refs_2_
  72.9 0.0 collective-permute-done.18.refs_3_
  72.9 0.1 mixed_plane.1
  73.0 0.1 collective-permute-start.22
  73.1 1.7 %collective-permute-start.19 = (bf16[16,1792]{1,0:T(8,128)(2,1)S(1)}, bf16[16,1792]{1,0:T(8,128)(2,1)S(1)}, u32[]{:S(2)}, u32[]{:S(2)}) collective-permute-start(bf16[16,1792]{1,0:T(8,128)(2,1)S(1)} %get-tuple-element.70), channel_id=1, source_target_pairs={{0,8},{1,9},{2,10},{3,11},{4,12},{5,13},{6,14},{7,15},{8,0},{9,1},... | collective-permute-start | bytes 172040 | tf_op jit(solution)/shard_map/ppermute | solution.py:54
  74.8 0.8 collective-permute-start.20
  75.6 0.0 collective-permute-done.22.refs_1_
  75.6 0.2 tokens_cores.1
  75.8 1.5 %collective-permute-start.23 = (bf16[64,1792]{1,0:T(8,128)(2,1)S(1)}, bf16[64,1792]{1,0:T(8,128)(2,1)S(1)}, u32[]{:S(2)}, u32[]{:S(2)}) collective-permute-start(bf16[64,1792]{1,0:T(8,128)(2,1)S(1)} %get-tuple-element.75), channel_id=1, source_target_pairs={{0,2},{1,3},{2,0},{3,1},{4,6},{5,7},{6,4},{7,5},{8,10},{9,11},{10,... | collective-permute-start | bytes 688136 | tf_op jit(solution)/shard_map/ppermute | solution.py:54
  77.3 1.5 %collective-permute-start.24 = (bf16[64,1792]{1,0:T(8,128)(2,1)S(1)}, bf16[64,1792]{1,0:T(8,128)(2,1)S(1)}, u32[]{:S(2)}, u32[]{:S(2)}) collective-permute-start(bf16[64,1792]{1,0:T(8,128)(2,1)S(1)} %get-tuple-element.76), channel_id=1, source_target_pairs={{0,4},{1,5},{2,6},{3,7},{4,0},{5,1},{6,2},{7,3},{8,12},{9,13},{10,... | collective-permute-start | bytes 688136 | tf_op jit(solution)/shard_map/ppermute | solution.py:54
  78.7 0.6 collective-permute-start.25
  79.4 14.3 %grad_gate_down.1 = (bf16[2,608,7168]{2,1,0:T(8,128)(2,1)}, bf16[2,608,7168]{2,1,0:T(8,128)(2,1)}, f32[8,128]{1,0:T(8,128)S(1)}) custom-call(bf16[2,32,608]{2,1,0:T(8,128)(2,1)S(1)} %get-tuple-element.60.refs_2_.dg_ref.refs_0_, bf16[2,32,608]{2,1,0:T(8,128)(2,1)S(1)} %get-tuple-element.52.act_ref.refs_1_, ...), custom_call_target="tpu_custom_call" | custom-call | flops 46000001024 | tf_op jit(solution)/shard_map/grad_gate_down/pallas_call | solution.py:78
  93.7 2.0 %collective-permute-start.21 = (bf16[16,1792]{1,0:T(8,128)(2,1)S(1)}, bf16[16,1792]{1,0:T(8,128)(2,1)S(1)}, u32[]{:S(2)}, u32[]{:S(2)}) collective-permute-start(bf16[16,1792]{1,0:T(8,128)(2,1)S(1)} %get-tuple-element.72), channel_id=1, source_target_pairs={{0,24},{1,25},{2,26},{3,27},{4,28},{5,29},{6,30},{7,31},{8,16},{9,... | collective-permute-start | bytes 172040 | tf_op jit(solution)/shard_map/ppermute | solution.py:54
  95.7 0.1 tokens_plane.1
  95.8 0.8 collective-permute-start.26
  96.7 1.7 %collective-permute-start.27 = (bf16[16,1792]{1,0:T(8,128)(2,1)S(1)}, bf16[16,1792]{1,0:T(8,128)(2,1)S(1)}, u32[]{:S(2)}, u32[]{:S(2)}) collective-permute-start(bf16[16,1792]{1,0:T(8,128)(2,1)S(1)} %get-tuple-element.83), channel_id=1, source_target_pairs={{0,16},{1,17},{2,18},{3,19},{4,20},{5,21},{6,22},{7,23},{8,24},{9,... | collective-permute-start | bytes 172040 | tf_op jit(solution)/shard_map/ppermute | solution.py:54
  98.3 0.0 collective-permute-done.19.refs_1_
  98.3 2.0 %collective-permute-start.28 = (bf16[16,1792]{1,0:T(8,128)(2,1)S(1)}, bf16[16,1792]{1,0:T(8,128)(2,1)S(1)}, u32[]{:S(2)}, u32[]{:S(2)}) collective-permute-start(bf16[16,1792]{1,0:T(8,128)(2,1)S(1)} %get-tuple-element.84), channel_id=1, source_target_pairs={{0,24},{1,25},{2,26},{3,27},{4,28},{5,29},{6,30},{7,31},{8,16},{9,... | collective-permute-start | bytes 172040 | tf_op jit(solution)/shard_map/ppermute | solution.py:54
  100.3 7.2 %grad_up.1 = (bf16[2,608,7168]{2,1,0:T(8,128)(2,1)}, f32[8,128]{1,0:T(8,128)S(1)}) custom-call(bf16[2,32,608]{2,1,0:T(8,128)(2,1)S(1)} %get-tuple-element.65.du_ref.refs_0_, bf16[4,64,1792]{2,1,0:T(8,128)(2,1)S(1)} %get-tuple-element.78.refs_2_.refs_1_, bf16[16,1792]{1,0:T(8,128)(2,1)S(1)} %get-tuple-element.81.refs_2_.refs_4_), custom_call_target="tpu_custom_call" | custom-call | flops 46000001024 | tf_op jit(solution)/shard_map/grad_up/pallas_call | solution.py:78
  107.5 0.0 collective-permute-done.20.refs_2_
  107.5 0.0 collective-permute-done.21.refs_3_
  107.5 0.0 collective-permute-done.28.refs_7_
  107.5 0.7 finish.1
  (13 shorter events, 0.1 us)
Async XLA Ops:
  1.6 7.6 %collective-permute-start.2 = (bf16[16,1920]{1,0:T(8,128)(2,1)S(1)}, bf16[16,1920]{1,0:T(8,128)(2,1)S(1)}, u32[]{:S(2)}, u32[]{:S(2)}) collective-permute-start(bf16[16,1920]{1,0:T(8,128)(2,1)S(1)} %get-tuple-element.48.refs_0_), channel_id=1, source_target_pairs={{0,24},{1,25},{2,26},{3,27},{4,28},{5,29},{6,30},{7,31},{8,16},{9,... | collective-permute-start | bytes 184328 | tf_op jit(solution)/shard_map/ppermute | solution.py:54
  6.8 5.3 %collective-permute-start.1 = (bf16[16,1920]{1,0:T(8,128)(2,1)S(1)}, bf16[16,1920]{1,0:T(8,128)(2,1)S(1)}, u32[]{:S(2)}, u32[]{:S(2)}) collective-permute-start(bf16[16,1920]{1,0:T(8,128)(2,1)S(1)} %get-tuple-element.48.refs_0_), channel_id=1, source_target_pairs={{0,16},{1,17},{2,18},{3,19},{4,20},{5,21},{6,22},{7,23},{8,24},{9,... | collective-permute-start | bytes 184328 | tf_op jit(solution)/shard_map/ppermute | solution.py:54
  6.8 5.3 %collective-permute-start = (bf16[16,1920]{1,0:T(8,128)(2,1)S(1)}, bf16[16,1920]{1,0:T(8,128)(2,1)S(1)}, u32[]{:S(2)}, u32[]{:S(2)}) collective-permute-start(bf16[16,1920]{1,0:T(8,128)(2,1)S(1)} %get-tuple-element.48.refs_0_), channel_id=1, source_target_pairs={{0,8},{1,9},{2,10},{3,11},{4,12},{5,13},{6,14},{7,15},{8,0},{9,1},... | collective-permute-start | bytes 184328 | tf_op jit(solution)/shard_map/ppermute | solution.py:54
  12.1 4.7 %collective-permute-start.6 = (bf16[16,1792]{1,0:T(8,128)(2,1)S(1)}, bf16[16,1792]{1,0:T(8,128)(2,1)S(1)}, u32[]{:S(2)}, u32[]{:S(2)}) collective-permute-start(bf16[16,1792]{1,0:T(8,128)(2,1)S(1)} %get-tuple-element.51.refs_0_), channel_id=1, source_target_pairs={{0,8},{1,9},{2,10},{3,11},{4,12},{5,13},{6,14},{7,15},{8,0},{9,1},... | collective-permute-start | bytes 172040 | tf_op jit(solution)/shard_map/ppermute | solution.py:54
  13.3 10.5 %collective-permute-start.5 = (bf16[64,1920]{1,0:T(8,128)(2,1)S(1)}, bf16[64,1920]{1,0:T(8,128)(2,1)S(1)}, u32[]{:S(2)}, u32[]{:S(2)}) collective-permute-start(bf16[64,1920]{1,0:T(8,128)(2,1)S(1)} %get-tuple-element.50.refs_0_), channel_id=1, source_target_pairs={{0,6},{1,7},{2,4},{3,5},{4,2},{5,3},{6,0},{7,1},{8,14},{9,15},{10,... | collective-permute-start | bytes 737288 | tf_op jit(solution)/shard_map/ppermute | solution.py:54
  15.7 10.2 %collective-permute-start.4 = (bf16[64,1920]{1,0:T(8,128)(2,1)S(1)}, bf16[64,1920]{1,0:T(8,128)(2,1)S(1)}, u32[]{:S(2)}, u32[]{:S(2)}) collective-permute-start(bf16[64,1920]{1,0:T(8,128)(2,1)S(1)} %get-tuple-element.50.refs_0_), channel_id=1, source_target_pairs={{0,4},{1,5},{2,6},{3,7},{4,0},{5,1},{6,2},{7,3},{8,12},{9,13},{10,... | collective-permute-start | bytes 737288 | tf_op jit(solution)/shard_map/ppermute | solution.py:54
  16.2 9.7 %collective-permute-start.3 = (bf16[64,1920]{1,0:T(8,128)(2,1)S(1)}, bf16[64,1920]{1,0:T(8,128)(2,1)S(1)}, u32[]{:S(2)}, u32[]{:S(2)}) collective-permute-start(bf16[64,1920]{1,0:T(8,128)(2,1)S(1)} %get-tuple-element.50.refs_0_), channel_id=1, source_target_pairs={{0,2},{1,3},{2,0},{3,1},{4,6},{5,7},{6,4},{7,5},{8,10},{9,11},{10,... | collective-permute-start | bytes 737288 | tf_op jit(solution)/shard_map/ppermute | solution.py:54
  16.8 7.0 %collective-permute-start.7 = (bf16[32,1792]{1,0:T(8,128)(2,1)S(1)}, bf16[32,1792]{1,0:T(8,128)(2,1)S(1)}, u32[]{:S(2)}, u32[]{:S(2)}) collective-permute-start(bf16[32,1792]{1,0:T(8,128)(2,1)S(1)} %double.2._.refs_0_), channel_id=1, source_target_pairs={{0,16},{1,17},{2,18},{3,19},{4,20},{5,21},{6,22},{7,23},{8,24},{9,... | collective-permute-start | bytes 344072 | tf_op jit(solution)/shard_map/ppermute | solution.py:54
  26.0 4.2 %collective-permute-start.9 = (bf16[192,1920]{1,0:T(8,128)(2,1)S(1)}, bf16[192,1920]{1,0:T(8,128)(2,1)S(1)}, u32[]{:S(2)}, u32[]{:S(2)}) collective-permute-start(bf16[192,1920]{1,0:T(8,128)(2,1)S(1)} %stack_tokens_plane.1.refs_1_), channel_id=1, source_target_pairs={{0,1},{1,0},{2,3},{3,2},{4,5},{5,4},{6,7},{7,6},{8,9},{9,8},{10,11... | collective-permute-start | bytes 2211848 | tf_op jit(solution)/shard_map/ppermute | solution.py:54
  26.1 3.5 %collective-permute-start.8 = (bf16[64,1920]{1,0:T(8,128)(2,1)S(1)}, bf16[64,1920]{1,0:T(8,128)(2,1)S(1)}, u32[]{:S(2)}, u32[]{:S(2)}) collective-permute-start(bf16[64,1920]{1,0:T(8,128)(2,1)S(1)} %get-tuple-element.50.refs_0_), channel_id=1, source_target_pairs={{0,1},{1,0},{2,3},{3,2},{4,5},{5,4},{6,7},{7,6},{8,9},{9,8},{10,11... | collective-permute-start | bytes 737288 | tf_op jit(solution)/shard_map/ppermute | solution.py:54
  26.6 24.3 %collective-permute-start.14 = (bf16[64,1792]{1,0:T(8,128)(2,1)S(1)}, bf16[64,1792]{1,0:T(8,128)(2,1)S(1)}, u32[]{:S(2)}, u32[]{:S(2)}) collective-permute-start(bf16[64,1792]{1,0:T(8,128)(2,1)S(1)} %stack_cotangents.1.refs_6_.refs_0_), channel_id=1, source_target_pairs={{0,1},{1,0},{2,3},{3,2},{4,5},{5,4},{6,7},{7,6},{8,9},{9,8},{10,11... | collective-permute-start | bytes 688136 | tf_op jit(solution)/shard_map/ppermute | solution.py:54
  26.7 18.0 %collective-permute-start.12 = (bf16[64,1792]{1,0:T(8,128)(2,1)S(1)}, bf16[64,1792]{1,0:T(8,128)(2,1)S(1)}, u32[]{:S(2)}, u32[]{:S(2)}) collective-permute-start(bf16[64,1792]{1,0:T(8,128)(2,1)S(1)} %stack_cotangents.1.refs_6_.refs_0_), channel_id=1, source_target_pairs={{0,6},{1,7},{2,4},{3,5},{4,2},{5,3},{6,0},{7,1},{8,14},{9,15},{10,... | collective-permute-start | bytes 688136 | tf_op jit(solution)/shard_map/ppermute | solution.py:54
  29.1 15.7 %collective-permute-start.11 = (bf16[64,1792]{1,0:T(8,128)(2,1)S(1)}, bf16[64,1792]{1,0:T(8,128)(2,1)S(1)}, u32[]{:S(2)}, u32[]{:S(2)}) collective-permute-start(bf16[64,1792]{1,0:T(8,128)(2,1)S(1)} %stack_cotangents.1.refs_6_.refs_0_), channel_id=1, source_target_pairs={{0,4},{1,5},{2,6},{3,7},{4,0},{5,1},{6,2},{7,3},{8,12},{9,13},{10,... | collective-permute-start | bytes 688136 | tf_op jit(solution)/shard_map/ppermute | solution.py:54
  29.6 15.2 %collective-permute-start.10 = (bf16[64,1792]{1,0:T(8,128)(2,1)S(1)}, bf16[64,1792]{1,0:T(8,128)(2,1)S(1)}, u32[]{:S(2)}, u32[]{:S(2)}) collective-permute-start(bf16[64,1792]{1,0:T(8,128)(2,1)S(1)} %stack_cotangents.1.refs_6_.refs_0_), channel_id=1, source_target_pairs={{0,2},{1,3},{2,0},{3,1},{4,6},{5,7},{6,4},{7,5},{8,10},{9,11},{10,... | collective-permute-start | bytes 688136 | tf_op jit(solution)/shard_map/ppermute | solution.py:54
  44.8 6.0 %collective-permute-start.15 = (bf16[192,1792]{1,0:T(8,128)(2,1)S(1)}, bf16[192,1792]{1,0:T(8,128)(2,1)S(1)}, u32[]{:S(2)}, u32[]{:S(2)}) collective-permute-start(bf16[192,1792]{1,0:T(8,128)(2,1)S(1)} %stack_cotangents_plane.1._.refs_1_), channel_id=1, source_target_pairs={{0,1},{1,0},{2,3},{3,2},{4,5},{5,4},{6,7},{7,6},{8,9},{9,8},{10,11... | collective-permute-start | bytes 2064392 | tf_op jit(solution)/shard_map/ppermute | solution.py:54
  50.3 8.6 %collective-permute-start.13 = (bf16[2,2,64,1792]{3,2,1,0:T(8,128)(2,1)S(1)}, bf16[2,2,64,1792]{3,2,1,0:T(8,128)(2,1)S(1)}, u32[]{:S(2)}, u32[]{:S(2)}) collective-permute-start(bf16[2,2,64,1792]{3,2,1,0:T(8,128)(2,1)S(1)} %get-tuple-element.56), channel_id=1, source_target_pairs={{0,1},{1,0},{2,3},{3,2},{4,5},{5,4},{6,7},{7,6},{8,9},{9,8},{10,11... | collective-permute-start | bytes 2752520 | tf_op jit(solution)/shard_map/ppermute | solution.py:54
  59.1 13.7 %collective-permute-start.16 = (bf16[64,1792]{1,0:T(8,128)(2,1)S(1)}, bf16[64,1792]{1,0:T(8,128)(2,1)S(1)}, u32[]{:S(2)}, u32[]{:S(2)}) collective-permute-start(bf16[64,1792]{1,0:T(8,128)(2,1)S(1)} %get-tuple-element.62), channel_id=1, source_target_pairs={{0,2},{1,3},{2,0},{3,1},{4,6},{5,7},{6,4},{7,5},{8,10},{9,11},{10,... | collective-permute-start | bytes 688136 | tf_op jit(solution)/shard_map/ppermute | solution.py:54
  60.6 12.3 %collective-permute-start.17 = (bf16[64,1792]{1,0:T(8,128)(2,1)S(1)}, bf16[64,1792]{1,0:T(8,128)(2,1)S(1)}, u32[]{:S(2)}, u32[]{:S(2)}) collective-permute-start(bf16[64,1792]{1,0:T(8,128)(2,1)S(1)} %get-tuple-element.63), channel_id=1, source_target_pairs={{0,4},{1,5},{2,6},{3,7},{4,0},{5,1},{6,2},{7,3},{8,12},{9,13},{10,... | collective-permute-start | bytes 688136 | tf_op jit(solution)/shard_map/ppermute | solution.py:54
  62.1 10.8 %collective-permute-start.18 = (bf16[64,1792]{1,0:T(8,128)(2,1)S(1)}, bf16[64,1792]{1,0:T(8,128)(2,1)S(1)}, u32[]{:S(2)}, u32[]{:S(2)}) collective-permute-start(bf16[64,1792]{1,0:T(8,128)(2,1)S(1)} %get-tuple-element.64), channel_id=1, source_target_pairs={{0,6},{1,7},{2,4},{3,5},{4,2},{5,3},{6,0},{7,1},{8,14},{9,15},{10,... | collective-permute-start | bytes 688136 | tf_op jit(solution)/shard_map/ppermute | solution.py:54
  73.0 2.6 %collective-permute-start.22 = (bf16[2,2,64,1792]{3,2,1,0:T(8,128)(2,1)S(1)}, bf16[2,2,64,1792]{3,2,1,0:T(8,128)(2,1)S(1)}, u32[]{:S(2)}, u32[]{:S(2)}) collective-permute-start(bf16[2,2,64,1792]{3,2,1,0:T(8,128)(2,1)S(1)} %get-tuple-element.73), channel_id=1, source_target_pairs={{0,1},{1,0},{2,3},{3,2},{4,5},{5,4},{6,7},{7,6},{8,9},{9,8},{10,11... | collective-permute-start | bytes 2752520 | tf_op jit(solution)/shard_map/ppermute | solution.py:54
  73.1 25.3 %collective-permute-start.19 = (bf16[16,1792]{1,0:T(8,128)(2,1)S(1)}, bf16[16,1792]{1,0:T(8,128)(2,1)S(1)}, u32[]{:S(2)}, u32[]{:S(2)}) collective-permute-start(bf16[16,1792]{1,0:T(8,128)(2,1)S(1)} %get-tuple-element.70), channel_id=1, source_target_pairs={{0,8},{1,9},{2,10},{3,11},{4,12},{5,13},{6,14},{7,15},{8,0},{9,1},... | collective-permute-start | bytes 172040 | tf_op jit(solution)/shard_map/ppermute | solution.py:54
  74.8 32.7 %collective-permute-start.20 = (bf16[16,1792]{1,0:T(8,128)(2,1)S(1)}, bf16[16,1792]{1,0:T(8,128)(2,1)S(1)}, u32[]{:S(2)}, u32[]{:S(2)}) collective-permute-start(bf16[16,1792]{1,0:T(8,128)(2,1)S(1)} %get-tuple-element.71), channel_id=1, source_target_pairs={{0,16},{1,17},{2,18},{3,19},{4,20},{5,21},{6,22},{7,23},{8,24},{9,... | collective-permute-start | bytes 172040 | tf_op jit(solution)/shard_map/ppermute | solution.py:54
  75.8 17.9 %collective-permute-start.23 = (bf16[64,1792]{1,0:T(8,128)(2,1)S(1)}, bf16[64,1792]{1,0:T(8,128)(2,1)S(1)}, u32[]{:S(2)}, u32[]{:S(2)}) collective-permute-start(bf16[64,1792]{1,0:T(8,128)(2,1)S(1)} %get-tuple-element.75), channel_id=1, source_target_pairs={{0,2},{1,3},{2,0},{3,1},{4,6},{5,7},{6,4},{7,5},{8,10},{9,11},{10,... | collective-permute-start | bytes 688136 | tf_op jit(solution)/shard_map/ppermute | solution.py:54
  77.3 18.5 %collective-permute-start.24 = (bf16[64,1792]{1,0:T(8,128)(2,1)S(1)}, bf16[64,1792]{1,0:T(8,128)(2,1)S(1)}, u32[]{:S(2)}, u32[]{:S(2)}) collective-permute-start(bf16[64,1792]{1,0:T(8,128)(2,1)S(1)} %get-tuple-element.76), channel_id=1, source_target_pairs={{0,4},{1,5},{2,6},{3,7},{4,0},{5,1},{6,2},{7,3},{8,12},{9,13},{10,... | collective-permute-start | bytes 688136 | tf_op jit(solution)/shard_map/ppermute | solution.py:54
  78.7 17.0 %collective-permute-start.25 = (bf16[64,1792]{1,0:T(8,128)(2,1)S(1)}, bf16[64,1792]{1,0:T(8,128)(2,1)S(1)}, u32[]{:S(2)}, u32[]{:S(2)}) collective-permute-start(bf16[64,1792]{1,0:T(8,128)(2,1)S(1)} %get-tuple-element.77), channel_id=1, source_target_pairs={{0,6},{1,7},{2,4},{3,5},{4,2},{5,3},{6,0},{7,1},{8,14},{9,15},{10,... | collective-permute-start | bytes 688136 | tf_op jit(solution)/shard_map/ppermute | solution.py:54
  93.7 13.8 %collective-permute-start.21 = (bf16[16,1792]{1,0:T(8,128)(2,1)S(1)}, bf16[16,1792]{1,0:T(8,128)(2,1)S(1)}, u32[]{:S(2)}, u32[]{:S(2)}) collective-permute-start(bf16[16,1792]{1,0:T(8,128)(2,1)S(1)} %get-tuple-element.72), channel_id=1, source_target_pairs={{0,24},{1,25},{2,26},{3,27},{4,28},{5,29},{6,30},{7,31},{8,16},{9,... | collective-permute-start | bytes 172040 | tf_op jit(solution)/shard_map/ppermute | solution.py:54
  95.8 11.7 %collective-permute-start.26 = (bf16[16,1792]{1,0:T(8,128)(2,1)S(1)}, bf16[16,1792]{1,0:T(8,128)(2,1)S(1)}, u32[]{:S(2)}, u32[]{:S(2)}) collective-permute-start(bf16[16,1792]{1,0:T(8,128)(2,1)S(1)} %get-tuple-element.82), channel_id=1, source_target_pairs={{0,8},{1,9},{2,10},{3,11},{4,12},{5,13},{6,14},{7,15},{8,0},{9,1},... | collective-permute-start | bytes 172040 | tf_op jit(solution)/shard_map/ppermute | solution.py:54
  96.7 10.8 %collective-permute-start.27 = (bf16[16,1792]{1,0:T(8,128)(2,1)S(1)}, bf16[16,1792]{1,0:T(8,128)(2,1)S(1)}, u32[]{:S(2)}, u32[]{:S(2)}) collective-permute-start(bf16[16,1792]{1,0:T(8,128)(2,1)S(1)} %get-tuple-element.83), channel_id=1, source_target_pairs={{0,16},{1,17},{2,18},{3,19},{4,20},{5,21},{6,22},{7,23},{8,24},{9,... | collective-permute-start | bytes 172040 | tf_op jit(solution)/shard_map/ppermute | solution.py:54
  98.3 9.2 %collective-permute-start.28 = (bf16[16,1792]{1,0:T(8,128)(2,1)S(1)}, bf16[16,1792]{1,0:T(8,128)(2,1)S(1)}, u32[]{:S(2)}, u32[]{:S(2)}) collective-permute-start(bf16[16,1792]{1,0:T(8,128)(2,1)S(1)} %get-tuple-element.84), channel_id=1, source_target_pairs={{0,24},{1,25},{2,26},{3,27},{4,28},{5,29},{6,30},{7,31},{8,16},{9,... | collective-permute-start | bytes 172040 | tf_op jit(solution)/shard_map/ppermute | solution.py:54

commit v2 on v1

--- a/solution.py
+++ b/solution.py
@@ -279,6 +279,27 @@
         copy.wait()
 
 
+def hold_gate_kernel(s, weight, _, held, sems):
+    copies = [held_copy(s, weight, held, sems, k, p) for k in range(s.early) for p in range(len(s.pieces))]
+    for copy in copies:
+        copy.start()
+    for copy in copies:
+        copy.wait()
+
+
+def hold_gate(s, weight, after):
+    (held,) = call(
+        functools.partial(hold_gate_kernel, s),
+        "hold_gate",
+        [pltpu.VMEM(weight.shape, BF16)],
+        [hbm(weight), after],
+        specs=[ANYWHERE] * 2,
+        scratch=[pltpu.SemaphoreType.DMA((s.early * len(s.pieces),))],
+        cost=12000,
+    )
+    return held
+
+
 def hold(s, weight, after):
     (held,) = call(
         functools.partial(hold_kernel, s),
@@ -323,10 +344,10 @@
 
 def gate_up_kernel(s, *refs):
     blocks, refs = refs[: 2 * s.grid.nc], refs[2 * s.grid.nc :]
-    wg_ref, wu_ref, _, x_ref, select_ref, back_ref, gate_ref, act_ref, p_ref, q_ref, held_ref = refs[:11]
-    room, sems, held_sems, g_acc, u_acc = refs[11:]
+    _, wg_ref, wu_ref, _, x_ref, select_ref, back_ref, gate_ref, act_ref, p_ref, q_ref, held_ref = refs[:12]
+    room, sems, held_sems, g_acc, u_acc = refs[12:]
     ups = Stream(s, wu_ref, room, sems, lambda k: k)
-    for k in range(min(2, s.slices)):
+    for k in range(s.early, min(2, s.slices)):
         for p in range(len(s.pieces)):
             held_copy(s, wg_ref, held_ref, held_sems, k, p).start()
     aux = jnp.concatenate([s.block_of(blocks, 0, a, 0)[:, s.width :] for a in range(s.grid.nx)], axis=0)
@@ -342,11 +363,14 @@
     def step(k, _):
         for p, (at, size) in enumerate(s.pieces):
 
-            @pl.when(k + 2 < s.slices)
+            @pl.when((k + 2 >= s.early) & (k + 2 < s.slices))
             def _():
                 held_copy(s, wg_ref, held_ref, held_sems, k + 2, p).start()
 
-            held_copy(s, wg_ref, held_ref, held_sems, k, p).wait()
+            @pl.when(k >= s.early)
+            def _():
+                held_copy(s, wg_ref, held_ref, held_sems, k, p).wait()
+
             up = ups.get(k, p)
             gate = held_ref.at[:, :, pl.ds(pl.multiple_of(k * s.width + at, LANES), size)]
             for e in range(s.local):
@@ -428,8 +452,9 @@
     def step(k, _):
         for p, (at, size) in enumerate(s.pieces):
             gate = held_ref.at[:, :, pl.ds(pl.multiple_of(s.grid.source(k) * s.width + at, LANES), size)]
+            found = [dot(dg_ref[e], gate[e]) for e in range(s.local)]
             up = weights.get(k, p)
-            found = [(dot(dg_ref[e], gate[e]) + dot(du_ref[e], up[e])).astype(BF16) for e in range(s.local)]
+            found = [(found[e] + dot(du_ref[e], up[e])).astype(BF16) for e in range(s.local)]
             to_tokens(s, k, at, found, back_ref, outs)
             weights.free(k, p)
         return 0
@@ -515,7 +540,8 @@
     x_column, cotangent = stack(x_parts, [], "stack_tokens", [cotangent])
     x_plane = grid.over_plane(x_column)
     d_column, held_down = doubled_along_z(grid, cotangent, lambda after: hold(s, w_down, after))
-    x_others = stack([x_plane[at] for at in grid.square[1:]], [d_column], "stack_tokens_plane")
+    held_gate = hold_gate(s, w_gate, d_column)
+    x_others = stack([x_plane[at] for at in grid.square[1:]], [d_column, held_gate], "stack_tokens_plane")
     x_blocks = grid.over_cores(x_column, x_others)
     d_column = stack([d_column], [x_others], "stack_cotangents")
     d_plane = grid.over_plane(d_column)
@@ -539,8 +565,9 @@
             shaped(F32, *hidden_shape),
             pltpu.VMEM(w_gate.shape, BF16),
         ],
-        [*x_blocks, hbm(w_gate), hbm(w_up), d_column],
-        specs=[VECTORS] * len(x_blocks) + [ANYWHERE] * 3,
+        [*x_blocks, held_gate, hbm(w_gate), hbm(w_up), d_column],
+        specs=[VECTORS] * (len(x_blocks) + 1) + [ANYWHERE] * 3,
+        aliases={len(x_blocks): 7},
         scratch=[*streams, pltpu.SemaphoreType.DMA((s.slices * len(s.pieces),)), sums_room, sums_room],
         cost=46000,
     )

time: 108 us -> 110 us (1.019)
  Pallas kernels: 65.7 us -> 69.2 us
  waiting for transfers between devices: 8.02 us -> 5.89 us
    pallas_call x19 -> x20, Pallas kernels: 65.7 us -> 69.2 us  [call(): pl.pallas_call(kernel, name=name, grid=grid, out_shape=outs, in_specs=spe...]
    ppermute x29, waiting for transfers between devices: 8.02 us -> 5.89 us  [shift(): return lax.ppermute(value, AXES, pairs)]
  transfers between devices with their start and end apart: 29 -> 29, of which waited for: 4 -> 3; matrix products, arithmetic and copies ran while one was open for 0% -> 0% of each run, Pallas kernels for 59% -> 61%
where the time goes in v2:
time: 110 us
  Pallas kernels  69.2 us (63%)
  starting transfers between devices  33.9 us (31%)
  waiting for transfers between devices  5.89 us (5%)
    pallas_call x20, Pallas kernels, call(): pl.pallas_call(kernel, name=name, grid=grid, out_shape=outs, in_specs=spe...  69.2 us
    ppermute x29, starting transfers between devices, shift(): return lax.ppermute(value, AXES, pairs)  33.9 us
    ppermute x29, waiting for transfers between devices, shift(): return lax.ppermute(value, AXES, pairs)  5.89 us
  transfers between devices with their start and end apart: 29, of which 3 were waited for; matrix products, arithmetic and copies ran while one was open for 0% of the time, Pallas kernels for 61%

profile of v2, /device:TPU:0, one launch (start us, length us, event | category | flops | bytes accessed | tf_op | source)
XLA Modules:
  0.0 109.9 jit_solution(15797305403702609560)
XLA Ops:
  0.6 1.0 pack.1
  1.6 5.1 %collective-permute-start.2 = (bf16[16,1920]{1,0:T(8,128)(2,1)S(1)}, bf16[16,1920]{1,0:T(8,128)(2,1)S(1)}, u32[]{:S(2)}, u32[]{:S(2)}) collective-permute-start(bf16[16,1920]{1,0:T(8,128)(2,1)S(1)} %get-tuple-element.48.refs_0_), channel_id=1, source_target_pairs={{0,24},{1,25},{2,26},{3,27},{4,28},{5,29},{6,30},{7,31},{8,16},{9,... | collective-permute-start | bytes 184328 | tf_op jit(solution)/shard_map/ppermute | solution.py:54
  6.8 0.0 collective-permute-start.1
  6.8 0.6 collective-permute-start
  7.4 1.8 %collective-permute-done.2.refs_3_ = bf16[16,1920]{1,0:T(8,128)(2,1)S(1)} collective-permute-done((bf16[16,1920]{1,0:T(8,128)(2,1)S(1)}, bf16[16,1920]{1,0:T(8,128)(2,1)S(1)}, u32[]{:S(2)}, u32[]{:S(2)}) %collective-permute-start.2) | collective-permute-done | bytes 61472 | tf_op jit(solution)/shard_map/ppermute | solution.py:54
  9.2 2.8 %collective-permute-done.1.refs_2_ = bf16[16,1920]{1,0:T(8,128)(2,1)S(1)} collective-permute-done((bf16[16,1920]{1,0:T(8,128)(2,1)S(1)}, bf16[16,1920]{1,0:T(8,128)(2,1)S(1)}, u32[]{:S(2)}, u32[]{:S(2)}) %collective-permute-start.1) | collective-permute-done | bytes 61472 | tf_op jit(solution)/shard_map/ppermute | solution.py:54
  12.1 0.0 collective-permute-done.refs_1_
  12.1 1.2 %collective-permute-start.6 = (bf16[16,1792]{1,0:T(8,128)(2,1)S(1)}, bf16[16,1792]{1,0:T(8,128)(2,1)S(1)}, u32[]{:S(2)}, u32[]{:S(2)}) collective-permute-start(bf16[16,1792]{1,0:T(8,128)(2,1)S(1)} %get-tuple-element.51.refs_0_), channel_id=1, source_target_pairs={{0,8},{1,9},{2,10},{3,11},{4,12},{5,13},{6,14},{7,15},{8,0},{9,1},... | collective-permute-start | bytes 172040 | tf_op jit(solution)/shard_map/ppermute | solution.py:54
  13.3 2.4 %collective-permute-start.5 = (bf16[64,1920]{1,0:T(8,128)(2,1)S(1)}, bf16[64,1920]{1,0:T(8,128)(2,1)S(1)}, u32[]{:S(2)}, u32[]{:S(2)}) collective-permute-start(bf16[64,1920]{1,0:T(8,128)(2,1)S(1)} %get-tuple-element.50.refs_0_), channel_id=1, source_target_pairs={{0,6},{1,7},{2,4},{3,5},{4,2},{5,3},{6,0},{7,1},{8,14},{9,15},{10,... | collective-permute-start | bytes 737288 | tf_op jit(solution)/shard_map/ppermute | solution.py:54
  15.7 0.5 collective-permute-start.4
  16.2 0.5 collective-permute-start.3
  16.8 0.0 collective-permute-done.6.refs_1_
  16.8 2.2 %collective-permute-start.7 = (bf16[32,1792]{1,0:T(8,128)(2,1)S(1)}, bf16[32,1792]{1,0:T(8,128)(2,1)S(1)}, u32[]{:S(2)}, u32[]{:S(2)}) collective-permute-start(bf16[32,1792]{1,0:T(8,128)(2,1)S(1)} %double.2._.refs_0_), channel_id=1, source_target_pairs={{0,16},{1,17},{2,18},{3,19},{4,20},{5,21},{6,22},{7,23},{8,24},{9,... | collective-permute-start | bytes 344072 | tf_op jit(solution)/shard_map/ppermute | solution.py:54
  19.0 3.6 %hold_down.1.refs_2_.held_ref = bf16[2,608,3584]{2,1,0:T(8,128)(2,1)S(1)} custom-call(bf16[2,608,7168]{2,1,0:T(8,128)(2,1)} %refs_8_.1, bf16[32,1792]{1,0:T(8,128)(2,1)S(1)} %double.2._.refs_0_), custom_call_target="tpu_custom_call" | custom-call | flops 12000000000 | tf_op jit(solution)/shard_map/hold_down/pallas_call | solution.py:78
  22.6 1.2 %collective-permute-done.7.refs_1_ = bf16[32,1792]{1,0:T(8,128)(2,1)S(1)} collective-permute-done((bf16[32,1792]{1,0:T(8,128)(2,1)S(1)}, bf16[32,1792]{1,0:T(8,128)(2,1)S(1)}, u32[]{:S(2)}, u32[]{:S(2)}) %collective-permute-start.7) | collective-permute-done | bytes 114720 | tf_op jit(solution)/shard_map/ppermute | solution.py:54
  23.8 3.6 %hold_gate.1.refs_4_ = bf16[2,608,7168]{2,1,0:T(8,128)(2,1)S(1)} custom-call(bf16[2,608,7168]{2,1,0:T(8,128)(2,1)} %refs_5_.1, bf16[64,1792]{1,0:T(8,128)(2,1)S(1)} %double.3._.refs_3_.refs_0_), custom_call_target="tpu_custom_call" | custom-call | flops 12000000000 | tf_op jit(solution)/shard_map/hold_gate/pallas_call | solution.py:78
  27.4 0.0 collective-permute-done.4.refs_1_
  27.4 0.0 collective-permute-done.3.refs_0_
  27.4 0.1 stack_tokens_plane.1.refs_1_
  27.5 0.1 collective-permute-start.9
  27.6 0.5 collective-permute-start.8
  28.1 0.1 collective-permute-start.14
  28.2 2.4 %collective-permute-start.12 = (bf16[64,1792]{1,0:T(8,128)(2,1)S(1)}, bf16[64,1792]{1,0:T(8,128)(2,1)S(1)}, u32[]{:S(2)}, u32[]{:S(2)}) collective-permute-start(bf16[64,1792]{1,0:T(8,128)(2,1)S(1)} %stack_cotangents.1.refs_7_.refs_0_), channel_id=1, source_target_pairs={{0,6},{1,7},{2,4},{3,5},{4,2},{5,3},{6,0},{7,1},{8,14},{9,15},{10,... | collective-permute-start | bytes 688136 | tf_op jit(solution)/shard_map/ppermute | solution.py:54
  30.7 0.5 collective-permute-start.11
  31.2 0.0 collective-permute-done.8.refs_2_
  31.2 0.5 collective-permute-start.10
  31.7 13.5 %gate_up.1 = (bf16[4,64,1792]{2,1,0:T(8,128)(2,1)S(1)}, bf16[64,128]{1,0:T(8,128)(2,1)S(1)}, bf16[128,64]{1,0:T(8,128)(2,1)S(1)}, f32[64,128]{1,0:T(8,128)S(1)},...) custom-call(bf16[64,1920]{1,0:T(8,128)(2,1)S(1)} %get-tuple-element., ...), custom_call_target="tpu_custom_call", output_to_operand_aliasing={{7}: (4, {})} | custom-call | flops 46000001024 | tf_op jit(solution)/shard_map/gate_up/pallas_call | solution.py:78
  45.2 0.0 collective-permute-done.12.refs_2_
  45.2 0.0 collective-permute-done.11.refs_1_
  45.3 0.1 collective-permute-start.15
  45.4 5.4 %forward.1 = (bf16[2,2,64,1792]{3,2,1,0:T(8,128)(2,1)S(1)}, bf16[2,2,64,1792]{3,2,1,0:T(8,128)(2,1)S(1)}) custom-call(bf16[2,32,608]{2,1,0:T(8,128)(2,1)S(1)} %get-tuple-element.52.act_ref.refs_1_, f32[64,128]{1,0:T(8,128)S(1)} %get-tuple-element.53.refs_3_.gate_ref.refs_5_, bf16[128,64]{1,0:T(8,128)(2,1)S(1)} %get-tuple-element.54.back_ref, ...), custom_call_target="tpu_custom_call" | custom-call | flops 46000001024 | tf_op jit(solution)/shard_map/forward/pallas_call | solution.py:78
  50.8 0.5 collective-permute-start.13
  51.3 0.0 collective-permute-done.14.refs_2_
  51.3 0.0 collective-permute-done.15.refs_3_
  51.3 8.0 %hidden_grads.1 = (bf16[4,64,1792]{2,1,0:T(8,128)(2,1)S(1)}, bf16[2,32,608]{2,1,0:T(8,128)(2,1)S(1)}, bf16[2,32,608]{2,1,0:T(8,128)(2,1)S(1)}) custom-call(bf16[64,1792]{1,0:T(8,128)(2,1)S(1)} %stack_cotangents.1.refs_7_.refs_0_, bf16[192,1792]{1,0:T(8,128)(2,1)S(1)} %stack_cotangents_plane.1._.refs_1_, ...), custom_call_target="tpu_custom_call" | custom-call | flops 46000001024 | tf_op jit(solution)/shard_map/hidden_grads/pallas_call | solution.py:78
  59.4 0.0 collective-permute-done.13.refs_1_
  59.4 0.2 mixed_cores.1
  59.6 1.6 %collective-permute-start.16 = (bf16[64,1792]{1,0:T(8,128)(2,1)S(1)}, bf16[64,1792]{1,0:T(8,128)(2,1)S(1)}, u32[]{:S(2)}, u32[]{:S(2)}) collective-permute-start(bf16[64,1792]{1,0:T(8,128)(2,1)S(1)} %get-tuple-element.62), channel_id=1, source_target_pairs={{0,2},{1,3},{2,0},{3,1},{4,6},{5,7},{6,4},{7,5},{8,10},{9,11},{10,... | collective-permute-start | bytes 688136 | tf_op jit(solution)/shard_map/ppermute | solution.py:54
  61.2 1.5 %collective-permute-start.17 = (bf16[64,1792]{1,0:T(8,128)(2,1)S(1)}, bf16[64,1792]{1,0:T(8,128)(2,1)S(1)}, u32[]{:S(2)}, u32[]{:S(2)}) collective-permute-start(bf16[64,1792]{1,0:T(8,128)(2,1)S(1)} %get-tuple-element.63), channel_id=1, source_target_pairs={{0,4},{1,5},{2,6},{3,7},{4,0},{5,1},{6,2},{7,3},{8,12},{9,13},{10,... | collective-permute-start | bytes 688136 | tf_op jit(solution)/shard_map/ppermute | solution.py:54
  62.6 0.5 collective-permute-start.18
  63.1 11.1 %backward.1 = (bf16[2,2,64,1792]{3,2,1,0:T(8,128)(2,1)S(1)}, bf16[2,2,64,1792]{3,2,1,0:T(8,128)(2,1)S(1)}) custom-call(bf16[2,32,608]{2,1,0:T(8,128)(2,1)S(1)} %get-tuple-element.60.refs_2_.dg_ref.refs_0_, bf16[2,32,608]{2,1,0:T(8,128)(2,1)S(1)} %get-tuple-element.65.du_ref.refs_0_, bf16[128,64]{1,0:T(8,128)(2,1)S(1)} %get-tuple-element.54.back_ref, ...), custom_call_target="tpu_custom_call" | custom-call | flops 46000001024 | tf_op jit(solution)/shard_map/backward/pallas_call | solution.py:78
  74.2 0.0 collective-permute-done.16.refs_1_
  74.2 0.1 mixed_plane.1
  74.4 0.1 collective-permute-start.22
  74.5 0.2 collective-permute-start.19
  74.7 2.7 %collective-permute-start.20 = (bf16[16,1792]{1,0:T(8,128)(2,1)S(1)}, bf16[16,1792]{1,0:T(8,128)(2,1)S(1)}, u32[]{:S(2)}, u32[]{:S(2)}) collective-permute-start(bf16[16,1792]{1,0:T(8,128)(2,1)S(1)} %get-tuple-element.71), channel_id=1, source_target_pairs={{0,16},{1,17},{2,18},{3,19},{4,20},{5,21},{6,22},{7,23},{8,24},{9,... | collective-permute-start | bytes 172040 | tf_op jit(solution)/shard_map/ppermute | solution.py:54
  77.4 0.2 tokens_cores.1
  77.6 1.6 %collective-permute-start.23 = (bf16[64,1792]{1,0:T(8,128)(2,1)S(1)}, bf16[64,1792]{1,0:T(8,128)(2,1)S(1)}, u32[]{:S(2)}, u32[]{:S(2)}) collective-permute-start(bf16[64,1792]{1,0:T(8,128)(2,1)S(1)} %get-tuple-element.75), channel_id=1, source_target_pairs={{0,2},{1,3},{2,0},{3,1},{4,6},{5,7},{6,4},{7,5},{8,10},{9,11},{10,... | collective-permute-start | bytes 688136 | tf_op jit(solution)/shard_map/ppermute | solution.py:54
  79.2 1.5 %collective-permute-start.24 = (bf16[64,1792]{1,0:T(8,128)(2,1)S(1)}, bf16[64,1792]{1,0:T(8,128)(2,1)S(1)}, u32[]{:S(2)}, u32[]{:S(2)}) collective-permute-start(bf16[64,1792]{1,0:T(8,128)(2,1)S(1)} %get-tuple-element.76), channel_id=1, source_target_pairs={{0,4},{1,5},{2,6},{3,7},{4,0},{5,1},{6,2},{7,3},{8,12},{9,13},{10,... | collective-permute-start | bytes 688136 | tf_op jit(solution)/shard_map/ppermute | solution.py:54
  80.7 0.5 collective-permute-start.25
  81.1 14.3 %grad_gate_down.1 = (bf16[2,608,7168]{2,1,0:T(8,128)(2,1)}, bf16[2,608,7168]{2,1,0:T(8,128)(2,1)}, f32[8,128]{1,0:T(8,128)S(1)}) custom-call(bf16[2,32,608]{2,1,0:T(8,128)(2,1)S(1)} %get-tuple-element.60.refs_2_.dg_ref.refs_0_, bf16[2,32,608]{2,1,0:T(8,128)(2,1)S(1)} %get-tuple-element.52.act_ref.refs_1_, ...), custom_call_target="tpu_custom_call" | custom-call | flops 46000001024 | tf_op jit(solution)/shard_map/grad_gate_down/pallas_call | solution.py:78
  95.5 0.0 collective-permute-done.23.refs_1_
  95.5 1.9 %collective-permute-start.21 = (bf16[16,1792]{1,0:T(8,128)(2,1)S(1)}, bf16[16,1792]{1,0:T(8,128)(2,1)S(1)}, u32[]{:S(2)}, u32[]{:S(2)}) collective-permute-start(bf16[16,1792]{1,0:T(8,128)(2,1)S(1)} %get-tuple-element.72), channel_id=1, source_target_pairs={{0,24},{1,25},{2,26},{3,27},{4,28},{5,29},{6,30},{7,31},{8,16},{9,... | collective-permute-start | bytes 172040 | tf_op jit(solution)/shard_map/ppermute | solution.py:54
  97.4 0.0 collective-permute-done.24.refs_2_
  97.4 0.0 collective-permute-done.25.refs_3_
  97.4 0.1 tokens_plane.1
  97.5 0.1 collective-permute-start.26
  97.6 2.5 %collective-permute-start.27 = (bf16[16,1792]{1,0:T(8,128)(2,1)S(1)}, bf16[16,1792]{1,0:T(8,128)(2,1)S(1)}, u32[]{:S(2)}, u32[]{:S(2)}) collective-permute-start(bf16[16,1792]{1,0:T(8,128)(2,1)S(1)} %get-tuple-element.83), channel_id=1, source_target_pairs={{0,16},{1,17},{2,18},{3,19},{4,20},{5,21},{6,22},{7,23},{8,24},{9,... | collective-permute-start | bytes 172040 | tf_op jit(solution)/shard_map/ppermute | solution.py:54
  100.1 0.0 collective-permute-done.19.refs_1_
  100.1 1.8 %collective-permute-start.28 = (bf16[16,1792]{1,0:T(8,128)(2,1)S(1)}, bf16[16,1792]{1,0:T(8,128)(2,1)S(1)}, u32[]{:S(2)}, u32[]{:S(2)}) collective-permute-start(bf16[16,1792]{1,0:T(8,128)(2,1)S(1)} %get-tuple-element.84), channel_id=1, source_target_pairs={{0,24},{1,25},{2,26},{3,27},{4,28},{5,29},{6,30},{7,31},{8,16},{9,... | collective-permute-start | bytes 172040 | tf_op jit(solution)/shard_map/ppermute | solution.py:54
  102.0 7.2 %grad_up.1 = (bf16[2,608,7168]{2,1,0:T(8,128)(2,1)}, f32[8,128]{1,0:T(8,128)S(1)}) custom-call(bf16[2,32,608]{2,1,0:T(8,128)(2,1)S(1)} %get-tuple-element.65.du_ref.refs_0_, bf16[4,64,1792]{2,1,0:T(8,128)(2,1)S(1)} %get-tuple-element.78.refs_2_.refs_1_, bf16[16,1792]{1,0:T(8,128)(2,1)S(1)} %get-tuple-element.81.refs_2_.refs_4_), custom_call_target="tpu_custom_call" | custom-call | flops 46000001024 | tf_op jit(solution)/shard_map/grad_up/pallas_call | solution.py:78
  109.2 0.0 collective-permute-done.26.refs_5_
  109.2 0.0 collective-permute-done.27.refs_6_
  109.2 0.7 finish.1
  (14 shorter events, 0.1 us)
Async XLA Ops:
  1.6 7.6 %collective-permute-start.2 = (bf16[16,1920]{1,0:T(8,128)(2,1)S(1)}, bf16[16,1920]{1,0:T(8,128)(2,1)S(1)}, u32[]{:S(2)}, u32[]{:S(2)}) collective-permute-start(bf16[16,1920]{1,0:T(8,128)(2,1)S(1)} %get-tuple-element.48.refs_0_), channel_id=1, source_target_pairs={{0,24},{1,25},{2,26},{3,27},{4,28},{5,29},{6,30},{7,31},{8,16},{9,... | collective-permute-start | bytes 184328 | tf_op jit(solution)/shard_map/ppermute | solution.py:54
  6.8 5.3 %collective-permute-start.1 = (bf16[16,1920]{1,0:T(8,128)(2,1)S(1)}, bf16[16,1920]{1,0:T(8,128)(2,1)S(1)}, u32[]{:S(2)}, u32[]{:S(2)}) collective-permute-start(bf16[16,1920]{1,0:T(8,128)(2,1)S(1)} %get-tuple-element.48.refs_0_), channel_id=1, source_target_pairs={{0,16},{1,17},{2,18},{3,19},{4,20},{5,21},{6,22},{7,23},{8,24},{9,... | collective-permute-start | bytes 184328 | tf_op jit(solution)/shard_map/ppermute | solution.py:54
  6.8 5.3 %collective-permute-start = (bf16[16,1920]{1,0:T(8,128)(2,1)S(1)}, bf16[16,1920]{1,0:T(8,128)(2,1)S(1)}, u32[]{:S(2)}, u32[]{:S(2)}) collective-permute-start(bf16[16,1920]{1,0:T(8,128)(2,1)S(1)} %get-tuple-element.48.refs_0_), channel_id=1, source_target_pairs={{0,8},{1,9},{2,10},{3,11},{4,12},{5,13},{6,14},{7,15},{8,0},{9,1},... | collective-permute-start | bytes 184328 | tf_op jit(solution)/shard_map/ppermute | solution.py:54
  12.1 4.7 %collective-permute-start.6 = (bf16[16,1792]{1,0:T(8,128)(2,1)S(1)}, bf16[16,1792]{1,0:T(8,128)(2,1)S(1)}, u32[]{:S(2)}, u32[]{:S(2)}) collective-permute-start(bf16[16,1792]{1,0:T(8,128)(2,1)S(1)} %get-tuple-element.51.refs_0_), channel_id=1, source_target_pairs={{0,8},{1,9},{2,10},{3,11},{4,12},{5,13},{6,14},{7,15},{8,0},{9,1},... | collective-permute-start | bytes 172040 | tf_op jit(solution)/shard_map/ppermute | solution.py:54
  13.3 14.1 %collective-permute-start.5 = (bf16[64,1920]{1,0:T(8,128)(2,1)S(1)}, bf16[64,1920]{1,0:T(8,128)(2,1)S(1)}, u32[]{:S(2)}, u32[]{:S(2)}) collective-permute-start(bf16[64,1920]{1,0:T(8,128)(2,1)S(1)} %get-tuple-element.50.refs_0_), channel_id=1, source_target_pairs={{0,6},{1,7},{2,4},{3,5},{4,2},{5,3},{6,0},{7,1},{8,14},{9,15},{10,... | collective-permute-start | bytes 737288 | tf_op jit(solution)/shard_map/ppermute | solution.py:54
  15.7 11.7 %collective-permute-start.4 = (bf16[64,1920]{1,0:T(8,128)(2,1)S(1)}, bf16[64,1920]{1,0:T(8,128)(2,1)S(1)}, u32[]{:S(2)}, u32[]{:S(2)}) collective-permute-start(bf16[64,1920]{1,0:T(8,128)(2,1)S(1)} %get-tuple-element.50.refs_0_), channel_id=1, source_target_pairs={{0,4},{1,5},{2,6},{3,7},{4,0},{5,1},{6,2},{7,3},{8,12},{9,13},{10,... | collective-permute-start | bytes 737288 | tf_op jit(solution)/shard_map/ppermute | solution.py:54
  16.2 11.2 %collective-permute-start.3 = (bf16[64,1920]{1,0:T(8,128)(2,1)S(1)}, bf16[64,1920]{1,0:T(8,128)(2,1)S(1)}, u32[]{:S(2)}, u32[]{:S(2)}) collective-permute-start(bf16[64,1920]{1,0:T(8,128)(2,1)S(1)} %get-tuple-element.50.refs_0_), channel_id=1, source_target_pairs={{0,2},{1,3},{2,0},{3,1},{4,6},{5,7},{6,4},{7,5},{8,10},{9,11},{10,... | collective-permute-start | bytes 737288 | tf_op jit(solution)/shard_map/ppermute | solution.py:54
  16.8 7.0 %collective-permute-start.7 = (bf16[32,1792]{1,0:T(8,128)(2,1)S(1)}, bf16[32,1792]{1,0:T(8,128)(2,1)S(1)}, u32[]{:S(2)}, u32[]{:S(2)}) collective-permute-start(bf16[32,1792]{1,0:T(8,128)(2,1)S(1)} %double.2._.refs_0_), channel_id=1, source_target_pairs={{0,16},{1,17},{2,18},{3,19},{4,20},{5,21},{6,22},{7,23},{8,24},{9,... | collective-permute-start | bytes 344072 | tf_op jit(solution)/shard_map/ppermute | solution.py:54
  27.5 4.2 %collective-permute-start.9 = (bf16[192,1920]{1,0:T(8,128)(2,1)S(1)}, bf16[192,1920]{1,0:T(8,128)(2,1)S(1)}, u32[]{:S(2)}, u32[]{:S(2)}) collective-permute-start(bf16[192,1920]{1,0:T(8,128)(2,1)S(1)} %stack_tokens_plane.1.refs_1_), channel_id=1, source_target_pairs={{0,1},{1,0},{2,3},{3,2},{4,5},{5,4},{6,7},{7,6},{8,9},{9,8},{10,11... | collective-permute-start | bytes 2211848 | tf_op jit(solution)/shard_map/ppermute | solution.py:54
  27.6 3.6 %collective-permute-start.8 = (bf16[64,1920]{1,0:T(8,128)(2,1)S(1)}, bf16[64,1920]{1,0:T(8,128)(2,1)S(1)}, u32[]{:S(2)}, u32[]{:S(2)}) collective-permute-start(bf16[64,1920]{1,0:T(8,128)(2,1)S(1)} %get-tuple-element.50.refs_0_), channel_id=1, source_target_pairs={{0,1},{1,0},{2,3},{3,2},{4,5},{5,4},{6,7},{7,6},{8,9},{9,8},{10,11... | collective-permute-start | bytes 737288 | tf_op jit(solution)/shard_map/ppermute | solution.py:54
  28.1 23.3 %collective-permute-start.14 = (bf16[64,1792]{1,0:T(8,128)(2,1)S(1)}, bf16[64,1792]{1,0:T(8,128)(2,1)S(1)}, u32[]{:S(2)}, u32[]{:S(2)}) collective-permute-start(bf16[64,1792]{1,0:T(8,128)(2,1)S(1)} %stack_cotangents.1.refs_7_.refs_0_), channel_id=1, source_target_pairs={{0,1},{1,0},{2,3},{3,2},{4,5},{5,4},{6,7},{7,6},{8,9},{9,8},{10,11... | collective-permute-start | bytes 688136 | tf_op jit(solution)/shard_map/ppermute | solution.py:54
  28.2 17.0 %collective-permute-start.12 = (bf16[64,1792]{1,0:T(8,128)(2,1)S(1)}, bf16[64,1792]{1,0:T(8,128)(2,1)S(1)}, u32[]{:S(2)}, u32[]{:S(2)}) collective-permute-start(bf16[64,1792]{1,0:T(8,128)(2,1)S(1)} %stack_cotangents.1.refs_7_.refs_0_), channel_id=1, source_target_pairs={{0,6},{1,7},{2,4},{3,5},{4,2},{5,3},{6,0},{7,1},{8,14},{9,15},{10,... | collective-permute-start | bytes 688136 | tf_op jit(solution)/shard_map/ppermute | solution.py:54
  30.7 14.6 %collective-permute-start.11 = (bf16[64,1792]{1,0:T(8,128)(2,1)S(1)}, bf16[64,1792]{1,0:T(8,128)(2,1)S(1)}, u32[]{:S(2)}, u32[]{:S(2)}) collective-permute-start(bf16[64,1792]{1,0:T(8,128)(2,1)S(1)} %stack_cotangents.1.refs_7_.refs_0_), channel_id=1, source_target_pairs={{0,4},{1,5},{2,6},{3,7},{4,0},{5,1},{6,2},{7,3},{8,12},{9,13},{10,... | collective-permute-start | bytes 688136 | tf_op jit(solution)/shard_map/ppermute | solution.py:54
  31.2 14.0 %collective-permute-start.10 = (bf16[64,1792]{1,0:T(8,128)(2,1)S(1)}, bf16[64,1792]{1,0:T(8,128)(2,1)S(1)}, u32[]{:S(2)}, u32[]{:S(2)}) collective-permute-start(bf16[64,1792]{1,0:T(8,128)(2,1)S(1)} %stack_cotangents.1.refs_7_.refs_0_), channel_id=1, source_target_pairs={{0,2},{1,3},{2,0},{3,1},{4,6},{5,7},{6,4},{7,5},{8,10},{9,11},{10,... | collective-permute-start | bytes 688136 | tf_op jit(solution)/shard_map/ppermute | solution.py:54
  45.3 6.0 %collective-permute-start.15 = (bf16[192,1792]{1,0:T(8,128)(2,1)S(1)}, bf16[192,1792]{1,0:T(8,128)(2,1)S(1)}, u32[]{:S(2)}, u32[]{:S(2)}) collective-permute-start(bf16[192,1792]{1,0:T(8,128)(2,1)S(1)} %stack_cotangents_plane.1._.refs_1_), channel_id=1, source_target_pairs={{0,1},{1,0},{2,3},{3,2},{4,5},{5,4},{6,7},{7,6},{8,9},{9,8},{10,11... | collective-permute-start | bytes 2064392 | tf_op jit(solution)/shard_map/ppermute | solution.py:54
  50.8 8.6 %collective-permute-start.13 = (bf16[2,2,64,1792]{3,2,1,0:T(8,128)(2,1)S(1)}, bf16[2,2,64,1792]{3,2,1,0:T(8,128)(2,1)S(1)}, u32[]{:S(2)}, u32[]{:S(2)}) collective-permute-start(bf16[2,2,64,1792]{3,2,1,0:T(8,128)(2,1)S(1)} %get-tuple-element.56), channel_id=1, source_target_pairs={{0,1},{1,0},{2,3},{3,2},{4,5},{5,4},{6,7},{7,6},{8,9},{9,8},{10,11... | collective-permute-start | bytes 2752520 | tf_op jit(solution)/shard_map/ppermute | solution.py:54
  59.6 14.6 %collective-permute-start.16 = (bf16[64,1792]{1,0:T(8,128)(2,1)S(1)}, bf16[64,1792]{1,0:T(8,128)(2,1)S(1)}, u32[]{:S(2)}, u32[]{:S(2)}) collective-permute-start(bf16[64,1792]{1,0:T(8,128)(2,1)S(1)} %get-tuple-element.62), channel_id=1, source_target_pairs={{0,2},{1,3},{2,0},{3,1},{4,6},{5,7},{6,4},{7,5},{8,10},{9,11},{10,... | collective-permute-start | bytes 688136 | tf_op jit(solution)/shard_map/ppermute | solution.py:54
  61.2 13.1 %collective-permute-start.17 = (bf16[64,1792]{1,0:T(8,128)(2,1)S(1)}, bf16[64,1792]{1,0:T(8,128)(2,1)S(1)}, u32[]{:S(2)}, u32[]{:S(2)}) collective-permute-start(bf16[64,1792]{1,0:T(8,128)(2,1)S(1)} %get-tuple-element.63), channel_id=1, source_target_pairs={{0,4},{1,5},{2,6},{3,7},{4,0},{5,1},{6,2},{7,3},{8,12},{9,13},{10,... | collective-permute-start | bytes 688136 | tf_op jit(solution)/shard_map/ppermute | solution.py:54
  62.6 11.6 %collective-permute-start.18 = (bf16[64,1792]{1,0:T(8,128)(2,1)S(1)}, bf16[64,1792]{1,0:T(8,128)(2,1)S(1)}, u32[]{:S(2)}, u32[]{:S(2)}) collective-permute-start(bf16[64,1792]{1,0:T(8,128)(2,1)S(1)} %get-tuple-element.64), channel_id=1, source_target_pairs={{0,6},{1,7},{2,4},{3,5},{4,2},{5,3},{6,0},{7,1},{8,14},{9,15},{10,... | collective-permute-start | bytes 688136 | tf_op jit(solution)/shard_map/ppermute | solution.py:54
  74.4 3.0 %collective-permute-start.22 = (bf16[2,2,64,1792]{3,2,1,0:T(8,128)(2,1)S(1)}, bf16[2,2,64,1792]{3,2,1,0:T(8,128)(2,1)S(1)}, u32[]{:S(2)}, u32[]{:S(2)}) collective-permute-start(bf16[2,2,64,1792]{3,2,1,0:T(8,128)(2,1)S(1)} %get-tuple-element.73), channel_id=1, source_target_pairs={{0,1},{1,0},{2,3},{3,2},{4,5},{5,4},{6,7},{7,6},{8,9},{9,8},{10,11... | collective-permute-start | bytes 2752520 | tf_op jit(solution)/shard_map/ppermute | solution.py:54
  74.5 25.7 %collective-permute-start.19 = (bf16[16,1792]{1,0:T(8,128)(2,1)S(1)}, bf16[16,1792]{1,0:T(8,128)(2,1)S(1)}, u32[]{:S(2)}, u32[]{:S(2)}) collective-permute-start(bf16[16,1792]{1,0:T(8,128)(2,1)S(1)} %get-tuple-element.70), channel_id=1, source_target_pairs={{0,8},{1,9},{2,10},{3,11},{4,12},{5,13},{6,14},{7,15},{8,0},{9,1},... | collective-permute-start | bytes 172040 | tf_op jit(solution)/shard_map/ppermute | solution.py:54
  74.7 34.5 %collective-permute-start.20 = (bf16[16,1792]{1,0:T(8,128)(2,1)S(1)}, bf16[16,1792]{1,0:T(8,128)(2,1)S(1)}, u32[]{:S(2)}, u32[]{:S(2)}) collective-permute-start(bf16[16,1792]{1,0:T(8,128)(2,1)S(1)} %get-tuple-element.71), channel_id=1, source_target_pairs={{0,16},{1,17},{2,18},{3,19},{4,20},{5,21},{6,22},{7,23},{8,24},{9,... | collective-permute-start | bytes 172040 | tf_op jit(solution)/shard_map/ppermute | solution.py:54
  77.6 17.9 %collective-permute-start.23 = (bf16[64,1792]{1,0:T(8,128)(2,1)S(1)}, bf16[64,1792]{1,0:T(8,128)(2,1)S(1)}, u32[]{:S(2)}, u32[]{:S(2)}) collective-permute-start(bf16[64,1792]{1,0:T(8,128)(2,1)S(1)} %get-tuple-element.75), channel_id=1, source_target_pairs={{0,2},{1,3},{2,0},{3,1},{4,6},{5,7},{6,4},{7,5},{8,10},{9,11},{10,... | collective-permute-start | bytes 688136 | tf_op jit(solution)/shard_map/ppermute | solution.py:54
  79.2 18.2 %collective-permute-start.24 = (bf16[64,1792]{1,0:T(8,128)(2,1)S(1)}, bf16[64,1792]{1,0:T(8,128)(2,1)S(1)}, u32[]{:S(2)}, u32[]{:S(2)}) collective-permute-start(bf16[64,1792]{1,0:T(8,128)(2,1)S(1)} %get-tuple-element.76), channel_id=1, source_target_pairs={{0,4},{1,5},{2,6},{3,7},{4,0},{5,1},{6,2},{7,3},{8,12},{9,13},{10,... | collective-permute-start | bytes 688136 | tf_op jit(solution)/shard_map/ppermute | solution.py:54
  80.7 16.7 %collective-permute-start.25 = (bf16[64,1792]{1,0:T(8,128)(2,1)S(1)}, bf16[64,1792]{1,0:T(8,128)(2,1)S(1)}, u32[]{:S(2)}, u32[]{:S(2)}) collective-permute-start(bf16[64,1792]{1,0:T(8,128)(2,1)S(1)} %get-tuple-element.77), channel_id=1, source_target_pairs={{0,6},{1,7},{2,4},{3,5},{4,2},{5,3},{6,0},{7,1},{8,14},{9,15},{10,... | collective-permute-start | bytes 688136 | tf_op jit(solution)/shard_map/ppermute | solution.py:54
  95.5 13.7 %collective-permute-start.21 = (bf16[16,1792]{1,0:T(8,128)(2,1)S(1)}, bf16[16,1792]{1,0:T(8,128)(2,1)S(1)}, u32[]{:S(2)}, u32[]{:S(2)}) collective-permute-start(bf16[16,1792]{1,0:T(8,128)(2,1)S(1)} %get-tuple-element.72), channel_id=1, source_target_pairs={{0,24},{1,25},{2,26},{3,27},{4,28},{5,29},{6,30},{7,31},{8,16},{9,... | collective-permute-start | bytes 172040 | tf_op jit(solution)/shard_map/ppermute | solution.py:54
  97.5 11.7 %collective-permute-start.26 = (bf16[16,1792]{1,0:T(8,128)(2,1)S(1)}, bf16[16,1792]{1,0:T(8,128)(2,1)S(1)}, u32[]{:S(2)}, u32[]{:S(2)}) collective-permute-start(bf16[16,1792]{1,0:T(8,128)(2,1)S(1)} %get-tuple-element.82), channel_id=1, source_target_pairs={{0,8},{1,9},{2,10},{3,11},{4,12},{5,13},{6,14},{7,15},{8,0},{9,1},... | collective-permute-start | bytes 172040 | tf_op jit(solution)/shard_map/ppermute | solution.py:54
  97.6 11.6 %collective-permute-start.27 = (bf16[16,1792]{1,0:T(8,128)(2,1)S(1)}, bf16[16,1792]{1,0:T(8,128)(2,1)S(1)}, u32[]{:S(2)}, u32[]{:S(2)}) collective-permute-start(bf16[16,1792]{1,0:T(8,128)(2,1)S(1)} %get-tuple-element.83), channel_id=1, source_target_pairs={{0,16},{1,17},{2,18},{3,19},{4,20},{5,21},{6,22},{7,23},{8,24},{9,... | collective-permute-start | bytes 172040 | tf_op jit(solution)/shard_map/ppermute | solution.py:54
  100.1 9.1 %collective-permute-start.28 = (bf16[16,1792]{1,0:T(8,128)(2,1)S(1)}, bf16[16,1792]{1,0:T(8,128)(2,1)S(1)}, u32[]{:S(2)}, u32[]{:S(2)}) collective-permute-start(bf16[16,1792]{1,0:T(8,128)(2,1)S(1)} %get-tuple-element.84), channel_id=1, source_target_pairs={{0,24},{1,25},{2,26},{3,27},{4,28},{5,29},{6,30},{7,31},{8,16},{9,... | collective-permute-start | bytes 172040 | tf_op jit(solution)/shard_map/ppermute | solution.py:54

commit v3 on v1

--- a/solution.py
+++ b/solution.py
@@ -421,9 +421,17 @@
         du_ref[e] = (acc[e] * q_ref[e]).astype(BF16)
 
 
-def backward_kernel(s, dg_ref, du_ref, back_ref, held_ref, w_ref, _, *refs):
-    outs, (room, sems) = refs[:-2], refs[-2:]
+def backward_kernel(s, dg_ref, du_ref, back_ref, act_ref, d_ref, held_ref, w_ref, _, *refs):
+    outs, (out, room, sems, turned, store, store_sems) = refs[:-6], refs[-6:]
     weights = Stream(s, w_ref, room, sems, s.grid.source)
+    turn(s, act_ref, turned)
+
+    def copy(k, p):
+        at, size = s.pieces[p]
+        start = pl.multiple_of(s.grid.source(k) * s.width + at, LANES)
+        return pltpu.make_async_copy(
+            store.at[p, :, :, pl.ds(0, size)], out.at[:, :, pl.ds(start, size)], store_sems.at[p]
+        )
 
     def step(k, _):
         for p, (at, size) in enumerate(s.pieces):
@@ -432,9 +440,20 @@
             found = [(dot(dg_ref[e], gate[e]) + dot(du_ref[e], up[e])).astype(BF16) for e in range(s.local)]
             to_tokens(s, k, at, found, back_ref, outs)
             weights.free(k, p)
+
+            @pl.when(k >= 1)
+            def _():
+                copy(k - 1, p).wait()
+
+            for e in range(s.local):
+                rows = d_ref[s.grid.source(k), s.at(e), at : at + size]
+                store[p, e, :, :size] = dot(turned[e], rows).astype(BF16)
+            copy(k, p).start()
         return 0
 
     lax.fori_loop(0, s.slices, step, 0)
+    for p in range(len(s.pieces)):
+        copy(s.slices - 1, p).wait()
 
 
 def turn(s, left_ref, turned):
@@ -442,9 +461,10 @@
         turned[e] = jnp.transpose(left_ref[e].astype(F32)).astype(BF16)
 
 
-def grads_kernel(s, count, *refs):
+def grads_kernel(s, spans, skip, *refs):
+    count = len(spans)
     lefts, rows_refs = refs[:count], refs[count : 2 * count]
-    outs, (marker, turned, store, sems) = refs[2 * count + 1 : -4], refs[-4:]
+    outs, (marker, turned, store, sems) = refs[2 * count + skip : -4], refs[-4:]
     marker[...] = jnp.zeros_like(marker)
     pieces = len(s.pieces)
 
@@ -456,13 +476,13 @@
             store.at[slot, :, :, pl.ds(0, size)], out.at[:, :, pl.ds(start, size)], sems.at[slot]
         )
 
-    for left_ref, rows_ref, out in zip(lefts, rows_refs, outs):
+    for (low, high), left_ref, rows_ref, out in zip(spans, lefts, rows_refs, outs):
         turn(s, left_ref, turned)
 
         def step(k, _):
             for p, (at, size) in enumerate(s.pieces):
 
-                @pl.when(k >= 2)
+                @pl.when(k >= low + 2)
                 def _():
                     copy(out, k - 2, p).wait()
 
@@ -472,28 +492,29 @@
                 copy(out, k, p).start()
             return 0
 
-        lax.fori_loop(0, s.slices, step, 0)
-        for k in range(max(0, s.slices - 2), s.slices):
+        lax.fori_loop(low, high, step, 0)
+        for k in range(max(low, high - 2), high):
             for p in range(pieces):
                 copy(out, k, p).wait()
 
 
-def grads(s, name, lefts, rights, after):
+def grads(s, name, lefts, rights, spans, after, into=()):
     room = max(size for _, size in s.pieces)
     count = len(lefts)
     slots = 2 * len(s.pieces)
     return call(
-        functools.partial(grads_kernel, s, count),
+        functools.partial(grads_kernel, s, spans, 1 + len(into)),
         name,
         [shaped(BF16, s.local, s.hidden, s.features)] * count + [shaped(F32, 8, LANES)],
-        [*lefts, *rights, after],
-        specs=[VECTORS] * (2 * count) + [ANYWHERE],
+        [*lefts, *rights, after, *into],
+        specs=[VECTORS] * (2 * count) + [ANYWHERE] * (1 + len(into)),
         out_specs=[ANYWHERE] * count + [VECTORS],
         scratch=[
             pltpu.VMEM((s.local, s.hidden, s.rows), BF16),
             pltpu.VMEM((slots, s.local, s.hidden, room), BF16),
             pltpu.SemaphoreType.DMA((slots,)),
         ],
+        aliases={2 * count + 1 + n: n for n in range(len(into))},
         cost=46000,
     )
 
@@ -566,20 +587,29 @@
         cost=46000,
     )
     mixed_kept = back_over_cores(grid, out_parts, [d_gate], "mixed_cores")
-    back_parts = call(
+    *back_parts, grad_down = call(
         functools.partial(backward_kernel, s),
         "backward",
-        [sums] * grid.nc,
-        [d_gate, d_up, back, held_gate, hbm(w_up), mixed_kept[0]],
-        specs=[VECTORS] * 4 + [ANYWHERE] * 2,
-        scratch=streams,
+        [sums] * grid.nc + [shaped(BF16, *w_down.shape)],
+        [d_gate, d_up, back, act, d_rows, held_gate, hbm(w_up), mixed_kept[0]],
+        specs=[VECTORS] * 6 + [ANYWHERE] * 2,
+        out_specs=[VECTORS] * grid.nc + [ANYWHERE],
+        scratch=[
+            *streams,
+            pltpu.VMEM((s.local, s.hidden, s.rows), BF16),
+            pltpu.VMEM((len(s.pieces), s.local, s.hidden, room), BF16),
+            pltpu.SemaphoreType.DMA((len(s.pieces),)),
+        ],
         cost=46000,
     )
     *mixed_total, last = back_over_plane(grid, mixed_kept, back_parts[:1], "mixed_plane", back_parts[-1:])
     token_kept = back_over_cores(grid, [*back_parts[:-1], last], [], "tokens_cores")
-    grad_gate, grad_down, done = grads(s, "grad_gate_down", [d_gate, act], [x_rows, d_rows], token_kept[0])
+    spans = [(0, s.slices), (0, s.slices // 2), (s.slices // 2, s.slices)]
+    grad_gate, grad_up, done = grads(
+        s, "grad_gate_up", [d_gate, d_up], [x_rows, x_rows], spans[:2], token_kept[0]
+    )
     token_total = back_over_plane(grid, token_kept, [done], "tokens_plane")
-    grad_up, done = grads(s, "grad_up", [d_up], [x_rows], token_total[0])
+    grad_up, done = grads(s, "grad_up", [d_up], [x_rows], spans[2:], token_total[0], [grad_up])
     mixed, grad_tokens = finish(back_along_z(grid, mixed_total), back_along_z(grid, token_total), [done])
     return mixed, grad_tokens, grad_gate, grad_up, grad_down
 

time: 108 us -> 110 us (1.019)
  Pallas kernels: 65.7 us -> 67 us
    pallas_call x19, Pallas kernels: 65.7 us -> 67 us  [call(): pl.pallas_call(kernel, name=name, grid=grid, out_shape=outs, in_specs=spe...]
where the time goes in v3:
time: 110 us; the launch traced here: 109 us
  Pallas kernels  67 us (61%)
  starting transfers between devices  33.6 us (31%)
  waiting for transfers between devices  8.02 us (7%)
    pallas_call x19, Pallas kernels, call(): pl.pallas_call(kernel, name=name, grid=grid, out_shape=outs, in_specs=spe...  67 us
    ppermute x29, starting transfers between devices, shift(): return lax.ppermute(value, AXES, pairs)  33.6 us
    ppermute x29, waiting for transfers between devices, shift(): return lax.ppermute(value, AXES, pairs)  8.02 us
  transfers between devices with their start and end apart: 29, of which 4 were waited for; matrix products, arithmetic and copies ran while one was open for 0% of the time, Pallas kernels for 59%

profile of v3, /device:TPU:0, one launch (start us, length us, event | category | flops | bytes accessed | tf_op | source)
XLA Modules:
  0.0 109.5 jit_solution(3272720283935678847)
XLA Ops:
  0.6 1.0 pack.1
  1.6 5.1 %collective-permute-start.2 = (bf16[16,1920]{1,0:T(8,128)(2,1)S(1)}, bf16[16,1920]{1,0:T(8,128)(2,1)S(1)}, u32[]{:S(2)}, u32[]{:S(2)}) collective-permute-start(bf16[16,1920]{1,0:T(8,128)(2,1)S(1)} %get-tuple-element.49.refs_0_), channel_id=1, source_target_pairs={{0,24},{1,25},{2,26},{3,27},{4,28},{5,29},{6,30},{7,31},{8,16},{9,... | collective-permute-start | bytes 184328 | tf_op jit(solution)/shard_map/ppermute | solution.py:54
  6.8 0.0 collective-permute-start.1
  6.8 0.6 collective-permute-start
  7.4 1.8 %collective-permute-done.2.refs_3_ = bf16[16,1920]{1,0:T(8,128)(2,1)S(1)} collective-permute-done((bf16[16,1920]{1,0:T(8,128)(2,1)S(1)}, bf16[16,1920]{1,0:T(8,128)(2,1)S(1)}, u32[]{:S(2)}, u32[]{:S(2)}) %collective-permute-start.2) | collective-permute-done | bytes 61472 | tf_op jit(solution)/shard_map/ppermute | solution.py:54
  9.2 2.8 %collective-permute-done.1.refs_2_ = bf16[16,1920]{1,0:T(8,128)(2,1)S(1)} collective-permute-done((bf16[16,1920]{1,0:T(8,128)(2,1)S(1)}, bf16[16,1920]{1,0:T(8,128)(2,1)S(1)}, u32[]{:S(2)}, u32[]{:S(2)}) %collective-permute-start.1) | collective-permute-done | bytes 61472 | tf_op jit(solution)/shard_map/ppermute | solution.py:54
  12.1 0.0 collective-permute-done.refs_1_
  12.1 1.2 %collective-permute-start.6 = (bf16[16,1792]{1,0:T(8,128)(2,1)S(1)}, bf16[16,1792]{1,0:T(8,128)(2,1)S(1)}, u32[]{:S(2)}, u32[]{:S(2)}) collective-permute-start(bf16[16,1792]{1,0:T(8,128)(2,1)S(1)} %get-tuple-element.52.refs_0_), channel_id=1, source_target_pairs={{0,8},{1,9},{2,10},{3,11},{4,12},{5,13},{6,14},{7,15},{8,0},{9,1},... | collective-permute-start | bytes 172040 | tf_op jit(solution)/shard_map/ppermute | solution.py:54
  13.3 2.4 %collective-permute-start.5 = (bf16[64,1920]{1,0:T(8,128)(2,1)S(1)}, bf16[64,1920]{1,0:T(8,128)(2,1)S(1)}, u32[]{:S(2)}, u32[]{:S(2)}) collective-permute-start(bf16[64,1920]{1,0:T(8,128)(2,1)S(1)} %get-tuple-element.51.refs_0_), channel_id=1, source_target_pairs={{0,6},{1,7},{2,4},{3,5},{4,2},{5,3},{6,0},{7,1},{8,14},{9,15},{10,... | collective-permute-start | bytes 737288 | tf_op jit(solution)/shard_map/ppermute | solution.py:54
  15.7 0.5 collective-permute-start.4
  16.2 0.5 collective-permute-start.3
  16.8 0.0 collective-permute-done.6.refs_1_
  16.8 2.2 %collective-permute-start.7 = (bf16[32,1792]{1,0:T(8,128)(2,1)S(1)}, bf16[32,1792]{1,0:T(8,128)(2,1)S(1)}, u32[]{:S(2)}, u32[]{:S(2)}) collective-permute-start(bf16[32,1792]{1,0:T(8,128)(2,1)S(1)} %double.2._.refs_0_), channel_id=1, source_target_pairs={{0,16},{1,17},{2,18},{3,19},{4,20},{5,21},{6,22},{7,23},{8,24},{9,... | collective-permute-start | bytes 344072 | tf_op jit(solution)/shard_map/ppermute | solution.py:54
  19.0 3.6 %hold_down.1.refs_2_.held_ref = bf16[2,608,3584]{2,1,0:T(8,128)(2,1)S(1)} custom-call(bf16[2,608,7168]{2,1,0:T(8,128)(2,1)} %refs_8_.1, bf16[32,1792]{1,0:T(8,128)(2,1)S(1)} %double.2._.refs_0_), custom_call_target="tpu_custom_call" | custom-call | flops 12000000000 | tf_op jit(solution)/shard_map/hold_down/pallas_call | solution.py:78
  22.6 1.2 %collective-permute-done.7.refs_1_ = bf16[32,1792]{1,0:T(8,128)(2,1)S(1)} collective-permute-done((bf16[32,1792]{1,0:T(8,128)(2,1)S(1)}, bf16[32,1792]{1,0:T(8,128)(2,1)S(1)}, u32[]{:S(2)}, u32[]{:S(2)}) %collective-permute-start.7) | collective-permute-done | bytes 114720 | tf_op jit(solution)/shard_map/ppermute | solution.py:54
  23.8 0.0 collective-permute-done.5.refs_2_
  23.8 2.1 %collective-permute-done.4.refs_1_ = bf16[64,1920]{1,0:T(8,128)(2,1)S(1)} collective-permute-done((bf16[64,1920]{1,0:T(8,128)(2,1)S(1)}, bf16[64,1920]{1,0:T(8,128)(2,1)S(1)}, u32[]{:S(2)}, u32[]{:S(2)}) %collective-permute-start.4) | collective-permute-done | bytes 245792 | tf_op jit(solution)/shard_map/ppermute | solution.py:54
  25.9 0.0 collective-permute-done.3.refs_0_
  25.9 0.1 stack_tokens_plane.1.refs_1_
  26.0 0.1 collective-permute-start.9
  26.1 0.5 collective-permute-start.8
  26.6 0.1 collective-permute-start.14
  26.7 2.3 %collective-permute-start.12 = (bf16[64,1792]{1,0:T(8,128)(2,1)S(1)}, bf16[64,1792]{1,0:T(8,128)(2,1)S(1)}, u32[]{:S(2)}, u32[]{:S(2)}) collective-permute-start(bf16[64,1792]{1,0:T(8,128)(2,1)S(1)} %stack_cotangents.1.refs_6_.refs_0_), channel_id=1, source_target_pairs={{0,6},{1,7},{2,4},{3,5},{4,2},{5,3},{6,0},{7,1},{8,14},{9,15},{10,... | collective-permute-start | bytes 688136 | tf_op jit(solution)/shard_map/ppermute | solution.py:54
  29.1 0.5 collective-permute-start.11
  29.6 0.0 collective-permute-done.8.refs_2_
  29.6 0.6 collective-permute-start.10
  30.2 0.0 collective-permute-done.9.refs_3_
  30.2 14.5 %gate_up.1 = (bf16[4,64,1792]{2,1,0:T(8,128)(2,1)S(1)}, bf16[64,128]{1,0:T(8,128)(2,1)S(1)}, bf16[128,64]{1,0:T(8,128)(2,1)S(1)}, f32[64,128]{1,0:T(8,128)S(1)},...) custom-call(bf16[64,1920]{1,0:T(8,128)(2,1)S(1)} %get-tuple-element., ...), custom_call_target="tpu_custom_call" | custom-call | flops 46000001024 | tf_op jit(solution)/shard_map/gate_up/pallas_call | solution.py:78
  44.7 0.0 collective-permute-done.12.refs_2_
  44.8 0.0 collective-permute-done.11.refs_1_
  44.8 0.0 collective-permute-done.10.refs_0_
  44.8 0.1 collective-permute-start.15
  44.9 5.4 %forward.1 = (bf16[2,2,64,1792]{3,2,1,0:T(8,128)(2,1)S(1)}, bf16[2,2,64,1792]{3,2,1,0:T(8,128)(2,1)S(1)}) custom-call(bf16[2,32,608]{2,1,0:T(8,128)(2,1)S(1)} %get-tuple-element.53.act_ref, f32[64,128]{1,0:T(8,128)S(1)} %get-tuple-element.54.refs_3_.gate_ref.refs_5_, bf16[128,64]{1,0:T(8,128)(2,1)S(1)} %get-tuple-element.55.back_ref, ...), custom_call_target="tpu_custom_call" | custom-call | flops 46000001024 | tf_op jit(solution)/shard_map/forward/pallas_call | solution.py:78
  50.3 0.5 collective-permute-start.13
  50.9 0.0 collective-permute-done.14.refs_2_
  50.9 0.0 collective-permute-done.15.refs_3_
  50.9 8.0 %hidden_grads.1 = (bf16[4,64,1792]{2,1,0:T(8,128)(2,1)S(1)}, bf16[2,32,608]{2,1,0:T(8,128)(2,1)S(1)}, bf16[2,32,608]{2,1,0:T(8,128)(2,1)S(1)}) custom-call(bf16[64,1792]{1,0:T(8,128)(2,1)S(1)} %stack_cotangents.1.refs_6_.refs_0_, bf16[192,1792]{1,0:T(8,128)(2,1)S(1)} %stack_cotangents_plane.1._.refs_1_, ...), custom_call_target="tpu_custom_call" | custom-call | flops 46000001024 | tf_op jit(solution)/shard_map/hidden_grads/pallas_call | solution.py:78
  58.9 0.2 mixed_cores.1
  59.1 1.5 %collective-permute-start.16 = (bf16[64,1792]{1,0:T(8,128)(2,1)S(1)}, bf16[64,1792]{1,0:T(8,128)(2,1)S(1)}, u32[]{:S(2)}, u32[]{:S(2)}) collective-permute-start(bf16[64,1792]{1,0:T(8,128)(2,1)S(1)} %get-tuple-element.63), channel_id=1, source_target_pairs={{0,2},{1,3},{2,0},{3,1},{4,6},{5,7},{6,4},{7,5},{8,10},{9,11},{10,... | collective-permute-start | bytes 688136 | tf_op jit(solution)/shard_map/ppermute | solution.py:54
  60.6 1.5 %collective-permute-start.17 = (bf16[64,1792]{1,0:T(8,128)(2,1)S(1)}, bf16[64,1792]{1,0:T(8,128)(2,1)S(1)}, u32[]{:S(2)}, u32[]{:S(2)}) collective-permute-start(bf16[64,1792]{1,0:T(8,128)(2,1)S(1)} %get-tuple-element.64), channel_id=1, source_target_pairs={{0,4},{1,5},{2,6},{3,7},{4,0},{5,1},{6,2},{7,3},{8,12},{9,13},{10,... | collective-permute-start | bytes 688136 | tf_op jit(solution)/shard_map/ppermute | solution.py:54
  62.1 0.6 collective-permute-start.18
  62.7 17.0 %backward.1 = (bf16[2,2,64,1792]{3,2,1,0:T(8,128)(2,1)S(1)}, bf16[2,2,64,1792]{3,2,1,0:T(8,128)(2,1)S(1)}, bf16[2,608,7168]{2,1,0:T(8,128)(2,1)}) custom-call(bf16[2,32,608]{2,1,0:T(8,128)(2,1)S(1)} %get-tuple-element.61.refs_2_.dg_ref.refs_0_, bf16[2,32,608]{2,1,0:T(8,128)(2,1)S(1)} %get-tuple-element.66.du_ref.refs_1_.refs_0_, ...), custom_call_target="tpu_custom_call" | custom-call | flops 46000001024 | tf_op jit(solution)/shard_map/backward/pallas_call | solution.py:78
  79.6 0.0 collective-permute-done.16.refs_1_
  79.7 0.0 collective-permute-done.18.refs_3_
  79.7 0.1 mixed_plane.1
  79.8 0.1 collective-permute-start.22
  79.9 1.7 %collective-permute-start.19 = (bf16[16,1792]{1,0:T(8,128)(2,1)S(1)}, bf16[16,1792]{1,0:T(8,128)(2,1)S(1)}, u32[]{:S(2)}, u32[]{:S(2)}) collective-permute-start(bf16[16,1792]{1,0:T(8,128)(2,1)S(1)} %get-tuple-element.72), channel_id=1, source_target_pairs={{0,8},{1,9},{2,10},{3,11},{4,12},{5,13},{6,14},{7,15},{8,0},{9,1},... | collective-permute-start | bytes 172040 | tf_op jit(solution)/shard_map/ppermute | solution.py:54
  81.6 0.8 collective-permute-start.20
  82.4 0.0 collective-permute-done.22.refs_1_
  82.4 0.2 tokens_cores.1
  82.6 1.5 %collective-permute-start.23 = (bf16[64,1792]{1,0:T(8,128)(2,1)S(1)}, bf16[64,1792]{1,0:T(8,128)(2,1)S(1)}, u32[]{:S(2)}, u32[]{:S(2)}) collective-permute-start(bf16[64,1792]{1,0:T(8,128)(2,1)S(1)} %get-tuple-element.77), channel_id=1, source_target_pairs={{0,2},{1,3},{2,0},{3,1},{4,6},{5,7},{6,4},{7,5},{8,10},{9,11},{10,... | collective-permute-start | bytes 688136 | tf_op jit(solution)/shard_map/ppermute | solution.py:54
  84.1 1.5 %collective-permute-start.24 = (bf16[64,1792]{1,0:T(8,128)(2,1)S(1)}, bf16[64,1792]{1,0:T(8,128)(2,1)S(1)}, u32[]{:S(2)}, u32[]{:S(2)}) collective-permute-start(bf16[64,1792]{1,0:T(8,128)(2,1)S(1)} %get-tuple-element.78), channel_id=1, source_target_pairs={{0,4},{1,5},{2,6},{3,7},{4,0},{5,1},{6,2},{7,3},{8,12},{9,13},{10,... | collective-permute-start | bytes 688136 | tf_op jit(solution)/shard_map/ppermute | solution.py:54
  85.6 0.6 collective-permute-start.25
  86.2 11.6 %grad_gate_up.1 = (bf16[2,608,7168]{2,1,0:T(8,128)(2,1)}, bf16[2,608,7168]{2,1,0:T(8,128)(2,1)}, f32[8,128]{1,0:T(8,128)S(1)}) custom-call(bf16[2,32,608]{2,1,0:T(8,128)(2,1)S(1)} %get-tuple-element.61.refs_2_.dg_ref.refs_0_, bf16[2,32,608]{2,1,0:T(8,128)(2,1)S(1)} %get-tuple-element.66.du_ref.refs_1_.refs_0_, ...), custom_call_target="tpu_custom_call" | custom-call | flops 46000001024 | tf_op jit(solution)/shard_map/grad_gate_up/pallas_call | solution.py:78
  97.7 0.0 collective-permute-done.23.refs_1_
  97.7 2.0 %collective-permute-start.21 = (bf16[16,1792]{1,0:T(8,128)(2,1)S(1)}, bf16[16,1792]{1,0:T(8,128)(2,1)S(1)}, u32[]{:S(2)}, u32[]{:S(2)}) collective-permute-start(bf16[16,1792]{1,0:T(8,128)(2,1)S(1)} %get-tuple-element.74), channel_id=1, source_target_pairs={{0,24},{1,25},{2,26},{3,27},{4,28},{5,29},{6,30},{7,31},{8,16},{9,... | collective-permute-start | bytes 172040 | tf_op jit(solution)/shard_map/ppermute | solution.py:54
  99.8 0.1 tokens_plane.1
  99.9 0.8 collective-permute-start.26
  100.7 1.7 %collective-permute-start.27 = (bf16[16,1792]{1,0:T(8,128)(2,1)S(1)}, bf16[16,1792]{1,0:T(8,128)(2,1)S(1)}, u32[]{:S(2)}, u32[]{:S(2)}) collective-permute-start(bf16[16,1792]{1,0:T(8,128)(2,1)S(1)} %get-tuple-element.84), channel_id=1, source_target_pairs={{0,16},{1,17},{2,18},{3,19},{4,20},{5,21},{6,22},{7,23},{8,24},{9,... | collective-permute-start | bytes 172040 | tf_op jit(solution)/shard_map/ppermute | solution.py:54
  102.4 2.0 %collective-permute-start.28 = (bf16[16,1792]{1,0:T(8,128)(2,1)S(1)}, bf16[16,1792]{1,0:T(8,128)(2,1)S(1)}, u32[]{:S(2)}, u32[]{:S(2)}) collective-permute-start(bf16[16,1792]{1,0:T(8,128)(2,1)S(1)} %get-tuple-element.85), channel_id=1, source_target_pairs={{0,24},{1,25},{2,26},{3,27},{4,28},{5,29},{6,30},{7,31},{8,16},{9,... | collective-permute-start | bytes 172040 | tf_op jit(solution)/shard_map/ppermute | solution.py:54
  104.3 4.4 %grad_up.1 = (bf16[2,608,7168]{2,1,0:T(8,128)(2,1)}, f32[8,128]{1,0:T(8,128)S(1)}) custom-call(bf16[2,32,608]{2,1,0:T(8,128)(2,1)S(1)} %get-tuple-element.66.du_ref.refs_1_.refs_0_, bf16[4,64,1792]{2,1,0:T(8,128)(2,1)S(1)} %get-tuple-element.80.refs_2_.refs_3_.refs_1_, ...), custom_call_target="tpu_custom_call", output_to_operand_aliasing={{0}: (3, {})} | custom-call | flops 46000001024 | tf_op jit(solution)/shard_map/grad_up/pallas_call | solution.py:78
  108.7 0.0 collective-permute-done.21.refs_3_
  108.8 0.0 collective-permute-done.26.refs_5_
  108.8 0.7 finish.1
  (13 shorter events, 0.1 us)
Async XLA Ops:
  1.6 7.6 %collective-permute-start.2 = (bf16[16,1920]{1,0:T(8,128)(2,1)S(1)}, bf16[16,1920]{1,0:T(8,128)(2,1)S(1)}, u32[]{:S(2)}, u32[]{:S(2)}) collective-permute-start(bf16[16,1920]{1,0:T(8,128)(2,1)S(1)} %get-tuple-element.49.refs_0_), channel_id=1, source_target_pairs={{0,24},{1,25},{2,26},{3,27},{4,28},{5,29},{6,30},{7,31},{8,16},{9,... | collective-permute-start | bytes 184328 | tf_op jit(solution)/shard_map/ppermute | solution.py:54
  6.8 5.3 %collective-permute-start.1 = (bf16[16,1920]{1,0:T(8,128)(2,1)S(1)}, bf16[16,1920]{1,0:T(8,128)(2,1)S(1)}, u32[]{:S(2)}, u32[]{:S(2)}) collective-permute-start(bf16[16,1920]{1,0:T(8,128)(2,1)S(1)} %get-tuple-element.49.refs_0_), channel_id=1, source_target_pairs={{0,16},{1,17},{2,18},{3,19},{4,20},{5,21},{6,22},{7,23},{8,24},{9,... | collective-permute-start | bytes 184328 | tf_op jit(solution)/shard_map/ppermute | solution.py:54
  6.8 5.3 %collective-permute-start = (bf16[16,1920]{1,0:T(8,128)(2,1)S(1)}, bf16[16,1920]{1,0:T(8,128)(2,1)S(1)}, u32[]{:S(2)}, u32[]{:S(2)}) collective-permute-start(bf16[16,1920]{1,0:T(8,128)(2,1)S(1)} %get-tuple-element.49.refs_0_), channel_id=1, source_target_pairs={{0,8},{1,9},{2,10},{3,11},{4,12},{5,13},{6,14},{7,15},{8,0},{9,1},... | collective-permute-start | bytes 184328 | tf_op jit(solution)/shard_map/ppermute | solution.py:54
  12.1 4.7 %collective-permute-start.6 = (bf16[16,1792]{1,0:T(8,128)(2,1)S(1)}, bf16[16,1792]{1,0:T(8,128)(2,1)S(1)}, u32[]{:S(2)}, u32[]{:S(2)}) collective-permute-start(bf16[16,1792]{1,0:T(8,128)(2,1)S(1)} %get-tuple-element.52.refs_0_), channel_id=1, source_target_pairs={{0,8},{1,9},{2,10},{3,11},{4,12},{5,13},{6,14},{7,15},{8,0},{9,1},... | collective-permute-start | bytes 172040 | tf_op jit(solution)/shard_map/ppermute | solution.py:54
  13.3 10.5 %collective-permute-start.5 = (bf16[64,1920]{1,0:T(8,128)(2,1)S(1)}, bf16[64,1920]{1,0:T(8,128)(2,1)S(1)}, u32[]{:S(2)}, u32[]{:S(2)}) collective-permute-start(bf16[64,1920]{1,0:T(8,128)(2,1)S(1)} %get-tuple-element.51.refs_0_), channel_id=1, source_target_pairs={{0,6},{1,7},{2,4},{3,5},{4,2},{5,3},{6,0},{7,1},{8,14},{9,15},{10,... | collective-permute-start | bytes 737288 | tf_op jit(solution)/shard_map/ppermute | solution.py:54
  15.7 10.2 %collective-permute-start.4 = (bf16[64,1920]{1,0:T(8,128)(2,1)S(1)}, bf16[64,1920]{1,0:T(8,128)(2,1)S(1)}, u32[]{:S(2)}, u32[]{:S(2)}) collective-permute-start(bf16[64,1920]{1,0:T(8,128)(2,1)S(1)} %get-tuple-element.51.refs_0_), channel_id=1, source_target_pairs={{0,4},{1,5},{2,6},{3,7},{4,0},{5,1},{6,2},{7,3},{8,12},{9,13},{10,... | collective-permute-start | bytes 737288 | tf_op jit(solution)/shard_map/ppermute | solution.py:54
  16.2 9.7 %collective-permute-start.3 = (bf16[64,1920]{1,0:T(8,128)(2,1)S(1)}, bf16[64,1920]{1,0:T(8,128)(2,1)S(1)}, u32[]{:S(2)}, u32[]{:S(2)}) collective-permute-start(bf16[64,1920]{1,0:T(8,128)(2,1)S(1)} %get-tuple-element.51.refs_0_), channel_id=1, source_target_pairs={{0,2},{1,3},{2,0},{3,1},{4,6},{5,7},{6,4},{7,5},{8,10},{9,11},{10,... | collective-permute-start | bytes 737288 | tf_op jit(solution)/shard_map/ppermute | solution.py:54
  16.8 7.0 %collective-permute-start.7 = (bf16[32,1792]{1,0:T(8,128)(2,1)S(1)}, bf16[32,1792]{1,0:T(8,128)(2,1)S(1)}, u32[]{:S(2)}, u32[]{:S(2)}) collective-permute-start(bf16[32,1792]{1,0:T(8,128)(2,1)S(1)} %double.2._.refs_0_), channel_id=1, source_target_pairs={{0,16},{1,17},{2,18},{3,19},{4,20},{5,21},{6,22},{7,23},{8,24},{9,... | collective-permute-start | bytes 344072 | tf_op jit(solution)/shard_map/ppermute | solution.py:54
  26.0 4.2 %collective-permute-start.9 = (bf16[192,1920]{1,0:T(8,128)(2,1)S(1)}, bf16[192,1920]{1,0:T(8,128)(2,1)S(1)}, u32[]{:S(2)}, u32[]{:S(2)}) collective-permute-start(bf16[192,1920]{1,0:T(8,128)(2,1)S(1)} %stack_tokens_plane.1.refs_1_), channel_id=1, source_target_pairs={{0,1},{1,0},{2,3},{3,2},{4,5},{5,4},{6,7},{7,6},{8,9},{9,8},{10,11... | collective-permute-start | bytes 2211848 | tf_op jit(solution)/shard_map/ppermute | solution.py:54
  26.1 3.5 %collective-permute-start.8 = (bf16[64,1920]{1,0:T(8,128)(2,1)S(1)}, bf16[64,1920]{1,0:T(8,128)(2,1)S(1)}, u32[]{:S(2)}, u32[]{:S(2)}) collective-permute-start(bf16[64,1920]{1,0:T(8,128)(2,1)S(1)} %get-tuple-element.51.refs_0_), channel_id=1, source_target_pairs={{0,1},{1,0},{2,3},{3,2},{4,5},{5,4},{6,7},{7,6},{8,9},{9,8},{10,11... | collective-permute-start | bytes 737288 | tf_op jit(solution)/shard_map/ppermute | solution.py:54
  26.6 24.3 %collective-permute-start.14 = (bf16[64,1792]{1,0:T(8,128)(2,1)S(1)}, bf16[64,1792]{1,0:T(8,128)(2,1)S(1)}, u32[]{:S(2)}, u32[]{:S(2)}) collective-permute-start(bf16[64,1792]{1,0:T(8,128)(2,1)S(1)} %stack_cotangents.1.refs_6_.refs_0_), channel_id=1, source_target_pairs={{0,1},{1,0},{2,3},{3,2},{4,5},{5,4},{6,7},{7,6},{8,9},{9,8},{10,11... | collective-permute-start | bytes 688136 | tf_op jit(solution)/shard_map/ppermute | solution.py:54
  26.7 18.0 %collective-permute-start.12 = (bf16[64,1792]{1,0:T(8,128)(2,1)S(1)}, bf16[64,1792]{1,0:T(8,128)(2,1)S(1)}, u32[]{:S(2)}, u32[]{:S(2)}) collective-permute-start(bf16[64,1792]{1,0:T(8,128)(2,1)S(1)} %stack_cotangents.1.refs_6_.refs_0_), channel_id=1, source_target_pairs={{0,6},{1,7},{2,4},{3,5},{4,2},{5,3},{6,0},{7,1},{8,14},{9,15},{10,... | collective-permute-start | bytes 688136 | tf_op jit(solution)/shard_map/ppermute | solution.py:54
  29.1 15.7 %collective-permute-start.11 = (bf16[64,1792]{1,0:T(8,128)(2,1)S(1)}, bf16[64,1792]{1,0:T(8,128)(2,1)S(1)}, u32[]{:S(2)}, u32[]{:S(2)}) collective-permute-start(bf16[64,1792]{1,0:T(8,128)(2,1)S(1)} %stack_cotangents.1.refs_6_.refs_0_), channel_id=1, source_target_pairs={{0,4},{1,5},{2,6},{3,7},{4,0},{5,1},{6,2},{7,3},{8,12},{9,13},{10,... | collective-permute-start | bytes 688136 | tf_op jit(solution)/shard_map/ppermute | solution.py:54
  29.6 15.2 %collective-permute-start.10 = (bf16[64,1792]{1,0:T(8,128)(2,1)S(1)}, bf16[64,1792]{1,0:T(8,128)(2,1)S(1)}, u32[]{:S(2)}, u32[]{:S(2)}) collective-permute-start(bf16[64,1792]{1,0:T(8,128)(2,1)S(1)} %stack_cotangents.1.refs_6_.refs_0_), channel_id=1, source_target_pairs={{0,2},{1,3},{2,0},{3,1},{4,6},{5,7},{6,4},{7,5},{8,10},{9,11},{10,... | collective-permute-start | bytes 688136 | tf_op jit(solution)/shard_map/ppermute | solution.py:54
  44.8 6.0 %collective-permute-start.15 = (bf16[192,1792]{1,0:T(8,128)(2,1)S(1)}, bf16[192,1792]{1,0:T(8,128)(2,1)S(1)}, u32[]{:S(2)}, u32[]{:S(2)}) collective-permute-start(bf16[192,1792]{1,0:T(8,128)(2,1)S(1)} %stack_cotangents_plane.1._.refs_1_), channel_id=1, source_target_pairs={{0,1},{1,0},{2,3},{3,2},{4,5},{5,4},{6,7},{7,6},{8,9},{9,8},{10,11... | collective-permute-start | bytes 2064392 | tf_op jit(solution)/shard_map/ppermute | solution.py:54
  50.3 8.6 %collective-permute-start.13 = (bf16[2,2,64,1792]{3,2,1,0:T(8,128)(2,1)S(1)}, bf16[2,2,64,1792]{3,2,1,0:T(8,128)(2,1)S(1)}, u32[]{:S(2)}, u32[]{:S(2)}) collective-permute-start(bf16[2,2,64,1792]{3,2,1,0:T(8,128)(2,1)S(1)} %get-tuple-element.57), channel_id=1, source_target_pairs={{0,1},{1,0},{2,3},{3,2},{4,5},{5,4},{6,7},{7,6},{8,9},{9,8},{10,11... | collective-permute-start | bytes 2752520 | tf_op jit(solution)/shard_map/ppermute | solution.py:54
  59.1 20.5 %collective-permute-start.16 = (bf16[64,1792]{1,0:T(8,128)(2,1)S(1)}, bf16[64,1792]{1,0:T(8,128)(2,1)S(1)}, u32[]{:S(2)}, u32[]{:S(2)}) collective-permute-start(bf16[64,1792]{1,0:T(8,128)(2,1)S(1)} %get-tuple-element.63), channel_id=1, source_target_pairs={{0,2},{1,3},{2,0},{3,1},{4,6},{5,7},{6,4},{7,5},{8,10},{9,11},{10,... | collective-permute-start | bytes 688136 | tf_op jit(solution)/shard_map/ppermute | solution.py:54
  60.6 19.1 %collective-permute-start.17 = (bf16[64,1792]{1,0:T(8,128)(2,1)S(1)}, bf16[64,1792]{1,0:T(8,128)(2,1)S(1)}, u32[]{:S(2)}, u32[]{:S(2)}) collective-permute-start(bf16[64,1792]{1,0:T(8,128)(2,1)S(1)} %get-tuple-element.64), channel_id=1, source_target_pairs={{0,4},{1,5},{2,6},{3,7},{4,0},{5,1},{6,2},{7,3},{8,12},{9,13},{10,... | collective-permute-start | bytes 688136 | tf_op jit(solution)/shard_map/ppermute | solution.py:54
  62.1 17.6 %collective-permute-start.18 = (bf16[64,1792]{1,0:T(8,128)(2,1)S(1)}, bf16[64,1792]{1,0:T(8,128)(2,1)S(1)}, u32[]{:S(2)}, u32[]{:S(2)}) collective-permute-start(bf16[64,1792]{1,0:T(8,128)(2,1)S(1)} %get-tuple-element.65), channel_id=1, source_target_pairs={{0,6},{1,7},{2,4},{3,5},{4,2},{5,3},{6,0},{7,1},{8,14},{9,15},{10,... | collective-permute-start | bytes 688136 | tf_op jit(solution)/shard_map/ppermute | solution.py:54
  79.8 2.6 %collective-permute-start.22 = (bf16[2,2,64,1792]{3,2,1,0:T(8,128)(2,1)S(1)}, bf16[2,2,64,1792]{3,2,1,0:T(8,128)(2,1)S(1)}, u32[]{:S(2)}, u32[]{:S(2)}) collective-permute-start(bf16[2,2,64,1792]{3,2,1,0:T(8,128)(2,1)S(1)} %get-tuple-element.75), channel_id=1, source_target_pairs={{0,1},{1,0},{2,3},{3,2},{4,5},{5,4},{6,7},{7,6},{8,9},{9,8},{10,11... | collective-permute-start | bytes 2752520 | tf_op jit(solution)/shard_map/ppermute | solution.py:54
  79.9 22.5 %collective-permute-start.19 = (bf16[16,1792]{1,0:T(8,128)(2,1)S(1)}, bf16[16,1792]{1,0:T(8,128)(2,1)S(1)}, u32[]{:S(2)}, u32[]{:S(2)}) collective-permute-start(bf16[16,1792]{1,0:T(8,128)(2,1)S(1)} %get-tuple-element.72), channel_id=1, source_target_pairs={{0,8},{1,9},{2,10},{3,11},{4,12},{5,13},{6,14},{7,15},{8,0},{9,1},... | collective-permute-start | bytes 172040 | tf_op jit(solution)/shard_map/ppermute | solution.py:54
  81.6 27.1 %collective-permute-start.20 = (bf16[16,1792]{1,0:T(8,128)(2,1)S(1)}, bf16[16,1792]{1,0:T(8,128)(2,1)S(1)}, u32[]{:S(2)}, u32[]{:S(2)}) collective-permute-start(bf16[16,1792]{1,0:T(8,128)(2,1)S(1)} %get-tuple-element.73), channel_id=1, source_target_pairs={{0,16},{1,17},{2,18},{3,19},{4,20},{5,21},{6,22},{7,23},{8,24},{9,... | collective-permute-start | bytes 172040 | tf_op jit(solution)/shard_map/ppermute | solution.py:54
  82.6 15.1 %collective-permute-start.23 = (bf16[64,1792]{1,0:T(8,128)(2,1)S(1)}, bf16[64,1792]{1,0:T(8,128)(2,1)S(1)}, u32[]{:S(2)}, u32[]{:S(2)}) collective-permute-start(bf16[64,1792]{1,0:T(8,128)(2,1)S(1)} %get-tuple-element.77), channel_id=1, source_target_pairs={{0,2},{1,3},{2,0},{3,1},{4,6},{5,7},{6,4},{7,5},{8,10},{9,11},{10,... | collective-permute-start | bytes 688136 | tf_op jit(solution)/shard_map/ppermute | solution.py:54
  84.1 15.7 %collective-permute-start.24 = (bf16[64,1792]{1,0:T(8,128)(2,1)S(1)}, bf16[64,1792]{1,0:T(8,128)(2,1)S(1)}, u32[]{:S(2)}, u32[]{:S(2)}) collective-permute-start(bf16[64,1792]{1,0:T(8,128)(2,1)S(1)} %get-tuple-element.78), channel_id=1, source_target_pairs={{0,4},{1,5},{2,6},{3,7},{4,0},{5,1},{6,2},{7,3},{8,12},{9,13},{10,... | collective-permute-start | bytes 688136 | tf_op jit(solution)/shard_map/ppermute | solution.py:54
  85.6 14.2 %collective-permute-start.25 = (bf16[64,1792]{1,0:T(8,128)(2,1)S(1)}, bf16[64,1792]{1,0:T(8,128)(2,1)S(1)}, u32[]{:S(2)}, u32[]{:S(2)}) collective-permute-start(bf16[64,1792]{1,0:T(8,128)(2,1)S(1)} %get-tuple-element.79), channel_id=1, source_target_pairs={{0,6},{1,7},{2,4},{3,5},{4,2},{5,3},{6,0},{7,1},{8,14},{9,15},{10,... | collective-permute-start | bytes 688136 | tf_op jit(solution)/shard_map/ppermute | solution.py:54
  97.7 11.0 %collective-permute-start.21 = (bf16[16,1792]{1,0:T(8,128)(2,1)S(1)}, bf16[16,1792]{1,0:T(8,128)(2,1)S(1)}, u32[]{:S(2)}, u32[]{:S(2)}) collective-permute-start(bf16[16,1792]{1,0:T(8,128)(2,1)S(1)} %get-tuple-element.74), channel_id=1, source_target_pairs={{0,24},{1,25},{2,26},{3,27},{4,28},{5,29},{6,30},{7,31},{8,16},{9,... | collective-permute-start | bytes 172040 | tf_op jit(solution)/shard_map/ppermute | solution.py:54
  99.9 8.9 %collective-permute-start.26 = (bf16[16,1792]{1,0:T(8,128)(2,1)S(1)}, bf16[16,1792]{1,0:T(8,128)(2,1)S(1)}, u32[]{:S(2)}, u32[]{:S(2)}) collective-permute-start(bf16[16,1792]{1,0:T(8,128)(2,1)S(1)} %get-tuple-element.83), channel_id=1, source_target_pairs={{0,8},{1,9},{2,10},{3,11},{4,12},{5,13},{6,14},{7,15},{8,0},{9,1},... | collective-permute-start | bytes 172040 | tf_op jit(solution)/shard_map/ppermute | solution.py:54
  100.7 8.1 %collective-permute-start.27 = (bf16[16,1792]{1,0:T(8,128)(2,1)S(1)}, bf16[16,1792]{1,0:T(8,128)(2,1)S(1)}, u32[]{:S(2)}, u32[]{:S(2)}) collective-permute-start(bf16[16,1792]{1,0:T(8,128)(2,1)S(1)} %get-tuple-element.84), channel_id=1, source_target_pairs={{0,16},{1,17},{2,18},{3,19},{4,20},{5,21},{6,22},{7,23},{8,24},{9,... | collective-permute-start | bytes 172040 | tf_op jit(solution)/shard_map/ppermute | solution.py:54
  102.4 6.4 %collective-permute-start.28 = (bf16[16,1792]{1,0:T(8,128)(2,1)S(1)}, bf16[16,1792]{1,0:T(8,128)(2,1)S(1)}, u32[]{:S(2)}, u32[]{:S(2)}) collective-permute-start(bf16[16,1792]{1,0:T(8,128)(2,1)S(1)} %get-tuple-element.85), channel_id=1, source_target_pairs={{0,24},{1,25},{2,26},{3,27},{4,28},{5,29},{6,30},{7,31},{8,16},{9,... | collective-permute-start | bytes 172040 | tf_op jit(solution)/shard_map/ppermute | solution.py:54

commit v4 on v1

--- a/solution.py
+++ b/solution.py
@@ -439,7 +439,9 @@
 
 def turn(s, left_ref, turned):
     for e in range(s.local):
-        turned[e] = jnp.transpose(left_ref[e].astype(F32)).astype(BF16)
+        zeros = jnp.zeros((s.rows, s.hidden), F32)
+        rows = [left_ref[e].astype(F32) if n == e else zeros for n in range(s.local)]
+        turned[e] = jnp.transpose(jnp.concatenate(rows, axis=0)).astype(BF16)
 
 
 def grads_kernel(s, count, *refs):
@@ -466,9 +468,9 @@
                 def _():
                     copy(out, k - 2, p).wait()
 
-                for e in range(s.local):
-                    rows = rows_ref[k, s.at(e), at : at + size]
-                    store[lax.rem(k, 2) * pieces + p, e, :, :size] = dot(turned[e], rows).astype(BF16)
+                left = turned[...].reshape(s.local * s.hidden, s.total)
+                value = dot(left, rows_ref[k, :, at : at + size]).astype(BF16)
+                store[lax.rem(k, 2) * pieces + p, :, :, :size] = value.reshape(s.local, s.hidden, size)
                 copy(out, k, p).start()
             return 0
 
@@ -490,7 +492,7 @@
         specs=[VECTORS] * (2 * count) + [ANYWHERE],
         out_specs=[ANYWHERE] * count + [VECTORS],
         scratch=[
-            pltpu.VMEM((s.local, s.hidden, s.rows), BF16),
+            pltpu.VMEM((s.local, s.hidden, s.total), BF16),
             pltpu.VMEM((slots, s.local, s.hidden, room), BF16),
             pltpu.SemaphoreType.DMA((slots,)),
         ],

time: 108 us -> 112 us (1.037)
  Pallas kernels: 65.7 us -> 69.2 us
    pallas_call x19, Pallas kernels: 65.7 us -> 69.2 us  [call(): pl.pallas_call(kernel, name=name, grid=grid, out_shape=outs, in_specs=spe...]
  transfers between devices with their start and end apart: 29 -> 29, of which waited for: 4 -> 4; matrix products, arithmetic and copies ran while one was open for 0% -> 0% of each run, Pallas kernels for 59% -> 60%
where the time goes in v4:
time: 112 us
  Pallas kernels  69.2 us (62%)
  starting transfers between devices  33.6 us (30%)
  waiting for transfers between devices  8.02 us (7%)
    pallas_call x19, Pallas kernels, call(): pl.pallas_call(kernel, name=name, grid=grid, out_shape=outs, in_specs=spe...  69.2 us
    ppermute x29, starting transfers between devices, shift(): return lax.ppermute(value, AXES, pairs)  33.6 us
    ppermute x29, waiting for transfers between devices, shift(): return lax.ppermute(value, AXES, pairs)  8.02 us
  transfers between devices with their start and end apart: 29, of which 4 were waited for; matrix products, arithmetic and copies ran while one was open for 0% of the time, Pallas kernels for 60%

profile of v4, /device:TPU:0, one launch (start us, length us, event | category | flops | bytes accessed | tf_op | source)
XLA Modules:
  0.0 111.7 jit_solution(5225924732666313085)
XLA Ops:
  0.6 1.0 pack.1
  1.6 5.1 %collective-permute-start.2 = (bf16[16,1920]{1,0:T(8,128)(2,1)S(1)}, bf16[16,1920]{1,0:T(8,128)(2,1)S(1)}, u32[]{:S(2)}, u32[]{:S(2)}) collective-permute-start(bf16[16,1920]{1,0:T(8,128)(2,1)S(1)} %get-tuple-element.48.refs_0_), channel_id=1, source_target_pairs={{0,24},{1,25},{2,26},{3,27},{4,28},{5,29},{6,30},{7,31},{8,16},{9,... | collective-permute-start | bytes 184328 | tf_op jit(solution)/shard_map/ppermute | solution.py:54
  6.8 0.0 collective-permute-start.1
  6.8 0.6 collective-permute-start
  7.4 1.8 %collective-permute-done.2.refs_3_ = bf16[16,1920]{1,0:T(8,128)(2,1)S(1)} collective-permute-done((bf16[16,1920]{1,0:T(8,128)(2,1)S(1)}, bf16[16,1920]{1,0:T(8,128)(2,1)S(1)}, u32[]{:S(2)}, u32[]{:S(2)}) %collective-permute-start.2) | collective-permute-done | bytes 61472 | tf_op jit(solution)/shard_map/ppermute | solution.py:54
  9.2 2.8 %collective-permute-done.1.refs_2_ = bf16[16,1920]{1,0:T(8,128)(2,1)S(1)} collective-permute-done((bf16[16,1920]{1,0:T(8,128)(2,1)S(1)}, bf16[16,1920]{1,0:T(8,128)(2,1)S(1)}, u32[]{:S(2)}, u32[]{:S(2)}) %collective-permute-start.1) | collective-permute-done | bytes 61472 | tf_op jit(solution)/shard_map/ppermute | solution.py:54
  12.1 0.0 collective-permute-done.refs_1_
  12.1 1.2 %collective-permute-start.6 = (bf16[16,1792]{1,0:T(8,128)(2,1)S(1)}, bf16[16,1792]{1,0:T(8,128)(2,1)S(1)}, u32[]{:S(2)}, u32[]{:S(2)}) collective-permute-start(bf16[16,1792]{1,0:T(8,128)(2,1)S(1)} %get-tuple-element.51.refs_0_), channel_id=1, source_target_pairs={{0,8},{1,9},{2,10},{3,11},{4,12},{5,13},{6,14},{7,15},{8,0},{9,1},... | collective-permute-start | bytes 172040 | tf_op jit(solution)/shard_map/ppermute | solution.py:54
  13.3 2.4 %collective-permute-start.5 = (bf16[64,1920]{1,0:T(8,128)(2,1)S(1)}, bf16[64,1920]{1,0:T(8,128)(2,1)S(1)}, u32[]{:S(2)}, u32[]{:S(2)}) collective-permute-start(bf16[64,1920]{1,0:T(8,128)(2,1)S(1)} %get-tuple-element.50.refs_0_), channel_id=1, source_target_pairs={{0,6},{1,7},{2,4},{3,5},{4,2},{5,3},{6,0},{7,1},{8,14},{9,15},{10,... | collective-permute-start | bytes 737288 | tf_op jit(solution)/shard_map/ppermute | solution.py:54
  15.7 0.5 collective-permute-start.4
  16.2 0.5 collective-permute-start.3
  16.8 0.0 collective-permute-done.6.refs_1_
  16.8 2.2 %collective-permute-start.7 = (bf16[32,1792]{1,0:T(8,128)(2,1)S(1)}, bf16[32,1792]{1,0:T(8,128)(2,1)S(1)}, u32[]{:S(2)}, u32[]{:S(2)}) collective-permute-start(bf16[32,1792]{1,0:T(8,128)(2,1)S(1)} %double.2._.refs_0_), channel_id=1, source_target_pairs={{0,16},{1,17},{2,18},{3,19},{4,20},{5,21},{6,22},{7,23},{8,24},{9,... | collective-permute-start | bytes 344072 | tf_op jit(solution)/shard_map/ppermute | solution.py:54
  19.0 3.6 %hold_down.1.refs_2_.held_ref = bf16[2,608,3584]{2,1,0:T(8,128)(2,1)S(1)} custom-call(bf16[2,608,7168]{2,1,0:T(8,128)(2,1)} %refs_8_.1, bf16[32,1792]{1,0:T(8,128)(2,1)S(1)} %double.2._.refs_0_), custom_call_target="tpu_custom_call" | custom-call | flops 12000000000 | tf_op jit(solution)/shard_map/hold_down/pallas_call | solution.py:78
  22.6 1.2 %collective-permute-done.7.refs_1_ = bf16[32,1792]{1,0:T(8,128)(2,1)S(1)} collective-permute-done((bf16[32,1792]{1,0:T(8,128)(2,1)S(1)}, bf16[32,1792]{1,0:T(8,128)(2,1)S(1)}, u32[]{:S(2)}, u32[]{:S(2)}) %collective-permute-start.7) | collective-permute-done | bytes 114720 | tf_op jit(solution)/shard_map/ppermute | solution.py:54
  23.8 0.0 collective-permute-done.5.refs_2_
  23.8 2.1 %collective-permute-done.4.refs_1_ = bf16[64,1920]{1,0:T(8,128)(2,1)S(1)} collective-permute-done((bf16[64,1920]{1,0:T(8,128)(2,1)S(1)}, bf16[64,1920]{1,0:T(8,128)(2,1)S(1)}, u32[]{:S(2)}, u32[]{:S(2)}) %collective-permute-start.4) | collective-permute-done | bytes 245792 | tf_op jit(solution)/shard_map/ppermute | solution.py:54
  25.9 0.0 collective-permute-done.3.refs_0_
  25.9 0.1 stack_tokens_plane.1.refs_1_
  26.0 0.1 collective-permute-start.9
  26.1 0.5 collective-permute-start.8
  26.6 0.1 collective-permute-start.14
  26.7 2.3 %collective-permute-start.12 = (bf16[64,1792]{1,0:T(8,128)(2,1)S(1)}, bf16[64,1792]{1,0:T(8,128)(2,1)S(1)}, u32[]{:S(2)}, u32[]{:S(2)}) collective-permute-start(bf16[64,1792]{1,0:T(8,128)(2,1)S(1)} %stack_cotangents.1.refs_6_.refs_0_), channel_id=1, source_target_pairs={{0,6},{1,7},{2,4},{3,5},{4,2},{5,3},{6,0},{7,1},{8,14},{9,15},{10,... | collective-permute-start | bytes 688136 | tf_op jit(solution)/shard_map/ppermute | solution.py:54
  29.1 0.5 collective-permute-start.11
  29.6 0.0 collective-permute-done.8.refs_2_
  29.6 0.6 collective-permute-start.10
  30.2 0.0 collective-permute-done.9.refs_3_
  30.2 14.5 %gate_up.1 = (bf16[4,64,1792]{2,1,0:T(8,128)(2,1)S(1)}, bf16[64,128]{1,0:T(8,128)(2,1)S(1)}, bf16[128,64]{1,0:T(8,128)(2,1)S(1)}, f32[64,128]{1,0:T(8,128)S(1)},...) custom-call(bf16[64,1920]{1,0:T(8,128)(2,1)S(1)} %get-tuple-element., ...), custom_call_target="tpu_custom_call" | custom-call | flops 46000001024 | tf_op jit(solution)/shard_map/gate_up/pallas_call | solution.py:78
  44.7 0.0 collective-permute-done.12.refs_2_
  44.8 0.0 collective-permute-done.11.refs_1_
  44.8 0.0 collective-permute-done.10.refs_0_
  44.8 0.1 collective-permute-start.15
  44.9 5.4 %forward.1 = (bf16[2,2,64,1792]{3,2,1,0:T(8,128)(2,1)S(1)}, bf16[2,2,64,1792]{3,2,1,0:T(8,128)(2,1)S(1)}) custom-call(bf16[2,32,608]{2,1,0:T(8,128)(2,1)S(1)} %get-tuple-element.52.act_ref.refs_1_, f32[64,128]{1,0:T(8,128)S(1)} %get-tuple-element.53.refs_3_.gate_ref.refs_5_, bf16[128,64]{1,0:T(8,128)(2,1)S(1)} %get-tuple-element.54.back_ref, ...), custom_call_target="tpu_custom_call" | custom-call | flops 46000001024 | tf_op jit(solution)/shard_map/forward/pallas_call | solution.py:78
  50.3 0.5 collective-permute-start.13
  50.9 0.0 collective-permute-done.14.refs_2_
  50.9 8.0 %hidden_grads.1 = (bf16[4,64,1792]{2,1,0:T(8,128)(2,1)S(1)}, bf16[2,32,608]{2,1,0:T(8,128)(2,1)S(1)}, bf16[2,32,608]{2,1,0:T(8,128)(2,1)S(1)}) custom-call(bf16[64,1792]{1,0:T(8,128)(2,1)S(1)} %stack_cotangents.1.refs_6_.refs_0_, bf16[192,1792]{1,0:T(8,128)(2,1)S(1)} %stack_cotangents_plane.1._.refs_1_, ...), custom_call_target="tpu_custom_call" | custom-call | flops 46000001024 | tf_op jit(solution)/shard_map/hidden_grads/pallas_call | solution.py:78
  58.9 0.2 mixed_cores.1
  59.1 1.5 %collective-permute-start.16 = (bf16[64,1792]{1,0:T(8,128)(2,1)S(1)}, bf16[64,1792]{1,0:T(8,128)(2,1)S(1)}, u32[]{:S(2)}, u32[]{:S(2)}) collective-permute-start(bf16[64,1792]{1,0:T(8,128)(2,1)S(1)} %get-tuple-element.62), channel_id=1, source_target_pairs={{0,2},{1,3},{2,0},{3,1},{4,6},{5,7},{6,4},{7,5},{8,10},{9,11},{10,... | collective-permute-start | bytes 688136 | tf_op jit(solution)/shard_map/ppermute | solution.py:54
  60.6 1.5 %collective-permute-start.17 = (bf16[64,1792]{1,0:T(8,128)(2,1)S(1)}, bf16[64,1792]{1,0:T(8,128)(2,1)S(1)}, u32[]{:S(2)}, u32[]{:S(2)}) collective-permute-start(bf16[64,1792]{1,0:T(8,128)(2,1)S(1)} %get-tuple-element.63), channel_id=1, source_target_pairs={{0,4},{1,5},{2,6},{3,7},{4,0},{5,1},{6,2},{7,3},{8,12},{9,13},{10,... | collective-permute-start | bytes 688136 | tf_op jit(solution)/shard_map/ppermute | solution.py:54
  62.1 0.6 collective-permute-start.18
  62.7 10.2 %backward.1 = (bf16[2,2,64,1792]{3,2,1,0:T(8,128)(2,1)S(1)}, bf16[2,2,64,1792]{3,2,1,0:T(8,128)(2,1)S(1)}) custom-call(bf16[2,32,608]{2,1,0:T(8,128)(2,1)S(1)} %get-tuple-element.60.refs_2_.dg_ref.refs_0_, bf16[2,32,608]{2,1,0:T(8,128)(2,1)S(1)} %get-tuple-element.65.du_ref.refs_0_, bf16[128,64]{1,0:T(8,128)(2,1)S(1)} %get-tuple-element.54.back_ref, ...), custom_call_target="tpu_custom_call" | custom-call | flops 46000001024 | tf_op jit(solution)/shard_map/backward/pallas_call | solution.py:78
  72.9 0.0 collective-permute-done.18.refs_3_
  72.9 0.1 mixed_plane.1
  73.0 0.1 collective-permute-start.22
  73.1 1.7 %collective-permute-start.19 = (bf16[16,1792]{1,0:T(8,128)(2,1)S(1)}, bf16[16,1792]{1,0:T(8,128)(2,1)S(1)}, u32[]{:S(2)}, u32[]{:S(2)}) collective-permute-start(bf16[16,1792]{1,0:T(8,128)(2,1)S(1)} %get-tuple-element.70), channel_id=1, source_target_pairs={{0,8},{1,9},{2,10},{3,11},{4,12},{5,13},{6,14},{7,15},{8,0},{9,1},... | collective-permute-start | bytes 172040 | tf_op jit(solution)/shard_map/ppermute | solution.py:54
  74.8 0.8 collective-permute-start.20
  75.6 0.0 collective-permute-done.22.refs_1_
  75.6 0.2 tokens_cores.1
  75.8 1.5 %collective-permute-start.23 = (bf16[64,1792]{1,0:T(8,128)(2,1)S(1)}, bf16[64,1792]{1,0:T(8,128)(2,1)S(1)}, u32[]{:S(2)}, u32[]{:S(2)}) collective-permute-start(bf16[64,1792]{1,0:T(8,128)(2,1)S(1)} %get-tuple-element.75), channel_id=1, source_target_pairs={{0,2},{1,3},{2,0},{3,1},{4,6},{5,7},{6,4},{7,5},{8,10},{9,11},{10,... | collective-permute-start | bytes 688136 | tf_op jit(solution)/shard_map/ppermute | solution.py:54
  77.3 1.5 %collective-permute-start.24 = (bf16[64,1792]{1,0:T(8,128)(2,1)S(1)}, bf16[64,1792]{1,0:T(8,128)(2,1)S(1)}, u32[]{:S(2)}, u32[]{:S(2)}) collective-permute-start(bf16[64,1792]{1,0:T(8,128)(2,1)S(1)} %get-tuple-element.76), channel_id=1, source_target_pairs={{0,4},{1,5},{2,6},{3,7},{4,0},{5,1},{6,2},{7,3},{8,12},{9,13},{10,... | collective-permute-start | bytes 688136 | tf_op jit(solution)/shard_map/ppermute | solution.py:54
  78.7 0.6 collective-permute-start.25
  79.4 16.6 %grad_gate_down.1 = (bf16[2,608,7168]{2,1,0:T(8,128)(2,1)}, bf16[2,608,7168]{2,1,0:T(8,128)(2,1)}, f32[8,128]{1,0:T(8,128)S(1)}) custom-call(bf16[2,32,608]{2,1,0:T(8,128)(2,1)S(1)} %get-tuple-element.60.refs_2_.dg_ref.refs_0_, bf16[2,32,608]{2,1,0:T(8,128)(2,1)S(1)} %get-tuple-element.52.act_ref.refs_1_, ...), custom_call_target="tpu_custom_call" | custom-call | flops 46000001024 | tf_op jit(solution)/shard_map/grad_gate_down/pallas_call | solution.py:78
  96.0 2.0 %collective-permute-start.21 = (bf16[16,1792]{1,0:T(8,128)(2,1)S(1)}, bf16[16,1792]{1,0:T(8,128)(2,1)S(1)}, u32[]{:S(2)}, u32[]{:S(2)}) collective-permute-start(bf16[16,1792]{1,0:T(8,128)(2,1)S(1)} %get-tuple-element.72), channel_id=1, source_target_pairs={{0,24},{1,25},{2,26},{3,27},{4,28},{5,29},{6,30},{7,31},{8,16},{9,... | collective-permute-start | bytes 172040 | tf_op jit(solution)/shard_map/ppermute | solution.py:54
  98.1 0.0 collective-permute-done.25.refs_3_
  98.1 0.1 tokens_plane.1
  98.2 0.8 collective-permute-start.26
  99.0 1.6 %collective-permute-start.27 = (bf16[16,1792]{1,0:T(8,128)(2,1)S(1)}, bf16[16,1792]{1,0:T(8,128)(2,1)S(1)}, u32[]{:S(2)}, u32[]{:S(2)}) collective-permute-start(bf16[16,1792]{1,0:T(8,128)(2,1)S(1)} %get-tuple-element.83), channel_id=1, source_target_pairs={{0,16},{1,17},{2,18},{3,19},{4,20},{5,21},{6,22},{7,23},{8,24},{9,... | collective-permute-start | bytes 172040 | tf_op jit(solution)/shard_map/ppermute | solution.py:54
  100.7 0.0 collective-permute-done.19.refs_1_
  100.7 2.0 %collective-permute-start.28 = (bf16[16,1792]{1,0:T(8,128)(2,1)S(1)}, bf16[16,1792]{1,0:T(8,128)(2,1)S(1)}, u32[]{:S(2)}, u32[]{:S(2)}) collective-permute-start(bf16[16,1792]{1,0:T(8,128)(2,1)S(1)} %get-tuple-element.84), channel_id=1, source_target_pairs={{0,24},{1,25},{2,26},{3,27},{4,28},{5,29},{6,30},{7,31},{8,16},{9,... | collective-permute-start | bytes 172040 | tf_op jit(solution)/shard_map/ppermute | solution.py:54
  102.6 8.3 %grad_up.1 = (bf16[2,608,7168]{2,1,0:T(8,128)(2,1)}, f32[8,128]{1,0:T(8,128)S(1)}) custom-call(bf16[2,32,608]{2,1,0:T(8,128)(2,1)S(1)} %get-tuple-element.65.du_ref.refs_0_, bf16[4,64,1792]{2,1,0:T(8,128)(2,1)S(1)} %get-tuple-element.78.refs_2_.refs_1_, bf16[16,1792]{1,0:T(8,128)(2,1)S(1)} %get-tuple-element.81.refs_2_.refs_4_), custom_call_target="tpu_custom_call" | custom-call | flops 46000001024 | tf_op jit(solution)/shard_map/grad_up/pallas_call | solution.py:78
  111.0 0.0 collective-permute-done.20.refs_2_
  111.0 0.0 collective-permute-done.26.refs_5_
  111.0 0.0 collective-permute-done.27.refs_6_
  111.0 0.7 finish.1
  (13 shorter events, 0.1 us)
Async XLA Ops:
  1.6 7.6 %collective-permute-start.2 = (bf16[16,1920]{1,0:T(8,128)(2,1)S(1)}, bf16[16,1920]{1,0:T(8,128)(2,1)S(1)}, u32[]{:S(2)}, u32[]{:S(2)}) collective-permute-start(bf16[16,1920]{1,0:T(8,128)(2,1)S(1)} %get-tuple-element.48.refs_0_), channel_id=1, source_target_pairs={{0,24},{1,25},{2,26},{3,27},{4,28},{5,29},{6,30},{7,31},{8,16},{9,... | collective-permute-start | bytes 184328 | tf_op jit(solution)/shard_map/ppermute | solution.py:54
  6.8 5.3 %collective-permute-start.1 = (bf16[16,1920]{1,0:T(8,128)(2,1)S(1)}, bf16[16,1920]{1,0:T(8,128)(2,1)S(1)}, u32[]{:S(2)}, u32[]{:S(2)}) collective-permute-start(bf16[16,1920]{1,0:T(8,128)(2,1)S(1)} %get-tuple-element.48.refs_0_), channel_id=1, source_target_pairs={{0,16},{1,17},{2,18},{3,19},{4,20},{5,21},{6,22},{7,23},{8,24},{9,... | collective-permute-start | bytes 184328 | tf_op jit(solution)/shard_map/ppermute | solution.py:54
  6.8 5.3 %collective-permute-start = (bf16[16,1920]{1,0:T(8,128)(2,1)S(1)}, bf16[16,1920]{1,0:T(8,128)(2,1)S(1)}, u32[]{:S(2)}, u32[]{:S(2)}) collective-permute-start(bf16[16,1920]{1,0:T(8,128)(2,1)S(1)} %get-tuple-element.48.refs_0_), channel_id=1, source_target_pairs={{0,8},{1,9},{2,10},{3,11},{4,12},{5,13},{6,14},{7,15},{8,0},{9,1},... | collective-permute-start | bytes 184328 | tf_op jit(solution)/shard_map/ppermute | solution.py:54
  12.1 4.7 %collective-permute-start.6 = (bf16[16,1792]{1,0:T(8,128)(2,1)S(1)}, bf16[16,1792]{1,0:T(8,128)(2,1)S(1)}, u32[]{:S(2)}, u32[]{:S(2)}) collective-permute-start(bf16[16,1792]{1,0:T(8,128)(2,1)S(1)} %get-tuple-element.51.refs_0_), channel_id=1, source_target_pairs={{0,8},{1,9},{2,10},{3,11},{4,12},{5,13},{6,14},{7,15},{8,0},{9,1},... | collective-permute-start | bytes 172040 | tf_op jit(solution)/shard_map/ppermute | solution.py:54
  13.3 10.5 %collective-permute-start.5 = (bf16[64,1920]{1,0:T(8,128)(2,1)S(1)}, bf16[64,1920]{1,0:T(8,128)(2,1)S(1)}, u32[]{:S(2)}, u32[]{:S(2)}) collective-permute-start(bf16[64,1920]{1,0:T(8,128)(2,1)S(1)} %get-tuple-element.50.refs_0_), channel_id=1, source_target_pairs={{0,6},{1,7},{2,4},{3,5},{4,2},{5,3},{6,0},{7,1},{8,14},{9,15},{10,... | collective-permute-start | bytes 737288 | tf_op jit(solution)/shard_map/ppermute | solution.py:54
  15.7 10.2 %collective-permute-start.4 = (bf16[64,1920]{1,0:T(8,128)(2,1)S(1)}, bf16[64,1920]{1,0:T(8,128)(2,1)S(1)}, u32[]{:S(2)}, u32[]{:S(2)}) collective-permute-start(bf16[64,1920]{1,0:T(8,128)(2,1)S(1)} %get-tuple-element.50.refs_0_), channel_id=1, source_target_pairs={{0,4},{1,5},{2,6},{3,7},{4,0},{5,1},{6,2},{7,3},{8,12},{9,13},{10,... | collective-permute-start | bytes 737288 | tf_op jit(solution)/shard_map/ppermute | solution.py:54
  16.2 9.7 %collective-permute-start.3 = (bf16[64,1920]{1,0:T(8,128)(2,1)S(1)}, bf16[64,1920]{1,0:T(8,128)(2,1)S(1)}, u32[]{:S(2)}, u32[]{:S(2)}) collective-permute-start(bf16[64,1920]{1,0:T(8,128)(2,1)S(1)} %get-tuple-element.50.refs_0_), channel_id=1, source_target_pairs={{0,2},{1,3},{2,0},{3,1},{4,6},{5,7},{6,4},{7,5},{8,10},{9,11},{10,... | collective-permute-start | bytes 737288 | tf_op jit(solution)/shard_map/ppermute | solution.py:54
  16.8 7.0 %collective-permute-start.7 = (bf16[32,1792]{1,0:T(8,128)(2,1)S(1)}, bf16[32,1792]{1,0:T(8,128)(2,1)S(1)}, u32[]{:S(2)}, u32[]{:S(2)}) collective-permute-start(bf16[32,1792]{1,0:T(8,128)(2,1)S(1)} %double.2._.refs_0_), channel_id=1, source_target_pairs={{0,16},{1,17},{2,18},{3,19},{4,20},{5,21},{6,22},{7,23},{8,24},{9,... | collective-permute-start | bytes 344072 | tf_op jit(solution)/shard_map/ppermute | solution.py:54
  26.0 4.2 %collective-permute-start.9 = (bf16[192,1920]{1,0:T(8,128)(2,1)S(1)}, bf16[192,1920]{1,0:T(8,128)(2,1)S(1)}, u32[]{:S(2)}, u32[]{:S(2)}) collective-permute-start(bf16[192,1920]{1,0:T(8,128)(2,1)S(1)} %stack_tokens_plane.1.refs_1_), channel_id=1, source_target_pairs={{0,1},{1,0},{2,3},{3,2},{4,5},{5,4},{6,7},{7,6},{8,9},{9,8},{10,11... | collective-permute-start | bytes 2211848 | tf_op jit(solution)/shard_map/ppermute | solution.py:54
  26.1 3.5 %collective-permute-start.8 = (bf16[64,1920]{1,0:T(8,128)(2,1)S(1)}, bf16[64,1920]{1,0:T(8,128)(2,1)S(1)}, u32[]{:S(2)}, u32[]{:S(2)}) collective-permute-start(bf16[64,1920]{1,0:T(8,128)(2,1)S(1)} %get-tuple-element.50.refs_0_), channel_id=1, source_target_pairs={{0,1},{1,0},{2,3},{3,2},{4,5},{5,4},{6,7},{7,6},{8,9},{9,8},{10,11... | collective-permute-start | bytes 737288 | tf_op jit(solution)/shard_map/ppermute | solution.py:54
  26.6 24.3 %collective-permute-start.14 = (bf16[64,1792]{1,0:T(8,128)(2,1)S(1)}, bf16[64,1792]{1,0:T(8,128)(2,1)S(1)}, u32[]{:S(2)}, u32[]{:S(2)}) collective-permute-start(bf16[64,1792]{1,0:T(8,128)(2,1)S(1)} %stack_cotangents.1.refs_6_.refs_0_), channel_id=1, source_target_pairs={{0,1},{1,0},{2,3},{3,2},{4,5},{5,4},{6,7},{7,6},{8,9},{9,8},{10,11... | collective-permute-start | bytes 688136 | tf_op jit(solution)/shard_map/ppermute | solution.py:54
  26.7 18.0 %collective-permute-start.12 = (bf16[64,1792]{1,0:T(8,128)(2,1)S(1)}, bf16[64,1792]{1,0:T(8,128)(2,1)S(1)}, u32[]{:S(2)}, u32[]{:S(2)}) collective-permute-start(bf16[64,1792]{1,0:T(8,128)(2,1)S(1)} %stack_cotangents.1.refs_6_.refs_0_), channel_id=1, source_target_pairs={{0,6},{1,7},{2,4},{3,5},{4,2},{5,3},{6,0},{7,1},{8,14},{9,15},{10,... | collective-permute-start | bytes 688136 | tf_op jit(solution)/shard_map/ppermute | solution.py:54
  29.1 15.7 %collective-permute-start.11 = (bf16[64,1792]{1,0:T(8,128)(2,1)S(1)}, bf16[64,1792]{1,0:T(8,128)(2,1)S(1)}, u32[]{:S(2)}, u32[]{:S(2)}) collective-permute-start(bf16[64,1792]{1,0:T(8,128)(2,1)S(1)} %stack_cotangents.1.refs_6_.refs_0_), channel_id=1, source_target_pairs={{0,4},{1,5},{2,6},{3,7},{4,0},{5,1},{6,2},{7,3},{8,12},{9,13},{10,... | collective-permute-start | bytes 688136 | tf_op jit(solution)/shard_map/ppermute | solution.py:54
  29.6 15.2 %collective-permute-start.10 = (bf16[64,1792]{1,0:T(8,128)(2,1)S(1)}, bf16[64,1792]{1,0:T(8,128)(2,1)S(1)}, u32[]{:S(2)}, u32[]{:S(2)}) collective-permute-start(bf16[64,1792]{1,0:T(8,128)(2,1)S(1)} %stack_cotangents.1.refs_6_.refs_0_), channel_id=1, source_target_pairs={{0,2},{1,3},{2,0},{3,1},{4,6},{5,7},{6,4},{7,5},{8,10},{9,11},{10,... | collective-permute-start | bytes 688136 | tf_op jit(solution)/shard_map/ppermute | solution.py:54
  44.8 6.0 %collective-permute-start.15 = (bf16[192,1792]{1,0:T(8,128)(2,1)S(1)}, bf16[192,1792]{1,0:T(8,128)(2,1)S(1)}, u32[]{:S(2)}, u32[]{:S(2)}) collective-permute-start(bf16[192,1792]{1,0:T(8,128)(2,1)S(1)} %stack_cotangents_plane.1._.refs_1_), channel_id=1, source_target_pairs={{0,1},{1,0},{2,3},{3,2},{4,5},{5,4},{6,7},{7,6},{8,9},{9,8},{10,11... | collective-permute-start | bytes 2064392 | tf_op jit(solution)/shard_map/ppermute | solution.py:54
  50.3 8.6 %collective-permute-start.13 = (bf16[2,2,64,1792]{3,2,1,0:T(8,128)(2,1)S(1)}, bf16[2,2,64,1792]{3,2,1,0:T(8,128)(2,1)S(1)}, u32[]{:S(2)}, u32[]{:S(2)}) collective-permute-start(bf16[2,2,64,1792]{3,2,1,0:T(8,128)(2,1)S(1)} %get-tuple-element.56), channel_id=1, source_target_pairs={{0,1},{1,0},{2,3},{3,2},{4,5},{5,4},{6,7},{7,6},{8,9},{9,8},{10,11... | collective-permute-start | bytes 2752520 | tf_op jit(solution)/shard_map/ppermute | solution.py:54
  59.1 13.7 %collective-permute-start.16 = (bf16[64,1792]{1,0:T(8,128)(2,1)S(1)}, bf16[64,1792]{1,0:T(8,128)(2,1)S(1)}, u32[]{:S(2)}, u32[]{:S(2)}) collective-permute-start(bf16[64,1792]{1,0:T(8,128)(2,1)S(1)} %get-tuple-element.62), channel_id=1, source_target_pairs={{0,2},{1,3},{2,0},{3,1},{4,6},{5,7},{6,4},{7,5},{8,10},{9,11},{10,... | collective-permute-start | bytes 688136 | tf_op jit(solution)/shard_map/ppermute | solution.py:54
  60.6 12.3 %collective-permute-start.17 = (bf16[64,1792]{1,0:T(8,128)(2,1)S(1)}, bf16[64,1792]{1,0:T(8,128)(2,1)S(1)}, u32[]{:S(2)}, u32[]{:S(2)}) collective-permute-start(bf16[64,1792]{1,0:T(8,128)(2,1)S(1)} %get-tuple-element.63), channel_id=1, source_target_pairs={{0,4},{1,5},{2,6},{3,7},{4,0},{5,1},{6,2},{7,3},{8,12},{9,13},{10,... | collective-permute-start | bytes 688136 | tf_op jit(solution)/shard_map/ppermute | solution.py:54
  62.1 10.8 %collective-permute-start.18 = (bf16[64,1792]{1,0:T(8,128)(2,1)S(1)}, bf16[64,1792]{1,0:T(8,128)(2,1)S(1)}, u32[]{:S(2)}, u32[]{:S(2)}) collective-permute-start(bf16[64,1792]{1,0:T(8,128)(2,1)S(1)} %get-tuple-element.64), channel_id=1, source_target_pairs={{0,6},{1,7},{2,4},{3,5},{4,2},{5,3},{6,0},{7,1},{8,14},{9,15},{10,... | collective-permute-start | bytes 688136 | tf_op jit(solution)/shard_map/ppermute | solution.py:54
  73.0 2.6 %collective-permute-start.22 = (bf16[2,2,64,1792]{3,2,1,0:T(8,128)(2,1)S(1)}, bf16[2,2,64,1792]{3,2,1,0:T(8,128)(2,1)S(1)}, u32[]{:S(2)}, u32[]{:S(2)}) collective-permute-start(bf16[2,2,64,1792]{3,2,1,0:T(8,128)(2,1)S(1)} %get-tuple-element.73), channel_id=1, source_target_pairs={{0,1},{1,0},{2,3},{3,2},{4,5},{5,4},{6,7},{7,6},{8,9},{9,8},{10,11... | collective-permute-start | bytes 2752520 | tf_op jit(solution)/shard_map/ppermute | solution.py:54
  73.1 27.6 %collective-permute-start.19 = (bf16[16,1792]{1,0:T(8,128)(2,1)S(1)}, bf16[16,1792]{1,0:T(8,128)(2,1)S(1)}, u32[]{:S(2)}, u32[]{:S(2)}) collective-permute-start(bf16[16,1792]{1,0:T(8,128)(2,1)S(1)} %get-tuple-element.70), channel_id=1, source_target_pairs={{0,8},{1,9},{2,10},{3,11},{4,12},{5,13},{6,14},{7,15},{8,0},{9,1},... | collective-permute-start | bytes 172040 | tf_op jit(solution)/shard_map/ppermute | solution.py:54
  74.8 36.2 %collective-permute-start.20 = (bf16[16,1792]{1,0:T(8,128)(2,1)S(1)}, bf16[16,1792]{1,0:T(8,128)(2,1)S(1)}, u32[]{:S(2)}, u32[]{:S(2)}) collective-permute-start(bf16[16,1792]{1,0:T(8,128)(2,1)S(1)} %get-tuple-element.71), channel_id=1, source_target_pairs={{0,16},{1,17},{2,18},{3,19},{4,20},{5,21},{6,22},{7,23},{8,24},{9,... | collective-permute-start | bytes 172040 | tf_op jit(solution)/shard_map/ppermute | solution.py:54
  75.8 20.2 %collective-permute-start.23 = (bf16[64,1792]{1,0:T(8,128)(2,1)S(1)}, bf16[64,1792]{1,0:T(8,128)(2,1)S(1)}, u32[]{:S(2)}, u32[]{:S(2)}) collective-permute-start(bf16[64,1792]{1,0:T(8,128)(2,1)S(1)} %get-tuple-element.75), channel_id=1, source_target_pairs={{0,2},{1,3},{2,0},{3,1},{4,6},{5,7},{6,4},{7,5},{8,10},{9,11},{10,... | collective-permute-start | bytes 688136 | tf_op jit(solution)/shard_map/ppermute | solution.py:54
  77.3 20.8 %collective-permute-start.24 = (bf16[64,1792]{1,0:T(8,128)(2,1)S(1)}, bf16[64,1792]{1,0:T(8,128)(2,1)S(1)}, u32[]{:S(2)}, u32[]{:S(2)}) collective-permute-start(bf16[64,1792]{1,0:T(8,128)(2,1)S(1)} %get-tuple-element.76), channel_id=1, source_target_pairs={{0,4},{1,5},{2,6},{3,7},{4,0},{5,1},{6,2},{7,3},{8,12},{9,13},{10,... | collective-permute-start | bytes 688136 | tf_op jit(solution)/shard_map/ppermute | solution.py:54
  78.7 19.3 %collective-permute-start.25 = (bf16[64,1792]{1,0:T(8,128)(2,1)S(1)}, bf16[64,1792]{1,0:T(8,128)(2,1)S(1)}, u32[]{:S(2)}, u32[]{:S(2)}) collective-permute-start(bf16[64,1792]{1,0:T(8,128)(2,1)S(1)} %get-tuple-element.77), channel_id=1, source_target_pairs={{0,6},{1,7},{2,4},{3,5},{4,2},{5,3},{6,0},{7,1},{8,14},{9,15},{10,... | collective-permute-start | bytes 688136 | tf_op jit(solution)/shard_map/ppermute | solution.py:54
  96.0 15.0 %collective-permute-start.21 = (bf16[16,1792]{1,0:T(8,128)(2,1)S(1)}, bf16[16,1792]{1,0:T(8,128)(2,1)S(1)}, u32[]{:S(2)}, u32[]{:S(2)}) collective-permute-start(bf16[16,1792]{1,0:T(8,128)(2,1)S(1)} %get-tuple-element.72), channel_id=1, source_target_pairs={{0,24},{1,25},{2,26},{3,27},{4,28},{5,29},{6,30},{7,31},{8,16},{9,... | collective-permute-start | bytes 172040 | tf_op jit(solution)/shard_map/ppermute | solution.py:54
  98.2 12.8 %collective-permute-start.26 = (bf16[16,1792]{1,0:T(8,128)(2,1)S(1)}, bf16[16,1792]{1,0:T(8,128)(2,1)S(1)}, u32[]{:S(2)}, u32[]{:S(2)}) collective-permute-start(bf16[16,1792]{1,0:T(8,128)(2,1)S(1)} %get-tuple-element.82), channel_id=1, source_target_pairs={{0,8},{1,9},{2,10},{3,11},{4,12},{5,13},{6,14},{7,15},{8,0},{9,1},... | collective-permute-start | bytes 172040 | tf_op jit(solution)/shard_map/ppermute | solution.py:54
  99.0 12.0 %collective-permute-start.27 = (bf16[16,1792]{1,0:T(8,128)(2,1)S(1)}, bf16[16,1792]{1,0:T(8,128)(2,1)S(1)}, u32[]{:S(2)}, u32[]{:S(2)}) collective-permute-start(bf16[16,1792]{1,0:T(8,128)(2,1)S(1)} %get-tuple-element.83), channel_id=1, source_target_pairs={{0,16},{1,17},{2,18},{3,19},{4,20},{5,21},{6,22},{7,23},{8,24},{9,... | collective-permute-start | bytes 172040 | tf_op jit(solution)/shard_map/ppermute | solution.py:54
  100.7 10.4 %collective-permute-start.28 = (bf16[16,1792]{1,0:T(8,128)(2,1)S(1)}, bf16[16,1792]{1,0:T(8,128)(2,1)S(1)}, u32[]{:S(2)}, u32[]{:S(2)}) collective-permute-start(bf16[16,1792]{1,0:T(8,128)(2,1)S(1)} %get-tuple-element.84), channel_id=1, source_target_pairs={{0,24},{1,25},{2,26},{3,27},{4,28},{5,29},{6,30},{7,31},{8,16},{9,... | collective-permute-start | bytes 172040 | tf_op jit(solution)/shard_map/ppermute | solution.py:54
